TPU v7x, 32 devices: a whole 2x2x4 slice. The times are simulated.
32 devices in a mesh: pipe: 2 (over core), dp: 16 (over z, y, x).
Axes of the slice: x: 2, y: 2, z: 4, core: 2. Of those that a mesh axis runs over, the one named last changes fastest.
Arguments:
- section_inputs: bfloat16 [2, 256, 49, 768], P('pipe', 'dp'), may hold values from -6 to 6
- conv_weight: float32 [2, 2, 9, 768], P('pipe'), may hold values from -2 to 2
- conv_bias: float32 [2, 2, 768], P('pipe'), may hold values from -4 to 4
- norm_gain: float32 [2, 2, 768], P('pipe'), may hold values from 0.1 to 1.9
- norm_bias: float32 [2, 2, 768], P('pipe'), may hold values from -4 to 4
- w_qkv: bfloat16 [2, 768, 2304], P('pipe'), may hold values from -0.21875 to 0.21875
- w_proj: bfloat16 [2, 768, 768], P('pipe'), may hold values from -0.625 to 0.625
- b_proj: float32 [2, 768], P('pipe'), may hold values from -4 to 4
- w_fc1: bfloat16 [2, 768, 3072], P('pipe'), may hold values from -0.21875 to 0.21875
- b_fc1: float32 [2, 3072], P('pipe'), may hold values from -6 to 6
- w_fc2: bfloat16 [2, 3072, 768], P('pipe'), may hold values from -0.109375 to 0.109375
- b_fc2: float32 [2, 768], P('pipe'), may hold values from -4 to 4
Outputs:
- section_ends: float32 [2, 256, 49, 768], P('pipe', 'dp')
- grad_conv_weight: float32 [2, 2, 9, 768], P('pipe')
- grad_conv_bias: float32 [2, 2, 768], P('pipe')
- grad_norm_gain: float32 [2, 2, 768], P('pipe')
- grad_norm_bias: float32 [2, 2, 768], P('pipe')
- grad_w_qkv: float32 [2, 768, 2304], P('pipe')
- grad_w_proj: float32 [2, 768, 768], P('pipe')
- grad_b_proj: float32 [2, 768], P('pipe')
- grad_w_fc1: float32 [2, 768, 3072], P('pipe')
- grad_b_fc1: float32 [2, 3072], P('pipe')
- grad_w_fc2: float32 [2, 3072, 768], P('pipe')
- grad_b_fc2: float32 [2, 768], P('pipe')
All inputs are finite; a program needn't handle non-finite values.
Results may differ from a plain program's by a relative error of at most 0.023.
Values may be sent and summed in bfloat16 or wider, within the bound.
A program may use at most 320 MiB of HBM per device.

v0:
```python
import jax
import jax.numpy as jnp
from jax import lax
from jax.sharding import PartitionSpec as P

MICRO = 4


def shifted(x, axis, by):
    count = lax.axis_size(axis)
    pairs = [(i, i + by) for i in range(count) if 0 <= i + by < count]
    return lax.ppermute(x, axis, pairs)


def matmul_low(left, right):
    return jnp.einsum(
        "...ij,...jk->...ik",
        left.astype(jnp.bfloat16),
        right.astype(jnp.bfloat16),
        preferred_element_type=jnp.float32,
    )


def matmul_back(left, right, grad):
    grad_low = grad.astype(jnp.bfloat16)
    left_grad = jnp.einsum(
        "...ik,...jk->...ij",
        grad_low,
        right.astype(jnp.bfloat16),
        preferred_element_type=jnp.float32,
    )
    right_grad = jnp.einsum(
        "...ij,...ik->...jk",
        left.astype(jnp.bfloat16),
        grad_low,
        preferred_element_type=jnp.float32,
    )
    return (left_grad, right_grad)


def depthwise(tensor_in, kernel, shift_row):
    image_count = tensor_in.shape[0]
    channels = tensor_in.shape[2]
    square = tensor_in.reshape(image_count, 7, 7, channels)
    padded = jnp.pad(square, ((0, 0), (1, 1), (1, 1), (0, 0)))
    running = jnp.zeros_like(square) + shift_row
    for offset in range(9):
        row_at = offset // 3
        col_at = offset % 3
        running = running + padded[:, row_at : row_at + 7, col_at : col_at + 7, :] * kernel[offset]
    return running.reshape(image_count, 49, channels)


def layer_norm(tensor_in, gain_row, shift_row):
    centered = tensor_in - jnp.mean(tensor_in, axis=-1, keepdims=True)
    spread_sq = jnp.mean(centered * centered, axis=-1, keepdims=True)
    return centered * lax.rsqrt(spread_sq + 1e-05) * gain_row + shift_row


def first_piece(tensor_in, conv_weight, conv_bias, norm_gain, norm_bias):
    stream = tensor_in + depthwise(tensor_in, conv_weight[0], conv_bias[0])
    normed = layer_norm(stream, norm_gain[0], norm_bias[0]).reshape(-1, tensor_in.shape[2])
    return (stream, normed)


def second_piece(stream, attended, b_proj, conv_weight, conv_bias, norm_gain, norm_bias):
    stream = stream + (attended + b_proj).reshape(stream.shape)
    stream = stream + depthwise(stream, conv_weight[1], conv_bias[1])
    normed = layer_norm(stream, norm_gain[1], norm_bias[1]).reshape(-1, stream.shape[2])
    return (stream, normed)


def gelu_piece(hidden_pre, b_fc1):
    return jax.nn.gelu(hidden_pre + b_fc1, approximate=False)


def softmax_back(weights_soft, grad):
    return weights_soft * (grad - jnp.sum(grad * weights_soft, axis=-1, keepdims=True))


def spatial_mix(queries, keys_all, values_all):
    scaled = queries * 32.0 ** (-0.5)
    weights_soft = jax.nn.softmax(matmul_low(scaled, jnp.swapaxes(keys_all, 2, 3)), axis=-1)
    return matmul_low(weights_soft, values_all)


def channel_mix(queries, keys_all, values_all):
    scaled = jnp.swapaxes(queries, 2, 3) * 32.0 ** (-0.5)
    weights_soft = jax.nn.softmax(matmul_low(scaled, keys_all), axis=-1)
    return jnp.swapaxes(matmul_low(weights_soft, jnp.swapaxes(values_all, 2, 3)), 2, 3)


def spatial_back(queries, keys_all, values_all, grad_mixed):
    scaled = queries * 32.0 ** (-0.5)
    keys_turned = jnp.swapaxes(keys_all, 2, 3)
    weights_soft = jax.nn.softmax(matmul_low(scaled, keys_turned), axis=-1)
    grad_weights, grad_values = matmul_back(weights_soft, values_all, grad_mixed)
    grad_scores = softmax_back(weights_soft, grad_weights)
    grad_scaled, grad_turned = matmul_back(scaled, keys_turned, grad_scores)
    return (grad_scaled * 32.0 ** (-0.5), jnp.swapaxes(grad_turned, 2, 3), grad_values)


def channel_back(queries, keys_all, values_all, grad_mixed):
    scaled = jnp.swapaxes(queries, 2, 3) * 32.0 ** (-0.5)
    weights_soft = jax.nn.softmax(matmul_low(scaled, keys_all), axis=-1)
    values_turned = jnp.swapaxes(values_all, 2, 3)
    grad_weights, grad_turned = matmul_back(
        weights_soft, values_turned, jnp.swapaxes(grad_mixed, 2, 3)
    )
    grad_scores = softmax_back(weights_soft, grad_weights)
    grad_scaled, grad_keys = matmul_back(scaled, keys_all, grad_scores)
    return (
        jnp.swapaxes(grad_scaled, 2, 3) * 32.0 ** (-0.5),
        grad_keys,
        jnp.swapaxes(grad_turned, 2, 3),
    )


def block_forward(tensor_in, params, is_first):
    (
        conv_weight,
        conv_bias,
        norm_gain,
        norm_bias,
        w_qkv,
        w_proj,
        b_proj,
        w_fc1,
        b_fc1,
        w_fc2,
        b_fc2,
    ) = params
    image_count = tensor_in.shape[0]
    channels = tensor_in.shape[2]
    head_count = channels // 32
    stream_one, normed_one = first_piece(tensor_in, conv_weight, conv_bias, norm_gain, norm_bias)
    packed = matmul_low(normed_one, w_qkv).reshape(image_count, 49, 3, head_count, 32)
    queries = jnp.transpose(packed[:, :, 0], (0, 2, 1, 3))
    keys_all = jnp.transpose(packed[:, :, 1], (0, 2, 1, 3))
    values_all = jnp.transpose(packed[:, :, 2], (0, 2, 1, 3))
    mixed = lax.cond(is_first, spatial_mix, channel_mix, queries, keys_all, values_all)
    mixed = jnp.transpose(mixed, (0, 2, 1, 3)).reshape(image_count * 49, channels)
    attended = matmul_low(mixed, w_proj)
    stream_two, normed_two = second_piece(
        stream_one, attended, b_proj, conv_weight, conv_bias, norm_gain, norm_bias
    )
    hidden_pre = matmul_low(normed_two, w_fc1)
    hidden = gelu_piece(hidden_pre, b_fc1)
    result = stream_two + (matmul_low(hidden, w_fc2) + b_fc2).reshape(stream_two.shape)
    saved = (
        tensor_in,
        normed_one,
        queries,
        keys_all,
        values_all,
        mixed,
        stream_one,
        attended,
        normed_two,
        hidden_pre,
        hidden,
    )
    return (result, saved)


def block_backward(saved, cotangent, params, is_first):
    (
        conv_weight,
        conv_bias,
        norm_gain,
        norm_bias,
        w_qkv,
        w_proj,
        b_proj,
        w_fc1,
        b_fc1,
        w_fc2,
        b_fc2,
    ) = params
    (
        tensor_in,
        normed_one,
        queries,
        keys_all,
        values_all,
        mixed,
        stream_one,
        attended,
        normed_two,
        hidden_pre,
        hidden,
    ) = saved
    image_count = tensor_in.shape[0]
    channels = tensor_in.shape[2]
    head_count = channels // 32
    grad_b_fc2 = jnp.sum(cotangent, axis=(0, 1))
    grad_out = cotangent.reshape(image_count * 49, channels)
    grad_hidden, grad_w_fc2 = matmul_back(hidden, w_fc2, grad_out)
    unused_gelu, gelu_pull = jax.vjp(gelu_piece, hidden_pre, b_fc1)
    grad_pre, grad_b_fc1 = gelu_pull(grad_hidden)
    grad_normed_two, grad_w_fc1 = matmul_back(normed_two, w_fc1, grad_pre)
    unused_second, second_pull = jax.vjp(
        second_piece, stream_one, attended, b_proj, conv_weight, conv_bias, norm_gain, norm_bias
    )
    grad_stream_one, grad_attended, grad_b_proj, conv_w_two, conv_b_two, gain_two, shift_two = (
        second_pull((cotangent, grad_normed_two))
    )
    grad_mixed, grad_w_proj = matmul_back(mixed, w_proj, grad_attended)
    grad_mixed = jnp.transpose(grad_mixed.reshape(image_count, 49, head_count, 32), (0, 2, 1, 3))
    grad_q, grad_k, grad_v = lax.cond(
        is_first, spatial_back, channel_back, queries, keys_all, values_all, grad_mixed
    )
    grad_packed = jnp.transpose(
        jnp.stack([grad_q, grad_k, grad_v], axis=1), (0, 3, 1, 2, 4)
    ).reshape(image_count * 49, 3 * channels)
    grad_normed_one, grad_w_qkv = matmul_back(normed_one, w_qkv, grad_packed)
    unused_first, first_pull = jax.vjp(
        first_piece, tensor_in, conv_weight, conv_bias, norm_gain, norm_bias
    )
    grad_in, conv_w_one, conv_b_one, gain_one, shift_one = first_pull(
        (grad_stream_one, grad_normed_one)
    )
    grads = (
        conv_w_one + conv_w_two,
        conv_b_one + conv_b_two,
        gain_one + gain_two,
        shift_one + shift_two,
        grad_w_qkv,
        grad_w_proj,
        grad_b_proj,
        grad_w_fc1,
        grad_b_fc1,
        grad_w_fc2,
        grad_b_fc2,
    )
    return (grad_in, grads)


def on_device(
    section_inputs,
    conv_weight,
    conv_bias,
    norm_gain,
    norm_bias,
    w_qkv,
    w_proj,
    b_proj,
    w_fc1,
    b_fc1,
    w_fc2,
    b_fc2,
):
    is_first = lax.axis_index("pipe") == 0
    params = tuple(
        (
            weight[0].astype(jnp.float32)
            for weight in (
                conv_weight,
                conv_bias,
                norm_gain,
                norm_bias,
                w_qkv,
                w_proj,
                b_proj,
                w_fc1,
                b_fc1,
                w_fc2,
                b_fc2,
            )
        )
    )
    image_count = section_inputs.shape[1]
    width = section_inputs.shape[3]
    pieces = section_inputs[0].reshape(MICRO, image_count // MICRO, 49, width)
    received = jnp.zeros(pieces.shape[1:], jnp.bfloat16)
    saved_all = []
    outputs = []
    for moment in range(MICRO + 1):
        own_piece = pieces[min(moment, MICRO - 1)].astype(jnp.float32)
        section_in = jnp.where(is_first, own_piece, received.astype(jnp.float32))
        result, saved = block_forward(section_in, params, is_first)
        saved_all.append(saved)
        outputs.append(result)
        if moment < MICRO:
            received = shifted(result.astype(jnp.bfloat16), "pipe", 1)
    grad_received = jnp.zeros(pieces.shape[1:], jnp.bfloat16)
    totals = jax.tree.map(jnp.zeros_like, params)
    input_grads = []
    for moment in range(MICRO + 1):
        own_piece = pieces[max(MICRO - 1 - moment, 0)].astype(jnp.float32)
        cotangent = jnp.where(is_first, grad_received.astype(jnp.float32), own_piece)
        saved = saved_all[MICRO - moment]
        input_grad, weight_grads = block_backward(saved, cotangent, params, is_first)
        valid = jnp.where(
            is_first, 1.0 if moment >= 1 else 0.0, 1.0 if moment < MICRO else 0.0
        ).astype(jnp.float32)
        totals = jax.tree.map(lambda running, fresh: running + fresh * valid, totals, weight_grads)
        input_grads.append(input_grad)
        if moment < MICRO:
            grad_received = shifted(input_grad.astype(jnp.bfloat16), "pipe", -1)
    grads_ordered = jnp.concatenate(
        [input_grads[MICRO - index_mb] for index_mb in range(MICRO)], axis=0
    )
    acts_ordered = jnp.concatenate([outputs[index_mb + 1] for index_mb in range(MICRO)], axis=0)
    section_ends = jnp.where(is_first, grads_ordered, acts_ordered)[None]
    summed = lax.psum(
        (
            totals[0][None],
            totals[1][None],
            totals[2][None],
            totals[3][None],
            totals[4][None],
            totals[5][None],
            totals[6][None],
            totals[7][None],
            totals[8][None],
            totals[9][None],
            totals[10][None],
        ),
        "dp",
    )
    return (
        section_ends,
        summed[0],
        summed[1],
        summed[2],
        summed[3],
        summed[4],
        summed[5],
        summed[6],
        summed[7],
        summed[8],
        summed[9],
        summed[10],
    )


def solution(mesh):
    return jax.shard_map(
        on_device,
        mesh=mesh,
        in_specs=(
            P("pipe", "dp", None, None),
            P("pipe", None, None, None),
            P("pipe", None, None),
            P("pipe", None, None),
            P("pipe", None, None),
            P("pipe", None, None),
            P("pipe", None, None),
            P("pipe", None),
            P("pipe", None, None),
            P("pipe", None),
            P("pipe", None, None),
            P("pipe", None),
        ),
        out_specs=(
            P("pipe", "dp", None, None),
            P("pipe", None, None, None),
            P("pipe", None, None),
            P("pipe", None, None),
            P("pipe", None, None),
            P("pipe", None, None),
            P("pipe", None, None),
            P("pipe", None),
            P("pipe", None, None),
            P("pipe", None),
            P("pipe", None, None),
            P("pipe", None),
        ),
        check_vma=False,
    )
```

profile of v0, /device:TPU:0, one launch (start us, length us, event | category | flops | bytes accessed | tf_op | source)
XLA Modules:
  0.0 1724.6 jit_solution(13377779418028994739)
XLA Ops:
  15.9 5.8 copy.213
  30.0 9.2 conditional.10
  62.3 9.3 multiply_convert_fusion.59
  90.9 9.2 conditional.11
  107.4 9.2 multiply_convert_fusion.58
  134.2 9.2 conditional.12
  150.7 9.2 multiply_convert_fusion.57
  176.9 9.6 conditional.13
  202.0 9.1 multiply_convert_fusion.56
  256.0 9.9 conditional.14
  282.5 9.1 multiply_convert_fusion.55
  299.0 7.5 fusion.564
  325.9 17.7 %conditional.15 = (bf16[4,1,24,49,32]{3,4,2,0,1:T(8,128)(2,1)}, bf16[4,1,24,49,32]{3,4,2,0,1:T(8,128)(2,1)}, bf16[4,1,24,49,32]{3,4,2,0,1:T(8,128)(2,1)S(1)}) conditional(s32[]{:T(128)} %convert_element_type.916, (f32[4,49,24,32]{1,3,2,0:T(8,128)}, bf16[4,24,49,32]{2,3,1,0:T(8,128)(2,1)}, bf16[4,49,24,32]{1,3,2,0:T(8,128)(2,1)}, ...), branch_computations={%region_52.56_spmd, %region_56.0_spmd} | conditional | flops 77728992 | bytes 24677348 | solution.py:210
  356.6 6.6 fusion.588
  406.6 7.5 fusion.565
  433.4 15.9 conditional.16
  459.6 6.7 fusion.589
  507.3 6.4 fusion.566
  531.9 15.9 conditional.17
  558.0 6.7 fusion.590
  605.0 7.4 fusion.567
  630.1 16.5 conditional.18
  703.7 7.4 fusion.568
  730.6 16.5 conditional.19
  784.7 17.3 %add_bitcast_fusion.1 = f32[1,768,3072]{2,1,0:T(8,128)} fusion(f32[768,3072]{1,0:T(8,128)} %fusion.591, f32[768,3072]{1,0:T(8,128)} %fusion.590, f32[768,3072]{1,0:T(8,128)} %fusion.589, f32[768,3072]{1,0:T(8,128)} %fusion.588, bf16[196,768]{1,0:T(8,128)(2,1)S(1)} %copy-done.197, bf16[196,3072]{1,0:T(8,128)(2,1)S(1)} %copy-done.123, f32[]{:T(128)S(6)} %select_n.119, ...), kind=kOutput, calls=%fused_computation.391 | convolution fusion | flops 938999808 | bytes 48691208 | tf_op jit(solution)/shard_map/...ij,...ik->...jk/dot_general | solution.py:32
  802.0 18.6 %add_bitcast_fusion = f32[1,3072,768]{2,1,0:T(8,128)} fusion(f32[3072,768]{1,0:T(8,128)} %fusion.595, f32[3072,768]{1,0:T(8,128)} %fusion.594, f32[3072,768]{1,0:T(8,128)} %fusion.593, f32[3072,768]{1,0:T(8,128)} %fusion.592, bf16[196,3072]{1,0:T(8,128)(2,1)} %copy-done.198, bf16[196,768]{1,0:T(8,128)(2,1)} %copy-done.195, f32[]{:T(128)S(6)} %select_n.119, ...), kind=kOutput, calls=%fused_computation.390 | convolution fusion | flops 938999808 | bytes 48691208 | tf_op jit(solution)/shard_map/...ij,...ik->...jk/dot_general | solution.py:32
  822.4 13.0 add_bitcast_fusion.2
  838.4 6.0 add_bitcast_fusion.3
  852.4 95.2 %all-reduce.235.cloned.1.call-done = (f32[1,2,9,768]{3,1,2,0:T(2,128)}, f32[1,2,768]{2,1,0:T(2,128)}, f32[1,2,768]{2,1,0:T(2,128)}, f32[1,2,768]{2,1,0:T(2,128)}...) async-done(((f32[1,2,9,768]{3,1,2,0:T(2,128)}, f32[1,2,768]{2,1,0:T(2,128)}, f32[1,2,768]{2,1,0:T(2,128)}, f32[1,2,768]{2,1,0:T(2,128)}, f32[1,768]{1,0:T(1,128)}, ...) | async-done | bytes 92176 | tf_op jit(solution)/shard_map/psum | solution.py:306
  947.6 742.4 %all-reduce.237.cloned.1.call-done = (f32[1,768,2304]{2,1,0:T(8,128)}, f32[1,768,768]{2,1,0:T(8,128)}, f32[1,768,3072]{2,1,0:T(8,128)}, f32[1,3072,768]{2,1,0:T(8,128)}) async-done(((f32[1,768,2304]{2,1,0:T(8,128)}, f32[1,768,768]{2,1,0:T(8,128)}, f32[1,768,3072]{2,1,0:T(8,128)}, f32[1,3072,768]{2,1,0:T(8,128)}), (f32[1,768,2304]{2,1,0:T(8,128)}, f32[1,768,768]{2,1,0:T(8,128)}, f32[1,768,3072]{2,1,0:T(8,128)}, ...) | async-done | bytes 28311568 | tf_op jit(solution)/shard_map/psum | solution.py:306
  1695.2 6.6 copy.568
  1703.8 8.8 copy.571
  (1298 shorter events, 688.3 us)
Async XLA Ops:
  7.2 35.1 %copy-start = (bf16[1,768,768]{2,1,0:T(8,128)(2,1)S(1)}, bf16[1,768,768]{2,1,0:T(8,128)(2,1)}, u32[]{:S(2)}) copy-start(bf16[1,768,768]{2,1,0:T(8,128)(2,1)} %param.38) | copy-start | bytes 3538948
  7.2 940.4 %all-reduce.235.cloned.1.call-start = ((), (), s32[]{:S(2)}) async-start(), calls=%async_computation | async-start | bytes 184320 | tf_op jit(solution)/shard_map/psum | solution.py:306
  10.3 66.4 %copy-start.32 = (bf16[1,4,49,768]{3,1,2,0:T(4,128)(2,1)}, bf16[1,4,49,768]{3,1,2,0:T(4,128)(2,1)S(1)}, u32[]{:S(2)}) copy-start(bf16[1,4,49,768]{3,1,2,0:T(4,128)(2,1)S(1)} %get-tuple-element.672) | copy-start | bytes 903172
  10.3 71.4 %copy-start.77 = (bf16[1,4,49,768]{3,1,2,0:T(4,128)(2,1)}, bf16[1,4,49,768]{3,1,2,0:T(4,128)(2,1)S(1)}, u32[]{:S(2)}) copy-start(bf16[1,4,49,768]{3,1,2,0:T(4,128)(2,1)S(1)} %get-tuple-element.670) | copy-start | bytes 903172
  45.6 26.0 %copy-start.373 = (f32[768]{0:T(1024)}, f32[768]{0:T(1024)S(1)}, u32[]{:S(2)}) copy-start(f32[768]{0:T(1024)S(1)} %reduce.53) | copy-start | bytes 9220
  79.1 2.5 collective-permute-start
  83.8 19.8 %copy-start.26 = (f32[4,49,768]{2,1,0:T(8,128)}, f32[4,49,768]{2,1,0:T(8,128)S(1)}, u32[]{:S(2)}) copy-start(f32[4,49,768]{2,1,0:T(8,128)S(1)} %get-tuple-element.546) | copy-start | bytes 1806340
  122.3 2.5 collective-permute-start.1
  127.0 20.0 %copy-start.28 = (f32[4,49,768]{2,1,0:T(8,128)}, f32[4,49,768]{2,1,0:T(8,128)S(1)}, u32[]{:S(2)}) copy-start(f32[4,49,768]{2,1,0:T(8,128)S(1)} %get-tuple-element.540) | copy-start | bytes 1806340
  165.6 2.5 collective-permute-start.2
  170.3 25.5 %copy-start.30 = (f32[4,49,768]{2,1,0:T(8,128)}, f32[4,49,768]{2,1,0:T(8,128)S(1)}, u32[]{:S(2)}) copy-start(f32[4,49,768]{2,1,0:T(8,128)S(1)} %get-tuple-element.534) | copy-start | bytes 1806340
  220.7 19.1 %collective-permute-start.3 = (bf16[4,49,768]{2,1,0:T(8,128)(2,1)}, bf16[4,49,768]{2,1,0:T(8,128)(2,1)}, u32[]{:S(2)}, u32[]{:S(2)}) collective-permute-start(bf16[4,49,768]{2,1,0:T(8,128)(2,1)} %get-tuple-element.642), channel_id=1, source_target_pairs={{0,16},{1,17},{2,18},{3,19},{4,20},{5,21},{6,22},{7,23},{8,24},{9,... | collective-permute-start | bytes 903176 | tf_op jit(solution)/shard_map/ppermute | solution.py:12
  395.4 7.8 collective-permute-start.4
  497.8 7.8 collective-permute-start.5
  596.3 7.8 collective-permute-start.6
  694.1 7.9 collective-permute-start.7
  784.7 37.3 %slice-start = ((s8[7077888]{0:T(1024)(128)(4,1)}), s8[4194304]{0:T(1024)(128)(4,1)S(1)}, s32[]{:S(2)}) async-start(s8[7077888]{0:T(1024)(128)(4,1)} %bitcast.923), calls=%async_computation.2 | async-start | bytes 8388608
  802.0 20.0 %slice-start.1 = ((s8[7077888]{0:T(1024)(128)(4,1)}), s8[2883584]{0:T(1024)(128)(4,1)S(1)}, s32[]{:S(2)}) async-start(s8[7077888]{0:T(1024)(128)(4,1)} %bitcast.923), calls=%async_computation.3 | async-start | bytes 5767168
  822.2 14.6 copy-start.338
  822.2 14.6 copy-start.339
  822.2 14.6 copy-start.344
  822.2 14.6 copy-start.345
  822.2 14.6 copy-start.350
  822.3 15.2 copy-start.234
  822.3 15.2 copy-start.235
  822.3 15.2 copy-start.236
  822.3 15.2 copy-start.237
  822.3 15.1 copy-start.238
  822.3 15.1 copy-start.239
  822.4 15.1 copy-start.240
  822.4 15.1 copy-start.241
  838.4 851.6 %all-reduce.237.cloned.1.call-start = ((), (), s32[]{:S(2)}) async-start(), calls=%async_computation.1 | async-start | bytes 56623104 | tf_op jit(solution)/shard_map/psum | solution.py:306
  (349 other events, 1736.3 us)
Sparse Core Ops, SparseCore 0:
  838.5 109.0 all-reduce.234
  955.1 734.7 all-reduce.236
where the time goes:
time: 1740 us; the launch traced here: 1720 us
  waiting for transfers between devices  840 us (48%)
  matrix products  397 us (23%)
  local copies, waits for them, and re-layouts  307 us (18%)
  other arithmetic  145 us (8%)
  between operations  18.9 us (1%)
    psum x2, waiting for transfers between devices, on_device(): lax.psum((totals[0][None], totals[1][None], totals[2][None], totals[3][No...  838 us
    dot_general x30, matrix products, matmul_back(): jnp.einsum('...ij,...ik->...jk', left.astype(jnp.bfloat16), grad_low, pre...  156 us
    dot_general x35, matrix products, matmul_low(): jnp.einsum('...ij,...jk->...ik', left.astype(jnp.bfloat16), right.astype(...  126 us
    dot_general x30, matrix products, matmul_back(): jnp.einsum('...ik,...jk->...ij', grad_low, right.astype(jnp.bfloat16), pr...  116 us
    convert_element_type x30, local copies, waits for them, and re-layouts, matmul_back(): grad_low = grad.astype(jnp.bfloat16)  101 us
    unnamed x697, local copies, waits for them, and re-layouts  69.4 us
  transfers between devices with their start and end apart: 10, of which 5 were waited for; matrix products, arithmetic and copies ran while one was open for 3% of the time, Pallas kernels for 0%

commit v1 on v0

--- a/solution.py
+++ b/solution.py
@@ -1,7 +1,355 @@
+import functools
 import jax
 import jax.numpy as jnp
 from jax import lax
+from jax.experimental import pallas as pl
+from jax.experimental.pallas import tpu as pltpu
 from jax.sharding import PartitionSpec as P
+
+MESH = pl.DeviceIdType.MESH
+
+
+def dp_dims(n):
+    sizes = [1, 1, 1]
+    at = 0
+    left = n
+    while left > 1:
+        factor = 2 if left % 2 == 0 else left
+        sizes[at % 3] *= factor
+        left //= factor
+        at += 1
+    return tuple(sizes), (sizes[1] * sizes[2], sizes[2], 1)
+
+
+class Place:
+    def __init__(self, dp, size, stride):
+        self.size = size
+        pos = lax.rem(lax.div(dp, stride), size)
+        low = pos < (size + 1) // 2
+        self.outer = jnp.where(low, pos, size - 1 - pos)
+        self.pos = pos
+        self.low = low
+        step = jnp.where(low, stride, -stride)
+        self.inner_peer = dp + step
+        self.outer_peer = dp - step
+
+
+def pick(flag, a, b):
+    out = object.__new__(Place)
+    out.size = a.size
+    for name in ("pos", "low", "outer", "inner_peer", "outer_peer"):
+        setattr(out, name, jnp.where(flag, getattr(a, name), getattr(b, name)))
+    return out
+
+
+class Ring:
+    def __init__(self, dp, dims, rows, grad, land, out, send, recv, local):
+        (s0, s1, s2), (t0, t1, t2) = dims
+        self.mids = Place(dp, s0, t0)
+        self.fast, self.slow = Place(dp, s2, t2), Place(dp, s1, t1)
+        self.dp, self.rows = dp, rows
+        self.grad, self.land, self.out = grad, land, out
+        self.send, self.recv, self.local = send, recv, local
+        self.sizes = (s2, s0, s1)
+        self.lens = (rows // s2, rows // s2 // s0, rows // (s0 * s1 * s2))
+
+    @staticmethod
+    def land_rows(rows, dims):
+        s0, s1, s2 = dims[0]
+        lens = (rows // s2, rows // s2 // s0, rows // (s0 * s1 * s2))
+        total, starts = 0, []
+        for n, length in zip((s2, s0, s1), lens):
+            starts.append(total)
+            total += length * (1 if n == 2 else 5)
+        return total, starts
+
+    def level(self, c, i):
+        flag = lax.rem(c, 2) == 0
+        if i == 1:
+            return self.mids
+        return pick(flag, self.fast, self.slow) if i == 0 else pick(flag, self.slow, self.fast)
+
+    def base(self, c, i):
+        start = 0
+        for j in range(i):
+            start = start + self.level(c, j).pos * self.lens[j]
+        return start
+
+    def span(self, c, i, a, b):
+        place, length = self.level(c, i), self.lens[i]
+        n = self.sizes[i]
+        start = self.base(c, i) + jnp.where(place.low, a * length, (n - b) * length)
+        return pl.ds(pl.multiple_of(start, 8), (b - a) * length)
+
+    def copy(self, c, ev, src, dst, peer):
+        return pltpu.make_async_remote_copy(
+            src_ref=src, dst_ref=dst, send_sem=self.send.at[c, ev], recv_sem=self.recv.at[c, ev],
+            device_id={"dp": peer}, device_id_type=MESH)
+
+    def landing(self, c, i, at, length):
+        start = self.land_rows(self.rows, ((self.sizes[1], self.sizes[2], self.sizes[0]), None))[1][i]
+        return self.land.at[c, pl.ds(start + at, length)]
+
+    def add(self, c, i, a, b, at, lo=None):
+        rows = self.span(c, i, a, b)
+        length = (b - a) * self.lens[i]
+        got = self.landing(c, i, at, length)
+        self.grad[c, rows] = self.grad[c, rows] + got[...]
+
+    def reduce_send(self, c, i, ev, a, b, at, peer):
+        rows = self.span(c, i, a, b)
+        length = (b - a) * self.lens[i]
+        return self.copy(c, ev, self.grad.at[c, rows], self.landing(c, i, at, length), peer)
+
+    def reduce_stages(self, i):
+        n, length = self.sizes[i], self.lens[i]
+        ein, eout = 2 * i, 2 * i + 1
+        if n == 1:
+            return []
+        if n == 2:
+            def first(c):
+                self.reduce_send(c, i, eout, 1, 2, 0, self.level(c, i).inner_peer).start()
+
+            def last(c):
+                self.reduce_send(c, i, eout, 0, 1, 0, self.level(c, i).inner_peer).wait_recv()
+                self.add(c, i, 0, 1, 0)
+            return [first, last]
+
+        def zero(c):
+            place = self.level(c, i)
+
+            @pl.when(place.outer == 0)
+            def _():
+                self.reduce_send(c, i, ein, 1, 4, 0, place.inner_peer).start()
+
+        def one(c):
+            place = self.level(c, i)
+
+            @pl.when(place.outer == 1)
+            def _():
+                self.reduce_send(c, i, ein, 1, 4, 0, place.inner_peer).wait_recv()
+                self.add(c, i, 1, 4, 0)
+                self.reduce_send(c, i, eout, 2, 4, 3 * length, place.inner_peer).start()
+
+        def two(c):
+            place = self.level(c, i)
+
+            @pl.when(place.outer == 1)
+            def _():
+                self.reduce_send(c, i, eout, 0, 2, 3 * length, place.inner_peer).wait_recv()
+                self.add(c, i, 0, 2, 3 * length)
+                self.reduce_send(c, i, ein, 0, 1, 3 * length, place.outer_peer).start()
+
+        def three(c):
+            place = self.level(c, i)
+
+            @pl.when(place.outer == 0)
+            def _():
+                self.reduce_send(c, i, ein, 0, 1, 3 * length, place.inner_peer).wait_recv()
+                self.add(c, i, 0, 1, 3 * length)
+        return [zero, one, two, three]
+
+    def reduce_ends(self, i):
+        n = self.sizes[i]
+        ein, eout = 2 * i, 2 * i + 1
+
+        def ends(c):
+            place = self.level(c, i)
+            if n == 2:
+                self.reduce_send(c, i, eout, 1, 2, 0, place.inner_peer).wait_send()
+            elif n == 4:
+                @pl.when(place.outer == 0)
+                def _():
+                    self.reduce_send(c, i, ein, 1, 4, 0, place.inner_peer).wait_send()
+
+                @pl.when(place.outer == 1)
+                def _():
+                    self.reduce_send(c, i, eout, 2, 4, 0, place.inner_peer).wait_send()
+                    self.reduce_send(c, i, ein, 0, 1, 0, place.outer_peer).wait_send()
+        return ends
+
+    def gather_send(self, c, i, ev, a, b, peer):
+        rows = self.span(c, i, a, b)
+        dst = self.out.at[c, rows]
+        return self.copy(c, ev, dst, dst, peer)
+
+    def gather_stages(self, i):
+        n = self.sizes[i]
+        ein, eout = 6 + 2 * i, 7 + 2 * i
+        if n == 1:
+            return []
+        if n == 2:
+            def first(c):
+                self.gather_send(c, i, eout, 0, 1, self.level(c, i).inner_peer).start()
+
+            def last(c):
+                self.gather_send(c, i, eout, 1, 2, self.level(c, i).inner_peer).wait_recv()
+            return [first, last]
+
+        def zero(c):
+            place = self.level(c, i)
+
+            @pl.when(place.outer == 0)
+            def _():
+                self.gather_send(c, i, ein, 0, 1, place.inner_peer).start()
+
+        def one(c):
+            place = self.level(c, i)
+
+            @pl.when(place.outer == 1)
+            def _():
+                self.gather_send(c, i, ein, 0, 1, place.outer_peer).wait_recv()
+                self.gather_send(c, i, eout, 0, 2, place.inner_peer).start()
+
+        def two(c):
+            place = self.level(c, i)
+
+            @pl.when(place.outer == 1)
+            def _():
+                self.gather_send(c, i, eout, 2, 4, place.inner_peer).wait_recv()
+                self.gather_send(c, i, ein, 1, 4, place.outer_peer).start()
+
+        def three(c):
+            place = self.level(c, i)
+
+            @pl.when(place.outer == 0)
+            def _():
+                self.gather_send(c, i, ein, 1, 4, place.inner_peer).wait_recv()
+        return [zero, one, two, three]
+
+    def gather_ends(self, i):
+        n = self.sizes[i]
+        ein, eout = 6 + 2 * i, 7 + 2 * i
+
+        def ends(c):
+            place = self.level(c, i)
+            if n == 2:
+                self.gather_send(c, i, eout, 0, 1, place.inner_peer).wait_send()
+            elif n == 4:
+                @pl.when(place.outer == 0)
+                def _():
+                    self.gather_send(c, i, ein, 0, 1, place.inner_peer).wait_send()
+
+                @pl.when(place.outer == 1)
+                def _():
+                    self.gather_send(c, i, eout, 0, 2, place.inner_peer).wait_send()
+                    self.gather_send(c, i, ein, 1, 4, place.outer_peer).wait_send()
+        return ends
+
+    def own_copy(self, c):
+        start = self.base(c, 3)
+        rows = pl.ds(pl.multiple_of(start, 8), self.lens[2])
+        return pltpu.make_async_copy(self.grad.at[c, rows], self.out.at[c, rows], self.local.at[c])
+
+    def stages(self):
+        groups = [self.reduce_stages(0), self.reduce_stages(1), self.reduce_stages(2)]
+
+        def settle(c):
+            self.own_copy(c).start()
+            self.own_copy(c).wait()
+        groups += [[settle], self.gather_stages(2), self.gather_stages(1), self.gather_stages(0)]
+        joined = []
+        for group in groups:
+            if not group:
+                continue
+            if joined:
+                joined[-1] = joined[-1] + [group[0]]
+                joined += [[stage] for stage in group[1:]]
+            else:
+                joined = [[stage] for stage in group]
+        return [functools.partial(run_all, stages) for stages in joined]
+
+    def ends(self, c):
+        for i in range(3):
+            if self.sizes[i] > 1:
+                self.reduce_ends(i)(c)
+                self.gather_ends(i)(c)
+
+    def greet(self):
+        barrier = pltpu.get_barrier_semaphore()
+        count = jnp.int32(0)
+        for place in (self.fast, self.mids, self.slow):
+            if place.size == 1:
+                continue
+            pl.semaphore_signal(barrier, inc=1, device_id={"dp": place.inner_peer}, device_id_type=MESH)
+            count = count + 1
+            if place.size == 4:
+                @pl.when(place.outer == 1)
+                def _():
+                    pl.semaphore_signal(barrier, inc=1, device_id={"dp": place.outer_peer}, device_id_type=MESH)
+                count = count + jnp.where(place.outer == 1, 1, 0)
+        pl.semaphore_wait(barrier, count)
+
+
+def run_all(stages, c):
+    for stage in stages:
+        stage(c)
+
+
+def ar_kernel(dims, count, rows, small_rows, lead, src, small_src, out, small_out,
+              grad, land, small_grad, small_land, load, send, recv, local, ssend, srecv, slocal):
+    dp = lax.axis_index("dp")
+    main = Ring(dp, dims, rows, grad, land, out, send, recv, local)
+    small = Ring(dp, dims, small_rows, small_grad, small_land, small_out, ssend, srecv, slocal)
+
+    @pl.loop(0, count)
+    def _(c):
+        pltpu.make_async_copy(src.at[c], grad.at[c], load.at[c]).start()
+    pltpu.make_async_copy(small_src, small_grad, load.at[count]).start()
+    main.greet()
+    stages, small_stages = main.stages(), small.stages()
+    depth = len(stages)
+
+    @pl.loop(0, count + 1 + lead + depth)
+    def _(t):
+        for s in reversed(range(depth)):
+            c = t - s - (lead if s else 0)
+
+            @pl.when((c >= 0) & (c < count))
+            def _():
+                if s == 0:
+                    pltpu.make_async_copy(src.at[c], grad.at[c], load.at[c]).wait()
+                stages[s](c)
+
+            @pl.when(c == count)
+            def _():
+                if s == 0:
+                    pltpu.make_async_copy(small_src, small_grad, load.at[count]).wait()
+                small_stages[s](0)
+
+    @pl.loop(0, count)
+    def _(c):
+        main.ends(c)
+    small.ends(0)
+
+
+def all_reduce(src, small, n, lead=1, collective_id=0):
+    dims = dp_dims(n)
+    count, rows, width = src.shape
+    small_rows = small.shape[1]
+    land, _ = Ring.land_rows(rows, dims)
+    small_land, _ = Ring.land_rows(small_rows, dims)
+    return pl.pallas_call(
+        functools.partial(ar_kernel, dims, count, rows, small_rows, lead),
+        out_shape=(jax.ShapeDtypeStruct(src.shape, src.dtype), jax.ShapeDtypeStruct(small.shape, small.dtype)),
+        in_specs=[pl.BlockSpec(memory_space=pl.ANY)] * 2,
+        out_specs=(pl.BlockSpec(memory_space=pl.ANY),) * 2,
+        scratch_shapes=[
+            pltpu.VMEM((count, rows, width), src.dtype),
+            pltpu.VMEM((count, land, width), src.dtype),
+            pltpu.VMEM(small.shape, small.dtype),
+            pltpu.VMEM((1, small_land, small.shape[2]), small.dtype),
+            pltpu.SemaphoreType.DMA((count + 1,)),
+            pltpu.SemaphoreType.DMA((count, 12)),
+            pltpu.SemaphoreType.DMA((count, 12)),
+            pltpu.SemaphoreType.DMA((count,)),
+            pltpu.SemaphoreType.DMA((1, 12)),
+            pltpu.SemaphoreType.DMA((1, 12)),
+            pltpu.SemaphoreType.DMA((1,)),
+        ],
+        compiler_params=pltpu.CompilerParams(collective_id=collective_id, has_side_effects=True, vmem_limit_bytes=62 * 2**20),
+    )(src, small)
+
 
 MICRO = 4
 
@@ -303,36 +651,49 @@
     )
     acts_ordered = jnp.concatenate([outputs[index_mb + 1] for index_mb in range(MICRO)], axis=0)
     section_ends = jnp.where(is_first, grads_ordered, acts_ordered)[None]
-    summed = lax.psum(
-        (
-            totals[0][None],
-            totals[1][None],
-            totals[2][None],
-            totals[3][None],
-            totals[4][None],
-            totals[5][None],
-            totals[6][None],
-            totals[7][None],
-            totals[8][None],
-            totals[9][None],
-            totals[10][None],
-        ),
-        "dp",
-    )
-    return (
-        section_ends,
-        summed[0],
-        summed[1],
-        summed[2],
-        summed[3],
-        summed[4],
-        summed[5],
-        summed[6],
-        summed[7],
-        summed[8],
-        summed[9],
-        summed[10],
-    )
+    names = len(totals)
+    small = jnp.concatenate([totals[i].reshape(-1) for i in (0, 1, 2, 3, 6, 8, 10)])
+    lanes = 128
+    small_rows = 16 * lax.axis_size("dp")
+    small = jnp.pad(small, (0, small_rows * lanes - small.shape[0])).reshape(1, small_rows, lanes)
+    big = [to_chunks(totals[i].astype(jnp.bfloat16)) for i in (9, 7, 5, 4)]
+    counts = [v.shape[0] for v in big]
+    rows = padded_rows(width, lax.axis_size("dp"))
+    stacked = jnp.pad(jnp.concatenate(big, axis=0), ((0, 0), (0, rows - width), (0, 0)))
+    done, small_done = all_reduce(stacked, small, lax.axis_size("dp"))
+    done = done[:, :width]
+    small_done = small_done.reshape(-1)
+    summed = [None] * names
+    at = 0
+    for i in (0, 1, 2, 3, 6, 8, 10):
+        summed[i] = small_done[at : at + totals[i].size].reshape(totals[i].shape)[None]
+        at += totals[i].size
+    at = 0
+    for i, number in zip((9, 7, 5, 4), counts):
+        summed[i] = from_chunks(done[at : at + number], totals[i].shape)[None]
+        at += number
+    return (section_ends, *summed)
+
+
+CHUNK = 384
+
+
+def padded_rows(rows, n):
+    return -(-rows // (16 * n)) * 16 * n
+
+
+def to_chunks(grad):
+    rows, columns = grad.shape
+    side = 768
+    cut = grad.reshape(rows // side, side, columns // CHUNK, CHUNK)
+    return jnp.transpose(cut, (0, 2, 1, 3)).reshape(-1, side, CHUNK)
+
+
+def from_chunks(chunks, shape):
+    rows, columns = shape
+    side = 768
+    cut = chunks.reshape(rows // side, columns // CHUNK, side, CHUNK)
+    return jnp.transpose(cut, (0, 2, 1, 3)).reshape(shape).astype(jnp.float32)
 
 
 def solution(mesh):

time: 1740 us -> 1230 us (0.71)
  waiting for transfers between devices: 840 us -> 2.92 us
  Pallas kernels: 0 us -> 232 us
  local copies, waits for them, and re-layouts: 307 us -> 397 us
  other arithmetic: 145 us -> 174 us
    psum x2 -> x0, waiting for transfers between devices: 838 us -> none  [on_device(): lax.psum((totals[0][None], totals[1][None], totals[2][None], totals[3][No...]
    pallas_call x0 -> x1, Pallas kernels: none -> 232 us  [all_reduce(): pl.pallas_call(functools.partial(ar_kernel, dims, count, rows, small_rows...]
    convert_element_type x0 -> x7, local copies, waits for them, and re-layouts: none -> 59.5 us  [the longest x5 47.2 us: from_chunks(): return jnp.transpose(cut, (0, 2, 1, 3)).reshape(shape).astype(jnp.float32)]
    reshape x0 -> x10, local copies, waits for them, and re-layouts: none -> 28.2 us  [the longest x5 27.5 us: to_chunks(): cut = grad.reshape(rows // side, side, columns // CHUNK, CHUNK)]
    unnamed x697 -> x695, local copies, waits for them, and re-layouts: 69.4 us -> 67.8 us
  transfers between devices with their start and end apart: 10 -> 8, of which waited for: 5 -> 3; matrix products, arithmetic and copies ran while one was open for 3% -> 4% of each run, Pallas kernels for 0% -> 0%
where the time goes in v1:
time: 1230 us; the launch traced here: 1220 us
  local copies, waits for them, and re-layouts  397 us (32%)
  matrix products  391 us (32%)
  Pallas kernels  232 us (19%)
  other arithmetic  174 us (14%)
  starting transfers between devices  14.2 us (1%)
    pallas_call x1, Pallas kernels, all_reduce(): pl.pallas_call(functools.partial(ar_kernel, dims, count, rows, small_rows...  232 us
    dot_general x30, matrix products, matmul_back(): jnp.einsum('...ij,...ik->...jk', left.astype(jnp.bfloat16), grad_low, pre...  148 us
    dot_general x35, matrix products, matmul_low(): jnp.einsum('...ij,...jk->...ik', left.astype(jnp.bfloat16), right.astype(...  126 us
    dot_general x30, matrix products, matmul_back(): jnp.einsum('...ik,...jk->...ij', grad_low, right.astype(jnp.bfloat16), pr...  116 us
    convert_element_type x30, local copies, waits for them, and re-layouts, matmul_back(): grad_low = grad.astype(jnp.bfloat16)  101 us
    unnamed x695, local copies, waits for them, and re-layouts  67.8 us
    convert_element_type x5, local copies, waits for them, and re-layouts, from_chunks(): return jnp.transpose(cut, (0, 2, 1, 3)).reshape(shape).astype(jnp.float32)  47.2 us
    convert_element_type x20, local copies, waits for them, and re-layouts, matmul_low(): left.astype(jnp.bfloat16)  32.1 us
  transfers between devices with their start and end apart: 8, of which 3 were waited for; matrix products, arithmetic and copies ran while one was open for 4% of the time, Pallas kernels for 0%

profile of v1, /device:TPU:0, one launch (start us, length us, event | category | flops | bytes accessed | tf_op | source)
XLA Modules:
  0.0 1218.4 jit_solution(5585905047386140369)
XLA Ops:
  23.4 9.2 conditional.10
  55.7 9.3 multiply_convert_fusion.59
  84.3 9.2 conditional.11
  100.8 9.2 multiply_convert_fusion.58
  127.5 9.2 conditional.12
  144.1 9.2 multiply_convert_fusion.57
  170.3 9.6 conditional.13
  195.3 9.1 multiply_convert_fusion.56
  249.3 10.2 conditional.14
  276.2 9.1 multiply_convert_fusion.55
  292.6 7.5 fusion.565
  319.5 17.6 %conditional.15 = (bf16[4,1,24,49,32]{3,4,2,0,1:T(8,128)(2,1)}, bf16[4,1,24,49,32]{3,4,2,0,1:T(8,128)(2,1)}, bf16[4,1,24,49,32]{3,4,2,0,1:T(8,128)(2,1)S(1)}) conditional(s32[]{:T(128)} %convert_element_type.1006, (f32[4,49,24,32]{1,3,2,0:T(8,128)}, bf16[4,24,49,32]{2,3,1,0:T(8,128)(2,1)}, bf16[4,49,24,32]{1,3,2,0:T(8,128)(2,1)}, ...), branch_computations={%region_52.56_spmd, %region_56.0_spmd} | conditional | flops 77728992 | bytes 24677348 | solution.py:558
  397.8 7.5 fusion.566
  424.7 15.8 %conditional.16 = (bf16[4,1,24,49,32]{3,4,2,0,1:T(8,128)(2,1)}, bf16[4,1,24,49,32]{3,4,2,0,1:T(8,128)(2,1)}, bf16[4,1,24,49,32]{3,4,2,0,1:T(8,128)(2,1)S(1)}) conditional(s32[]{:T(128)} %convert_element_type.1006, (f32[4,49,24,32]{1,3,2,0:T(8,128)}, bf16[4,24,49,32]{2,3,1,0:T(8,128)(2,1)}, bf16[4,49,24,32]{1,3,2,0:T(8,128)(2,1)}, ...), branch_computations={%region_64.0_spmd, %region_68.0_spmd} | conditional | flops 77728992 | bytes 21139912 | solution.py:558
  523.1 15.8 %conditional.17 = (bf16[4,1,24,49,32]{3,4,2,0,1:T(8,128)(2,1)}, bf16[4,1,24,49,32]{3,4,2,0,1:T(8,128)(2,1)}, bf16[4,1,24,49,32]{3,4,2,0,1:T(8,128)(2,1)S(1)}) conditional(s32[]{:T(128)} %convert_element_type.1006, (f32[4,49,24,32]{1,3,2,0:T(8,128)}, bf16[4,24,49,32]{2,3,1,0:T(8,128)(2,1)}, bf16[4,49,24,32]{1,3,2,0:T(8,128)(2,1)}, ...), branch_computations={%region_76.0_spmd, %region_80.0_spmd} | conditional | flops 77728992 | bytes 21139912 | solution.py:558
  595.6 7.4 fusion.568
  620.7 16.3 %conditional.18 = (bf16[4,1,24,49,32]{3,4,2,0,1:T(8,128)(2,1)}, bf16[4,1,24,49,32]{3,4,2,0,1:T(8,128)(2,1)}, bf16[4,1,24,49,32]{3,4,2,0,1:T(8,128)(2,1)S(1)}) conditional(s32[]{:T(128)} %convert_element_type.1006, (f32[4,49,24,32]{1,3,2,0:T(8,128)}, bf16[4,24,49,32]{2,3,1,0:T(8,128)(2,1)}, bf16[4,49,24,32]{1,3,2,0:T(8,128)(2,1)}, ...), branch_computations={%region_88.0_spmd, %region_92.0_spmd} | conditional | flops 77728992 | bytes 22268872 | solution.py:558
  694.7 7.4 fusion.569
  720.6 16.4 %conditional.19 = (bf16[4,1,24,49,32]{3,4,2,0,1:T(8,128)(2,1)}, bf16[4,1,24,49,32]{3,4,2,0,1:T(8,128)(2,1)}, bf16[4,1,24,49,32]{3,4,2,0,1:T(8,128)(2,1)S(1)}) conditional(s32[]{:T(128)} %convert_element_type.1006, (f32[4,49,24,32]{1,3,2,0:T(8,128)}, bf16[4,24,49,32]{2,3,1,0:T(8,128)(2,1)}, bf16[4,49,24,32]{1,3,2,0:T(8,128)(2,1)}, ...), branch_computations={%region_100.104_spmd, %region_104.108_spmd} | conditional | flops 77728992 | bytes 22268872 | solution.py:558
  789.7 12.1 add_convert_fusion.2
  813.8 15.4 %add_convert_fusion = bf16[768,3072]{1,0:T(8,128)(2,1)} fusion(f32[768,3072]{1,0:T(8,128)} %fusion.589, f32[768,3072]{1,0:T(8,128)} %fusion.588, f32[768,3072]{1,0:T(8,128)} %fusion.587, f32[768,3072]{1,0:T(8,128)} %fusion.586, bf16[196,768]{1,0:T(8,128)(2,1)S(1)} %copy-done.200, bf16[196,3072]{1,0:T(8,128)(2,1)S(1)} %copy-done.121, f32[]{:T(128)S(6)} %select_n.119, ...), kind=kOutput, calls=%fused_computation.393 | convolution fusion | flops 941359104 | bytes 43972616 | tf_op jit(solution)/shard_map/...ij,...ik->...jk/dot_general | solution.py:380
  842.5 15.4 %add_convert_fusion.1 = bf16[3072,768]{1,0:T(8,128)(2,1)} fusion(f32[3072,768]{1,0:T(8,128)} %fusion.585, f32[3072,768]{1,0:T(8,128)} %fusion.584, f32[3072,768]{1,0:T(8,128)} %fusion.583, f32[3072,768]{1,0:T(8,128)} %fusion.582, bf16[196,3072]{1,0:T(8,128)(2,1)S(1)} %copy-done.202, bf16[196,768]{1,0:T(8,128)(2,1)S(1)} %copy-done.198, f32[]{:T(128)S(6)} %select_n.119, ...), kind=kOutput, calls=%fused_computation.394 | convolution fusion | flops 941359104 | bytes 43972616 | tf_op jit(solution)/shard_map/...ij,...ik->...jk/dot_general | solution.py:380
  857.9 10.1 reshape.1626
  873.0 6.9 pad_maximum_fusion.src
  879.8 231.9 %shard_map.211 = (bf16[24,768,384]{2,1,0:T(8,128)(2,1)}, f32[1,256,128]{2,1,0:T(8,128)}) custom-call(bf16[24,768,384]{2,1,0:T(8,128)(2,1)} %pad_maximum_fusion.src, f32[1,256,128]{2,1,0:T(8,128)} %pad_bitcast_fusion.small_src), custom_call_target="tpu_custom_call" | custom-call | tf_op jit(solution)/shard_map/pallas_call | solution.py:332
  1123.5 10.4 fusion.564
  1152.2 8.0 copy.310
  1160.2 8.0 copy.316
  1171.2 14.6 %copy.313 = f32[4,768,2,384]{3,2,1,0:T(2,128)} copy(f32[4,768,2,384]{3,1,2,0:T(8,128)S(1)} %convert_bitcast_fusion) | data formatting | bytes 18874368 | tf_op jit(solution)/shard_map/convert_element_type | solution.py:696
  1185.8 13.0 %reshape.1676 = f32[1,3072,768]{2,1,0:T(8,128)} reshape(f32[4,768,2,384]{3,2,1,0:T(2,128)} %copy.313) | data formatting | bytes 18874368 | tf_op jit(solution)/shard_map/convert_element_type | solution.py:696
  1198.8 9.6 copy.312
  1208.4 9.6 copy.318
  (1308 shorter events, 769.9 us)
Async XLA Ops:
  0.6 35.0 %copy-start = (bf16[1,768,768]{2,1,0:T(8,128)(2,1)S(1)}, bf16[1,768,768]{2,1,0:T(8,128)(2,1)}, u32[]{:S(2)}) copy-start(bf16[1,768,768]{2,1,0:T(8,128)(2,1)} %param.38) | copy-start | bytes 3538948
  3.7 66.4 %copy-start.32 = (bf16[1,4,49,768]{3,1,2,0:T(4,128)(2,1)}, bf16[1,4,49,768]{3,1,2,0:T(4,128)(2,1)S(1)}, u32[]{:S(2)}) copy-start(bf16[1,4,49,768]{3,1,2,0:T(4,128)(2,1)S(1)} %get-tuple-element.667) | copy-start | bytes 903172
  3.7 71.4 %copy-start.78 = (bf16[1,4,49,768]{3,1,2,0:T(4,128)(2,1)}, bf16[1,4,49,768]{3,1,2,0:T(4,128)(2,1)S(1)}, u32[]{:S(2)}) copy-start(bf16[1,4,49,768]{3,1,2,0:T(4,128)(2,1)S(1)} %get-tuple-element.665) | copy-start | bytes 903172
  4.0 11.1 copy-start.92
  39.0 26.0 %copy-start.377 = (f32[768]{0:T(1024)}, f32[768]{0:T(1024)S(1)}, u32[]{:S(2)}) copy-start(f32[768]{0:T(1024)S(1)} %reduce.53) | copy-start | bytes 9220
  53.8 12.2 %slice-start.2 = ((s8[4718592]{0:T(1024)(128)(4,1)}), s8[4194304]{0:T(1024)(128)(4,1)S(1)}, s32[]{:S(2)}) async-start(s8[4718592]{0:T(1024)(128)(4,1)} %bitcast.1059), calls=%async_computation.2 | async-start | bytes 8388608
  72.5 2.5 collective-permute-start
  77.2 19.8 %copy-start.26 = (f32[4,49,768]{2,1,0:T(8,128)}, f32[4,49,768]{2,1,0:T(8,128)S(1)}, u32[]{:S(2)}) copy-start(f32[4,49,768]{2,1,0:T(8,128)S(1)} %get-tuple-element.539) | copy-start | bytes 1806340
  100.2 14.5 %copy-start.18 = (f32[4,49,768]{2,1,0:T(8,128)}, f32[4,49,768]{2,1,0:T(8,128)S(1)}, u32[]{:S(2)}) copy-start(f32[4,49,768]{2,1,0:T(8,128)S(1)} %get-tuple-element.537) | copy-start | bytes 1806340
  115.7 2.5 collective-permute-start.1
  120.4 19.9 %copy-start.28 = (f32[4,49,768]{2,1,0:T(8,128)}, f32[4,49,768]{2,1,0:T(8,128)S(1)}, u32[]{:S(2)}) copy-start(f32[4,49,768]{2,1,0:T(8,128)S(1)} %get-tuple-element.533) | copy-start | bytes 1806340
  143.5 14.5 %copy-start.20 = (f32[4,49,768]{2,1,0:T(8,128)}, f32[4,49,768]{2,1,0:T(8,128)S(1)}, u32[]{:S(2)}) copy-start(f32[4,49,768]{2,1,0:T(8,128)S(1)} %get-tuple-element.531) | copy-start | bytes 1806340
  159.0 2.5 collective-permute-start.2
  163.7 25.5 %copy-start.30 = (f32[4,49,768]{2,1,0:T(8,128)}, f32[4,49,768]{2,1,0:T(8,128)S(1)}, u32[]{:S(2)}) copy-start(f32[4,49,768]{2,1,0:T(8,128)S(1)} %get-tuple-element.527) | copy-start | bytes 1806340
  192.3 12.1 copy-start.257
  192.6 11.9 copy-start.283
  192.6 11.9 copy-start.269
  211.9 12.4 %copy-start.243 = (f32[4,7,7]{0,2,1:T(8,128)S(1)}, f32[4,7,7]{0,2,1:T(8,128)}, u32[]{:S(2)}) copy-start(f32[4,7,7]{0,2,1:T(8,128)} %get-tuple-element.764) | copy-start | bytes 2356
  214.0 19.1 %collective-permute-start.3 = (bf16[4,49,768]{2,1,0:T(8,128)(2,1)}, bf16[4,49,768]{2,1,0:T(8,128)(2,1)}, u32[]{:S(2)}, u32[]{:S(2)}) collective-permute-start(bf16[4,49,768]{2,1,0:T(8,128)(2,1)} %get-tuple-element.637), channel_id=1, source_target_pairs={{0,16},{1,17},{2,18},{3,19},{4,20},{5,21},{6,22},{7,23},{8,24},{9,... | collective-permute-start | bytes 903176 | tf_op jit(solution)/shard_map/ppermute | solution.py:360
  385.3 9.2 collective-permute-start.4
  457.6 11.0 copy-start.87
  487.7 9.2 collective-permute-start.5
  556.0 11.0 copy-start.88
  586.0 8.6 collective-permute-start.6
  683.8 9.3 collective-permute-start.7
  744.8 11.2 copy-start.130
  857.9 13.3 %slice-start = ((s8[4718592]{0:T(1024)(128)(4,1)}), s8[524288]{0:T(1024)(128)(4,1)S(1)}, s32[]{:S(2)}) async-start(s8[4718592]{0:T(1024)(128)(4,1)} %bitcast.978), calls=%async_computation | async-start | bytes 1048576
  1123.5 10.5 copy-start.173
  1123.5 10.5 copy-start.174
  1123.5 10.5 copy-start.175
  1123.5 10.9 copy-start.171
  1123.5 10.9 copy-start.172
  (346 other events, 1516.8 us)

commit v2 on v1

v2 whole, which is shorter than its diff:
```python
import functools

import jax
import jax.numpy as jnp
from jax import lax
from jax.experimental import pallas as pl
from jax.experimental.pallas import tpu as pltpu
from jax.sharding import PartitionSpec as P

HEAD = 32
GROUP = 256
SLOT = 64
BF = jnp.bfloat16
F32 = jnp.float32


def cols(j, width=GROUP):
    return pl.ds(pl.multiple_of(j * width, width), width)


def dot(a, b):
    return lax.dot_general(a, b, (((1,), (0,)), ((), ())), preferred_element_type=F32)


def dot_t(a, b):
    return lax.dot_general(a, b, (((1,), (1,)), ((), ())), preferred_element_type=F32)


def t_dot(a, b):
    return lax.dot_general(a, b, (((0,), (0,)), ((), ())), preferred_element_type=F32)


def fill_swap(ref, images):
    rows, columns = ref.shape
    block = 128

    @pl.loop(0, rows // block)
    def _(b):
        r = lax.broadcasted_iota(jnp.int32, (block, columns), 0) + b * block
        c = lax.broadcasted_iota(jnp.int32, (block, columns), 1)
        image, position = lax.div(r, SLOT), lax.rem(r, SLOT)
        hit = (c == position * images + image) & (position < 49)
        ref[pl.ds(pl.multiple_of(b * block, block), block), :] = jnp.where(hit, 1.0, 0.0).astype(BF)


def clear_border(pad, images):
    zero = jnp.zeros((9 * images, pad.shape[1]), pad.dtype)
    pad[0 : 9 * images, :] = zero
    pad[72 * images : 81 * images, :] = zero
    one = jnp.zeros((images, pad.shape[1]), pad.dtype)

    @pl.loop(1, 8)
    def _(r):
        pad[pl.ds(pl.multiple_of(r * 9 * images, 16), images), :] = one
        pad[pl.ds(pl.multiple_of((r * 9 + 8) * images, 16), images), :] = one


def inside(r, images):
    return pl.ds(pl.multiple_of(((r + 1) * 9 + 1) * images, 16), 7 * images)


def grid_row(r, images):
    return pl.ds(pl.multiple_of(r * 7 * images, 16), 7 * images)


def encode(pad, kernel, bias, out, images):
    @pl.loop(0, pad.shape[1] // 128)
    def _(lane):
        ls = cols(lane, 128)
        taps = [jnp.broadcast_to(kernel[pl.ds(t, 1), ls], (images, 128)) for t in range(9)]
        shift = jnp.broadcast_to(bias[:, ls], (images, 128))

        @pl.loop(0, 7)
        def _(r):
            for c in range(7):
                total = shift
                for t in range(9):
                    at = pl.multiple_of(((r + t // 3) * 9 + c + t % 3) * images, 16)
                    piece = pad[pl.ds(at, images), ls]
                    total = total + piece * taps[t]
                    if t == 4:
                        total = total + piece
                out[pl.ds(pl.multiple_of((r * 7 + c) * images, 16), images), ls] = total


def normalise(stream, gain, bias, out, images):
    @pl.loop(0, 49, unroll=7)
    def _(p):
        rows = pl.ds(pl.multiple_of(p * images, 16), images)
        s = stream[rows, :]
        centered = s - jnp.mean(s, axis=-1, keepdims=True)
        spread = jnp.mean(centered * centered, axis=-1, keepdims=True)
        out[rows, :] = (centered * lax.rsqrt(spread + 1e-5) * gain[...] + bias[...]).astype(BF)


def head_mask(rows_per, count, lanes):
    shape = (count * rows_per, lanes)
    r = lax.broadcasted_iota(jnp.int32, shape, 0)
    c = lax.broadcasted_iota(jnp.int32, shape, 1)
    return lax.div(r, rows_per) == lax.div(c, HEAD)


def spread_heads(x, mask):
    count = mask.shape[0] // x.shape[0]
    return jnp.where(mask, jnp.concatenate([x] * count, axis=0), jnp.zeros((), x.dtype))


def fold_heads(x, mask, rows_per):
    kept = jnp.where(mask, x, 0.0)
    total = kept[0:rows_per]
    for h in range(1, x.shape[0] // rows_per):
        total = total + kept[h * rows_per : (h + 1) * rows_per]
    return total


def soft_down(scores, valid):
    if valid < scores.shape[0]:
        r = lax.broadcasted_iota(jnp.int32, scores.shape, 0)
        scores = jnp.where(r < valid, scores, -jnp.inf)
    e = jnp.exp(scores - jnp.max(scores, axis=0, keepdims=True))
    return e / jnp.sum(e, axis=0, keepdims=True)


def spatial_forward(packed, mixed, soft, images):
    width = mixed.shape[1]
    groups = width // GROUP

    @pl.loop(0, images)
    def _(i):
        rows = pl.ds(pl.multiple_of(i * SLOT, SLOT), SLOT)
        mask = head_mask(SLOT, GROUP // HEAD, GROUP)
        for g in range(groups):
            q, k, v = (packed[rows, part * width + g * GROUP : part * width + (g + 1) * GROUP] for part in range(3))
            weights = soft_down(dot_t(k, spread_heads(q, mask)), 49).astype(BF)
            soft[i, g] = weights
            mixed[rows, g * GROUP : (g + 1) * GROUP] = fold_heads(t_dot(weights, v), mask, SLOT).astype(BF)


def channel_forward(packed, mixed, soft, images):
    width = mixed.shape[1]

    @pl.loop(0, images)
    def _(i):
        rows = pl.ds(pl.multiple_of(i * SLOT, SLOT), SLOT)
        mask = head_mask(HEAD, 128 // HEAD, 128)
        for g in range(width // 128):
            q, k, v = (packed[rows, part * width + g * 128 : part * width + (g + 1) * 128] for part in range(3))
            weights = soft_down(fold_heads(t_dot(k, q), mask, HEAD), HEAD).astype(BF)
            soft[i, g // 2, g % 2 * HEAD : (g % 2 + 1) * HEAD, 0:128] = weights
            mixed[rows, g * 128 : (g + 1) * 128] = dot(v, spread_heads(weights, mask)).astype(BF)


def gelu_both(x):
    half = 0.5 + 0.5 * lax.erf(x * 0.7071067811865476)
    return x * half, half + x * (0.3989422804014327 * jnp.exp(-0.5 * x * x))


def forward_kernel(images, role, x, conv_w, conv_b, gain, shift, b_proj, b_fc1, b_fc2,
                   w_qkv, w_proj, w_fc1, w_fc2, *refs):
    earlier = len(refs) - 32
    (result, o_one, o_mid, o_two, o_n1, o_packed, o_soft, o_mixed, o_n2, o_hidden, o_slope,
     v_qkv, v_proj, v_fc1, v_fc2, pad, one, mid, two, n1, swap, n1s, packed, soft, mixed_s, mixed,
     n2, hidden, slope, end, load, store) = refs[earlier:]
    rows = 49 * images
    width = x.shape[1]
    loads = [pltpu.make_async_copy(src, dst, load.at[at]) for at, (src, dst) in enumerate(
        ((w_qkv, v_qkv), (w_proj, v_proj), (w_fc1, v_fc1), (w_fc2, v_fc2)))]
    stores = [pltpu.make_async_copy(src, dst, store.at[at]) for at, (src, dst) in enumerate(
        ((one, o_one), (mid, o_mid), (two, o_two), (n1, o_n1), (packed, o_packed), (soft, o_soft),
         (mixed, o_mixed), (n2, o_n2), (hidden, o_hidden), (slope, o_slope), (end, result)))]

    @pl.when(role[1] == 1)
    def _():
        for copy in loads:
            copy.start()
        fill_swap(swap, images)
        clear_border(pad, images)

        @pl.loop(0, 7)
        def _(r):
            pad[inside(r, images), :] = x[grid_row(r, images), :].astype(F32)
        encode(pad, conv_w.at[0], conv_b.at[pl.ds(0, 1)], one, images)
        stores[0].start()
        normalise(one, gain.at[pl.ds(0, 1)], shift.at[pl.ds(0, 1)], n1, images)
        stores[3].start()

        @pl.loop(0, width // GROUP)
        def _(j):
            n1s[:, cols(j)] = dot(swap[...], n1[:, cols(j)]).astype(BF)
        loads[0].wait()

        @pl.loop(0, 3 * width // GROUP)
        def _(j):
            scale = jnp.where(j < width // GROUP, HEAD ** -0.5, 1.0)
            packed[:, cols(j)] = (dot(n1s[...], v_qkv[:, cols(j)]) * scale).astype(BF)
        stores[4].start()

        @pl.when(role[0] == 1)
        def _():
            spatial_forward(packed, mixed_s, soft, images)

        @pl.when(role[0] == 0)
        def _():
            channel_forward(packed, mixed_s, soft, images)
        stores[5].start()

        @pl.loop(0, width // GROUP)
        def _(j):
            mixed[:, cols(j)] = t_dot(swap[...], mixed_s[:, cols(j)]).astype(BF)
        stores[6].start()
        loads[1].wait()

        @pl.loop(0, width // GROUP)
        def _(j):
            mid[:, cols(j)] = one[:, cols(j)] + dot(mixed[...], v_proj[:, cols(j)]) + b_proj[:, cols(j)]
        stores[1].start()

        @pl.loop(0, 7)
        def _(r):
            pad[inside(r, images), :] = mid[grid_row(r, images), :]
        encode(pad, conv_w.at[1], conv_b.at[pl.ds(1, 1)], two, images)
        stores[2].start()
        normalise(two, gain.at[pl.ds(1, 1)], shift.at[pl.ds(1, 1)], n2, images)
        stores[7].start()
        loads[2].wait()

        @pl.loop(0, v_fc1.shape[1] // GROUP)
        def _(j):
            pre = dot(n2[...], v_fc1[:, cols(j)]) + b_fc1[:, cols(j)]
            value, rate = gelu_both(pre)
            hidden[:, cols(j)] = value.astype(BF)
            slope[:, cols(j)] = rate.astype(BF)
        stores[8].start()
        stores[9].start()
        loads[3].wait()

        @pl.loop(0, width // GROUP)
        def _(j):
            end[:, cols(j)] = two[:, cols(j)] + dot(hidden[...], v_fc2[:, cols(j)]) + b_fc2[:, cols(j)]
        stores[10].start()
        for copy in stores:
            copy.wait()


def forward_block(role, x, params, images, earlier=()):
    conv_w, conv_b, gain, shift, w_qkv, w_proj, b_proj, w_fc1, b_fc1, w_fc2, b_fc2 = params
    rows, width = x.shape
    wide = w_fc1.shape[1]
    slots = images * SLOT
    any_space = pl.BlockSpec(memory_space=pl.ANY)
    vmem = pl.BlockSpec(memory_space=pltpu.VMEM)
    outs = [((rows, width), F32), ((rows, width), F32), ((rows, width), F32), ((rows, width), F32),
            ((rows, width), BF), ((slots, 3 * width), BF), ((images, width // GROUP, SLOT, 2 * GROUP), BF),
            ((rows, width), BF), ((rows, width), BF), ((rows, wide), BF), ((rows, wide), BF)]
    scratch = [w_qkv, w_proj, w_fc1, w_fc2]
    return pl.pallas_call(
        functools.partial(forward_kernel, images),
        out_shape=[jax.ShapeDtypeStruct(*o) for o in outs],
        in_specs=[pl.BlockSpec(memory_space=pltpu.SMEM)] + [vmem] * 8 + [any_space] * (4 + len(earlier)),
        out_specs=[any_space] * len(outs),
        input_output_aliases={13 + at: at for at in range(len(earlier))},
        scratch_shapes=[pltpu.VMEM(w.shape, w.dtype) for w in scratch] + [
            pltpu.VMEM((81 * images, width), F32),
            pltpu.VMEM((rows, width), F32), pltpu.VMEM((rows, width), F32), pltpu.VMEM((rows, width), F32),
            pltpu.VMEM((rows, width), BF), pltpu.VMEM((slots, rows), BF), pltpu.VMEM((slots, width), BF),
            pltpu.VMEM((slots, 3 * width), BF), pltpu.VMEM((images, width // GROUP, SLOT, 2 * GROUP), BF),
            pltpu.VMEM((slots, width), BF), pltpu.VMEM((rows, width), BF), pltpu.VMEM((rows, width), BF),
            pltpu.VMEM((rows, wide), BF), pltpu.VMEM((rows, wide), BF), pltpu.VMEM((rows, width), F32),
            pltpu.SemaphoreType.DMA((4,)), pltpu.SemaphoreType.DMA((11,)),
        ],
        compiler_params=pltpu.CompilerParams(vmem_limit_bytes=62 * 2**20),
    )(role, x, conv_w, conv_b, gain, shift, b_proj, b_fc1, b_fc2, w_qkv, w_proj, w_fc1, w_fc2, *earlier)


def encode_back(gpad, ipad, kernel, out, sums, first_row, bias_row, images):
    @pl.loop(0, gpad.shape[1] // 128)
    def _(lane):
        ls = cols(lane, 128)
        taps = [jnp.broadcast_to(kernel[pl.ds(8 - t, 1), ls], (images, 128)) for t in range(9)]
        zero = jnp.zeros((images, 128), F32)

        def row(r, totals):
            totals = list(totals)
            for c in range(7):
                centre = gpad[pl.ds(pl.multiple_of(((r + 1) * 9 + c + 1) * images, 16), images), ls]
                total = centre
                totals[9] = totals[9] + centre
                for t in range(9):
                    at = pl.ds(pl.multiple_of(((r + t // 3) * 9 + c + t % 3) * images, 16), images)
                    total = total + gpad[at, ls] * taps[t]
                    totals[t] = totals[t] + ipad[at, ls] * centre
                out[pl.ds(pl.multiple_of((r * 7 + c) * images, 16), images), ls] = total
            return tuple(totals)
        totals = lax.fori_loop(0, 7, row, (zero,) * 10)
        for t in range(9):
            sums[pl.ds(first_row + t, 1), ls] = jnp.sum(totals[t], axis=0, keepdims=True)
        sums[pl.ds(bias_row, 1), ls] = jnp.sum(totals[9], axis=0, keepdims=True)


def normalise_back(stream, grad, base, gain, out_rows, sums, gain_row, shift_row, acc, images):
    acc[...] = jnp.zeros_like(acc)

    @pl.loop(0, 49, unroll=7)
    def _(p):
        rows = pl.ds(pl.multiple_of(p * images, 16), images)
        s, dy = stream[rows, :], grad[rows, :]
        centered = s - jnp.mean(s, axis=-1, keepdims=True)
        rate = lax.rsqrt(jnp.mean(centered * centered, axis=-1, keepdims=True) + 1e-5)
        unit = centered * rate
        acc[0] += dy * unit
        acc[1] += dy
        dg = dy * gain[...]
        m1 = jnp.mean(dg, axis=-1, keepdims=True)
        m2 = jnp.mean(dg * unit, axis=-1, keepdims=True)
        ref, at = out_rows(p)
        ref[at, :] = base[rows, :].astype(F32) + rate * (dg - m1 - unit * m2)
    sums[pl.ds(gain_row, 1), :] = jnp.sum(acc[0], axis=0, keepdims=True)
    sums[pl.ds(shift_row, 1), :] = jnp.sum(acc[1], axis=0, keepdims=True)


def spatial_backward(packed, grad_mixed, soft, images):
    width = grad_mixed.shape[1]

    @pl.loop(0, images)
    def _(i):
        rows = pl.ds(pl.multiple_of(i * SLOT, SLOT), SLOT)
        mask = head_mask(SLOT, GROUP // HEAD, GROUP)
        for g in range(width // GROUP):
            at = [slice(part * width + g * GROUP, part * width + (g + 1) * GROUP) for part in range(3)]
            q, k, v = (packed[rows, a] for a in at)
            weights = soft[i, g]
            out_spread = spread_heads(grad_mixed[rows, g * GROUP : (g + 1) * GROUP], mask)
            w = weights.astype(F32)
            dw = dot_t(v, out_spread)
            ds = (w * (dw - jnp.sum(dw * w, axis=0, keepdims=True))).astype(BF)
            packed[rows, at[2]] = dot(weights, out_spread).astype(BF)
            packed[rows, at[1]] = dot(ds, spread_heads(q, mask)).astype(BF)
            packed[rows, at[0]] = (fold_heads(t_dot(ds, k), mask, SLOT) * HEAD ** -0.5).astype(BF)


def channel_backward(packed, grad_mixed, soft, images):
    width = grad_mixed.shape[1]

    @pl.loop(0, images)
    def _(i):
        rows = pl.ds(pl.multiple_of(i * SLOT, SLOT), SLOT)
        mask = head_mask(HEAD, 128 // HEAD, 128)
        for g in range(width // 128):
            at = [slice(part * width + g * 128, part * width + (g + 1) * 128) for part in range(3)]
            q, k, v = (packed[rows, a] for a in at)
            weights = soft[i, g // 2, g % 2 * HEAD : (g % 2 + 1) * HEAD, 0:128]
            do = grad_mixed[rows, g * 128 : (g + 1) * 128]
            w = weights.astype(F32)
            dw = fold_heads(t_dot(v, do), mask, HEAD)
            ds = spread_heads((w * (dw - jnp.sum(dw * w, axis=0, keepdims=True))).astype(BF), mask)
            packed[rows, at[2]] = dot_t(do, spread_heads(weights, mask)).astype(BF)
            packed[rows, at[1]] = dot_t(q, ds).astype(BF)
            packed[rows, at[0]] = (dot(k, ds) * HEAD ** -0.5).astype(BF)


def backward_kernel(images, role, cot, x, conv_w, gain, w_qkv, w_proj, w_fc1, w_fc2,
                    one, mid, two, h_packed, h_soft, h_slope, *refs):
    earlier = len(refs) - 26
    (o_grad, o_packed, o_att, o_pre, o_sums,
     v_qkv, v_proj, v_fc1, v_fc2, gpad, ipad, stream_two, stream_one, packed, soft, slope,
     swap, gm_s, gp, gn, gmid, gatt, acc, sums, load, store) = refs[earlier:]
    rows = 49 * images
    width = x.shape[1]
    loads = [pltpu.make_async_copy(src, dst, load.at[at]) for at, (src, dst) in enumerate(
        ((w_fc2, v_fc2), (h_slope, slope), (w_fc1, v_fc1), (two, stream_two), (mid, gmid), (w_proj, v_proj),
         (h_soft, soft), (h_packed, packed), (w_qkv, v_qkv), (one, stream_one)))]
    stores = [pltpu.make_async_copy(src, dst, store.at[at]) for at, (src, dst) in enumerate(
        ((slope, o_pre), (gatt, o_att), (gp, o_packed), (gmid, o_grad), (sums, o_sums)))]

    @pl.when(role[1] == 1)
    def _():
        for copy in loads:
            copy.start()
        fill_swap(swap, images)
        clear_border(gpad, images)
        clear_border(ipad, images)
        sums[...] = jnp.zeros_like(sums)
        loads[0].wait()
        loads[1].wait()

        @pl.loop(0, v_fc2.shape[0] // GROUP)
        def _(j):
            pre = dot_t(cot[...], v_fc2[cols(j), :]) * slope[:, cols(j)].astype(F32)
            slope[:, cols(j)] = pre.astype(BF)
            sums[pl.ds(25 + lax.div(j, 3), 1), cols(lax.rem(j, 3))] = jnp.sum(pre, axis=0, keepdims=True)
        stores[0].start()

        @pl.loop(0, width // GROUP)
        def _(j):
            sums[pl.ds(29, 1), cols(j)] = jnp.sum(cot[:, cols(j)].astype(F32), axis=0, keepdims=True)
        loads[2].wait()

        @pl.loop(0, width // GROUP)
        def _(j):
            gn[:, cols(j)] = dot_t(slope[...], v_fc1[cols(j), :])
        loads[3].wait()
        loads[4].wait()

        def in_pad(p):
            at = ((lax.div(p, 7) + 1) * 9 + lax.rem(p, 7) + 1) * images
            return gpad, pl.ds(pl.multiple_of(at, 16), images)
        normalise_back(stream_two, gn, cot, gain.at[pl.ds(1, 1)], in_pad, sums, 21, 23, acc, images)

        @pl.loop(0, 7)
        def _(r):
            ipad[inside(r, images), :] = gmid[grid_row(r, images), :]
        encode_back(gpad, ipad, conv_w.at[1], gmid, sums, 9, 19, images)

        @pl.loop(0, width // GROUP)
        def _(j):
            sums[pl.ds(24, 1), cols(j)] = jnp.sum(gmid[:, cols(j)], axis=0, keepdims=True)
            gatt[:, cols(j)] = gmid[:, cols(j)].astype(BF)
        stores[1].start()
        loads[5].wait()

        @pl.loop(0, width // GROUP)
        def _(j):
            gp[:, cols(j)] = dot_t(gatt[...], v_proj[cols(j), :]).astype(BF)

        @pl.loop(0, width // GROUP)
        def _(j):
            gm_s[:, cols(j)] = dot(swap[...], gp[:, cols(j)]).astype(BF)
        loads[6].wait()
        loads[7].wait()

        @pl.when(role[0] == 1)
        def _():
            spatial_backward(packed, gm_s, soft, images)

        @pl.when(role[0] == 0)
        def _():
            channel_backward(packed, gm_s, soft, images)

        @pl.loop(0, 3 * width // GROUP)
        def _(j):
            gp[:, cols(j)] = t_dot(swap[...], packed[:, cols(j)]).astype(BF)
        stores[2].start()
        loads[8].wait()

        @pl.loop(0, width // GROUP)
        def _(j):
            gn[:, cols(j)] = dot_t(gp[...], v_qkv[cols(j), :])
        loads[9].wait()
        normalise_back(stream_one, gn, gmid, gain.at[pl.ds(0, 1)], in_pad, sums, 20, 22, acc, images)

        @pl.loop(0, 7)
        def _(r):
            ipad[inside(r, images), :] = x[grid_row(r, images), :].astype(F32)
        encode_back(gpad, ipad, conv_w.at[0], gmid, sums, 0, 18, images)
        stores[3].start()
        stores[4].start()
        for copy in stores:
            copy.wait()


def backward_block(role, cot, x, saved, params, images, earlier=()):
    conv_w, conv_b, gain, shift, w_qkv, w_proj, b_proj, w_fc1, b_fc1, w_fc2, b_fc2 = params
    one, mid, two, packed, soft, slope = saved
    rows, width = x.shape
    wide = w_fc1.shape[1]
    slots = images * SLOT
    any_space = pl.BlockSpec(memory_space=pl.ANY)
    vmem = pl.BlockSpec(memory_space=pltpu.VMEM)
    outs = [((rows, width), F32), ((rows, 3 * width), BF), ((rows, width), BF), ((rows, wide), BF), ((32, width), F32)]
    return pl.pallas_call(
        functools.partial(backward_kernel, images),
        out_shape=[jax.ShapeDtypeStruct(*o) for o in outs],
        in_specs=[pl.BlockSpec(memory_space=pltpu.SMEM)] + [vmem] * 4 + [any_space] * (10 + len(earlier)),
        out_specs=[any_space] * len(outs),
        input_output_aliases={15 + at: at for at in range(len(earlier))},
        scratch_shapes=[pltpu.VMEM(w.shape, w.dtype) for w in (w_qkv, w_proj, w_fc1, w_fc2)] + [
            pltpu.VMEM((81 * images, width), F32), pltpu.VMEM((81 * images, width), F32),
            pltpu.VMEM((rows, width), F32), pltpu.VMEM((rows, width), F32),
            pltpu.VMEM(packed.shape, BF), pltpu.VMEM(soft.shape, BF), pltpu.VMEM((rows, wide), BF),
            pltpu.VMEM((slots, rows), BF), pltpu.VMEM((slots, width), BF), pltpu.VMEM((rows, 3 * width), BF),
            pltpu.VMEM((rows, width), F32), pltpu.VMEM((rows, width), F32), pltpu.VMEM((rows, width), BF),
            pltpu.VMEM((2, images, width), F32), pltpu.VMEM((32, width), F32),
            pltpu.SemaphoreType.DMA((10,)), pltpu.SemaphoreType.DMA((5,)),
        ],
        compiler_params=pltpu.CompilerParams(vmem_limit_bytes=63 * 2**20),
    )(role, cot, x, conv_w, gain, w_qkv, w_proj, w_fc1, w_fc2, one, mid, two, packed, soft, slope, *earlier)


MESH = pl.DeviceIdType.MESH


def dp_dims(n):
    sizes = [1, 1, 1]
    at = 0
    left = n
    while left > 1:
        factor = 2 if left % 2 == 0 else left
        sizes[at % 3] *= factor
        left //= factor
        at += 1
    return tuple(sizes), (sizes[1] * sizes[2], sizes[2], 1)


class Place:
    def __init__(self, dp, size, stride):
        self.size = size
        pos = lax.rem(lax.div(dp, stride), size)
        low = pos < (size + 1) // 2
        self.outer = jnp.where(low, pos, size - 1 - pos)
        self.pos = pos
        self.low = low
        step = jnp.where(low, stride, -stride)
        self.inner_peer = dp + step
        self.outer_peer = dp - step


def pick(flag, a, b):
    out = object.__new__(Place)
    out.size = a.size
    for name in ("pos", "low", "outer", "inner_peer", "outer_peer"):
        setattr(out, name, jnp.where(flag, getattr(a, name), getattr(b, name)))
    return out


class Ring:
    def __init__(self, dp, dims, rows, grad, land, out, send, recv, local):
        (s0, s1, s2), (t0, t1, t2) = dims
        self.mids = Place(dp, s0, t0)
        self.fast, self.slow = Place(dp, s2, t2), Place(dp, s1, t1)
        self.dp, self.rows = dp, rows
        self.grad, self.land, self.out = grad, land, out
        self.send, self.recv, self.local = send, recv, local
        self.sizes = (s2, s0, s1)
        self.lens = (rows // s2, rows // s2 // s0, rows // (s0 * s1 * s2))

    @staticmethod
    def land_rows(rows, dims):
        s0, s1, s2 = dims[0]
        lens = (rows // s2, rows // s2 // s0, rows // (s0 * s1 * s2))
        total, starts = 0, []
        for n, length in zip((s2, s0, s1), lens):
            starts.append(total)
            total += length * (1 if n == 2 else 5)
        return total, starts

    def level(self, c, i):
        flag = lax.rem(c, 2) == 0
        if i == 1:
            return self.mids
        return pick(flag, self.fast, self.slow) if i == 0 else pick(flag, self.slow, self.fast)

    def base(self, c, i):
        start = 0
        for j in range(i):
            start = start + self.level(c, j).pos * self.lens[j]
        return start

    def span(self, c, i, a, b):
        place, length = self.level(c, i), self.lens[i]
        n = self.sizes[i]
        start = self.base(c, i) + jnp.where(place.low, a * length, (n - b) * length)
        return pl.ds(pl.multiple_of(start, 8), (b - a) * length)

    def copy(self, c, ev, src, dst, peer):
        return pltpu.make_async_remote_copy(
            src_ref=src, dst_ref=dst, send_sem=self.send.at[c, ev], recv_sem=self.recv.at[c, ev],
            device_id={"dp": peer}, device_id_type=MESH)

    def landing(self, c, i, at, length):
        start = self.land_rows(self.rows, ((self.sizes[1], self.sizes[2], self.sizes[0]), None))[1][i]
        return self.land.at[c, pl.ds(start + at, length)]

    def add(self, c, i, a, b, at, lo=None):
        rows = self.span(c, i, a, b)
        length = (b - a) * self.lens[i]
        got = self.landing(c, i, at, length)
        self.grad[c, rows] = self.grad[c, rows] + got[...]

    def reduce_send(self, c, i, ev, a, b, at, peer):
        rows = self.span(c, i, a, b)
        length = (b - a) * self.lens[i]
        return self.copy(c, ev, self.grad.at[c, rows], self.landing(c, i, at, length), peer)

    def reduce_stages(self, i):
        n, length = self.sizes[i], self.lens[i]
        ein, eout = 2 * i, 2 * i + 1
        if n == 1:
            return []
        if n == 2:
            def first(c):
                self.reduce_send(c, i, eout, 1, 2, 0, self.level(c, i).inner_peer).start()

            def last(c):
                self.reduce_send(c, i, eout, 0, 1, 0, self.level(c, i).inner_peer).wait_recv()
                self.add(c, i, 0, 1, 0)
            return [first, last]

        def zero(c):
            place = self.level(c, i)

            @pl.when(place.outer == 0)
            def _():
                self.reduce_send(c, i, ein, 1, 4, 0, place.inner_peer).start()

        def one(c):
            place = self.level(c, i)

            @pl.when(place.outer == 1)
            def _():
                self.reduce_send(c, i, ein, 1, 4, 0, place.inner_peer).wait_recv()
                self.add(c, i, 1, 4, 0)
                self.reduce_send(c, i, eout, 2, 4, 3 * length, place.inner_peer).start()

        def two(c):
            place = self.level(c, i)

            @pl.when(place.outer == 1)
            def _():
                self.reduce_send(c, i, eout, 0, 2, 3 * length, place.inner_peer).wait_recv()
                self.add(c, i, 0, 2, 3 * length)
                self.reduce_send(c, i, ein, 0, 1, 3 * length, place.outer_peer).start()

        def three(c):
            place = self.level(c, i)

            @pl.when(place.outer == 0)
            def _():
                self.reduce_send(c, i, ein, 0, 1, 3 * length, place.inner_peer).wait_recv()
                self.add(c, i, 0, 1, 3 * length)
        return [zero, one, two, three]

    def reduce_ends(self, i):
        n = self.sizes[i]
        ein, eout = 2 * i, 2 * i + 1

        def ends(c):
            place = self.level(c, i)
            if n == 2:
                self.reduce_send(c, i, eout, 1, 2, 0, place.inner_peer).wait_send()
            elif n == 4:
                @pl.when(place.outer == 0)
                def _():
                    self.reduce_send(c, i, ein, 1, 4, 0, place.inner_peer).wait_send()

                @pl.when(place.outer == 1)
                def _():
                    self.reduce_send(c, i, eout, 2, 4, 0, place.inner_peer).wait_send()
                    self.reduce_send(c, i, ein, 0, 1, 0, place.outer_peer).wait_send()
        return ends

    def gather_send(self, c, i, ev, a, b, peer):
        rows = self.span(c, i, a, b)
        dst = self.out.at[c, rows]
        return self.copy(c, ev, dst, dst, peer)

    def gather_stages(self, i):
        n = self.sizes[i]
        ein, eout = 6 + 2 * i, 7 + 2 * i
        if n == 1:
            return []
        if n == 2:
            def first(c):
                self.gather_send(c, i, eout, 0, 1, self.level(c, i).inner_peer).start()

            def last(c):
                self.gather_send(c, i, eout, 1, 2, self.level(c, i).inner_peer).wait_recv()
            return [first, last]

        def zero(c):
            place = self.level(c, i)

            @pl.when(place.outer == 0)
            def _():
                self.gather_send(c, i, ein, 0, 1, place.inner_peer).start()

        def one(c):
            place = self.level(c, i)

            @pl.when(place.outer == 1)
            def _():
                self.gather_send(c, i, ein, 0, 1, place.outer_peer).wait_recv()
                self.gather_send(c, i, eout, 0, 2, place.inner_peer).start()

        def two(c):
            place = self.level(c, i)

            @pl.when(place.outer == 1)
            def _():
                self.gather_send(c, i, eout, 2, 4, place.inner_peer).wait_recv()
                self.gather_send(c, i, ein, 1, 4, place.outer_peer).start()

        def three(c):
            place = self.level(c, i)

            @pl.when(place.outer == 0)
            def _():
                self.gather_send(c, i, ein, 1, 4, place.inner_peer).wait_recv()
        return [zero, one, two, three]

    def gather_ends(self, i):
        n = self.sizes[i]
        ein, eout = 6 + 2 * i, 7 + 2 * i

        def ends(c):
            place = self.level(c, i)
            if n == 2:
                self.gather_send(c, i, eout, 0, 1, place.inner_peer).wait_send()
            elif n == 4:
                @pl.when(place.outer == 0)
                def _():
                    self.gather_send(c, i, ein, 0, 1, place.inner_peer).wait_send()

                @pl.when(place.outer == 1)
                def _():
                    self.gather_send(c, i, eout, 0, 2, place.inner_peer).wait_send()
                    self.gather_send(c, i, ein, 1, 4, place.outer_peer).wait_send()
        return ends

    def own_copy(self, c):
        start = self.base(c, 3)
        rows = pl.ds(pl.multiple_of(start, 8), self.lens[2])
        return pltpu.make_async_copy(self.grad.at[c, rows], self.out.at[c, rows], self.local.at[c])

    def stages(self):
        groups = [self.reduce_stages(0), self.reduce_stages(1), self.reduce_stages(2)]

        def settle(c):
            self.own_copy(c).start()
            self.own_copy(c).wait()
        groups += [[settle], self.gather_stages(2), self.gather_stages(1), self.gather_stages(0)]
        joined = []
        for group in groups:
            if not group:
                continue
            if joined:
                joined[-1] = joined[-1] + [group[0]]
                joined += [[stage] for stage in group[1:]]
            else:
                joined = [[stage] for stage in group]
        return [functools.partial(run_all, stages) for stages in joined]

    def ends(self, c):
        for i in range(3):
            if self.sizes[i] > 1:
                self.reduce_ends(i)(c)
                self.gather_ends(i)(c)

    def greet(self):
        barrier = pltpu.get_barrier_semaphore()
        count = jnp.int32(0)
        for place in (self.fast, self.mids, self.slow):
            if place.size == 1:
                continue
            pl.semaphore_signal(barrier, inc=1, device_id={"dp": place.inner_peer}, device_id_type=MESH)
            count = count + 1
            if place.size == 4:
                @pl.when(place.outer == 1)
                def _():
                    pl.semaphore_signal(barrier, inc=1, device_id={"dp": place.outer_peer}, device_id_type=MESH)
                count = count + jnp.where(place.outer == 1, 1, 0)
        pl.semaphore_wait(barrier, count)


def run_all(stages, c):
    for stage in stages:
        stage(c)


CHUNK = 384
SIDE = 768


class Makers:
    def __init__(self, lefts, rights):
        self.parts = []
        start = 0
        for left, right in zip(lefts, rights):
            across = right.shape[1] // CHUNK
            number = left.shape[1] // SIDE * across
            self.parts.append((start, number, across, left, right))
            start += number
        self.count = start

    def fetch(self, c, left_buf, right_buf, sems):
        slot = lax.rem(c, 2)
        for start, number, across, left, right in self.parts:
            @pl.when((c >= start) & (c < start + number))
            def _():
                at = c - start
                pltpu.make_async_copy(left.at[:, cols(lax.div(at, across), SIDE)], left_buf.at[slot], sems.at[slot, 0]).start()
                pltpu.make_async_copy(right.at[:, cols(lax.rem(at, across), CHUNK)], right_buf.at[slot], sems.at[slot, 1]).start()

    def wait(self, c, left_buf, right_buf, sems):
        slot = lax.rem(c, 2)
        _, _, _, left, right = self.parts[0]
        pltpu.make_async_copy(left.at[:, cols(0, SIDE)], left_buf.at[slot], sems.at[slot, 0]).wait()
        pltpu.make_async_copy(right.at[:, cols(0, CHUNK)], right_buf.at[slot], sems.at[slot, 1]).wait()


def sum_kernel(dims, rows, lead, h_left, h_right, n_left, n_right, m_left, m_right, q_left, q_right, small_src,
               out, small_out, grad, land, small_grad, small_land, left_buf, right_buf, load, send, recv, local, ssend, srecv, slocal):
    dp = lax.axis_index("dp")
    makers = Makers((h_left, n_left, m_left, q_left), (h_right, n_right, m_right, q_right))
    count = makers.count
    main = Ring(dp, dims, rows, grad, land, out, send, recv, local)
    small = Ring(dp, dims, small_grad.shape[1], small_grad, small_land, small_out, ssend, srecv, slocal)
    makers.fetch(0, left_buf, right_buf, load)
    pltpu.make_async_copy(small_src, small_grad, load.at[2, 0]).start()
    main.greet()
    stages, small_stages = main.stages(), small.stages()
    depth = len(stages)

    def make(c):
        makers.wait(c, left_buf, right_buf, load)
        makers.fetch(c + 1, left_buf, right_buf, load)
        slot = lax.rem(c, 2)
        for j in range(SIDE // GROUP):
            grad[c, j * GROUP : (j + 1) * GROUP] = t_dot(left_buf[slot, :, j * GROUP : (j + 1) * GROUP], right_buf[slot]).astype(BF)
        if rows > SIDE:
            grad[c, SIDE:rows] = jnp.zeros((rows - SIDE, CHUNK), BF)

    @pl.loop(0, count + 1 + lead + depth)
    def _(t):
        for s in reversed(range(depth)):
            c = t - s - (lead if s else 0)

            @pl.when((c >= 0) & (c < count))
            def _():
                if s == 0:
                    make(c)
                stages[s](c)

            @pl.when(c == count)
            def _():
                if s == 0:
                    pltpu.make_async_copy(small_src, small_grad, load.at[2, 0]).wait()
                small_stages[s](0)

    @pl.loop(0, count)
    def _(c):
        main.ends(c)
    small.ends(0)


def sum_grads(pairs, small, n, lead=2, collective_id=0):
    dims = dp_dims(n)
    rows = -(-SIDE // (16 * n)) * 16 * n
    count = sum(left.shape[1] // SIDE * right.shape[1] // CHUNK for left, right in pairs)
    tokens = pairs[0][0].shape[0]
    land, _ = Ring.land_rows(rows, dims)
    small_land, _ = Ring.land_rows(small.shape[1], dims)
    any_space = pl.BlockSpec(memory_space=pl.ANY)
    return pl.pallas_call(
        functools.partial(sum_kernel, dims, rows, lead),
        out_shape=(jax.ShapeDtypeStruct((count, rows, CHUNK), BF), jax.ShapeDtypeStruct(small.shape, small.dtype)),
        in_specs=[any_space] * 9,
        out_specs=(any_space,) * 2,
        scratch_shapes=[
            pltpu.VMEM((count, rows, CHUNK), BF),
            pltpu.VMEM((count, land, CHUNK), BF),
            pltpu.VMEM(small.shape, small.dtype),
            pltpu.VMEM((1, small_land, small.shape[2]), small.dtype),
            pltpu.VMEM((2, tokens, SIDE), BF),
            pltpu.VMEM((2, tokens, CHUNK), BF),
            pltpu.SemaphoreType.DMA((3, 2)),
            pltpu.SemaphoreType.DMA((count, 12)),
            pltpu.SemaphoreType.DMA((count, 12)),
            pltpu.SemaphoreType.DMA((count,)),
            pltpu.SemaphoreType.DMA((1, 12)),
            pltpu.SemaphoreType.DMA((1, 12)),
            pltpu.SemaphoreType.DMA((1,)),
        ],
        compiler_params=pltpu.CompilerParams(collective_id=collective_id, has_side_effects=True, vmem_limit_bytes=63 * 2**20),
    )(*[x for pair in pairs for x in pair], small)


def shifted(x, axis, by):
    count = lax.axis_size(axis)
    pairs = [(i, i + by) for i in range(count) if 0 <= i + by < count]
    return lax.ppermute(x, axis, pairs)


def widen(src, dst):
    dst[...] = src[0].astype(F32)


def from_chunks(done, start, shape):
    rows, columns = shape
    across = columns // CHUNK
    return pl.pallas_call(
        widen,
        grid=(rows // SIDE, across),
        in_specs=[pl.BlockSpec((1, SIDE, CHUNK), lambda r, j: (start + r * across + j, 0, 0))],
        out_specs=pl.BlockSpec((SIDE, CHUNK), lambda r, j: (r, j)),
        out_shape=jax.ShapeDtypeStruct(shape, F32),
    )(done)


def on_device(section_inputs, conv_weight, conv_bias, norm_gain, norm_bias, w_qkv, w_proj, b_proj, w_fc1, b_fc1, w_fc2, b_fc2):
    pipe, n = lax.axis_index("pipe"), lax.axis_size("dp")
    is_first = pipe == 0
    weights = (conv_weight, conv_bias, norm_gain, norm_bias, w_qkv, w_proj, b_proj, w_fc1, b_fc1, w_fc2, b_fc2)
    conv_w, conv_b, gain, shift, wq, wp, bp, w1, b1, w2, b2 = (weight[0] for weight in weights)
    params = (conv_w, conv_b, gain, shift, wq, wp, bp[None], w1, b1[None], w2, b2[None])
    images, _, width = section_inputs.shape[1:]

    def role(first):
        return jnp.stack([is_first.astype(jnp.int32), (is_first == first).astype(jnp.int32)])

    own = jnp.swapaxes(section_inputs[0], 0, 1).reshape(-1, width)
    first_out = forward_block(role(True), own, params, images)
    middle = shifted(first_out[0].astype(BF), "pipe", 1)
    second_out = forward_block(role(False), middle, params, images, first_out)
    x = jnp.where(is_first, own, middle)
    result, one, mid, two, n1, packed, soft, mixed, n2, hidden, slope = second_out
    saved = (one, mid, two, packed, soft, slope)
    back_second = backward_block(role(False), own, middle, saved, params, images)
    received = shifted(back_second[0].astype(BF), "pipe", -1)
    back_first = backward_block(role(True), received, own, saved, params, images, back_second)
    grad_in, grad_packed, grad_att, grad_pre, sums = back_first
    cot = jnp.where(is_first, received, own)
    ends = jnp.where(is_first, grad_in, result).reshape(49, images, width)
    section_ends = jnp.swapaxes(ends, 0, 1)[None]

    lanes = 128
    small = sums[:30].reshape(-1, lanes)
    small = jnp.pad(small, ((0, 16 * n - small.shape[0]), (0, 0)))[None]
    pairs = ((hidden, cot), (n2, grad_pre), (mixed, grad_att), (n1, grad_packed))
    done, small_done = sum_grads(pairs, small, n)
    grads, at = [], 0
    for shape in (w2.shape, w1.shape, wp.shape, wq.shape):
        number = shape[0] // SIDE * shape[1] // CHUNK
        grads.append(from_chunks(done, at, shape)[None])
        at += number
    grad_fc2, grad_fc1, grad_proj, grad_qkv = grads
    sums = small_done.reshape(-1)[: 30 * width].reshape(30, width)
    return (section_ends, sums[:18].reshape(conv_weight.shape), sums[18:20][None], sums[20:22][None], sums[22:24][None],
            grad_qkv, grad_proj, sums[24:25], grad_fc1, sums[25:29].reshape(b_fc1.shape), grad_fc2, sums[29:30])


def solution(mesh):
    return jax.shard_map(
        on_device,
        mesh=mesh,
        in_specs=(
            P("pipe", "dp", None, None),
            P("pipe", None, None, None),
            P("pipe", None, None),
            P("pipe", None, None),
            P("pipe", None, None),
            P("pipe", None, None),
            P("pipe", None, None),
            P("pipe", None),
            P("pipe", None, None),
            P("pipe", None),
            P("pipe", None, None),
            P("pipe", None),
        ),
        out_specs=(
            P("pipe", "dp", None, None),
            P("pipe", None, None, None),
            P("pipe", None, None),
            P("pipe", None, None),
            P("pipe", None, None),
            P("pipe", None, None),
            P("pipe", None, None),
            P("pipe", None),
            P("pipe", None, None),
            P("pipe", None),
            P("pipe", None, None),
            P("pipe", None),
        ),
        check_vma=False,
    )
```

time: 1230 us -> 507 us (0.41)
  matrix products: 391 us -> 0 us
  local copies, waits for them, and re-layouts: 397 us -> 10.8 us
  other arithmetic: 174 us -> 9.28 us
  Pallas kernels: 232 us -> 373 us
  waiting for transfers between devices: 2.92 us -> 109 us
    dot_general x95 -> x0, matrix products: 391 us -> none  [the longest x30 148 us: matmul_back(): jnp.einsum('...ij,...ik->...jk', left.astype(jnp.bfloat16), grad_low, pre...]
    convert_element_type x57 -> x0, local copies, waits for them, and re-layouts: 193 us -> none  [the longest x30 101 us: matmul_back(): grad_low = grad.astype(jnp.bfloat16)]
    pallas_call x1 -> x9, Pallas kernels: 232 us -> 373 us  [the longest x1 232 us: sum_grads(): pl.pallas_call(functools.partial(sum_kernel, dims, rows, lead), out_shape...]
    ppermute x8 -> x2, waiting for transfers between devices: 2.92 us -> 109 us  [shifted(): return lax.ppermute(x, axis, pairs)]
    unnamed x695 -> x7, local copies, waits for them, and re-layouts: 67.8 us -> 3.97 us
    reduce_sum x46 -> x0, other arithmetic: 55.3 us -> none  [the longest x10 27 us: depthwise(): padded[:, row_at:row_at + 7, col_at:col_at + 7, :] * kernel[offset]]
    reshape x23 -> x2, local copies, waits for them, and re-layouts: 46.1 us -> 0.91 us  [the longest x1 0.9 us: on_device(): small = sums[:30].reshape(-1, lanes)]
    convert_element_type x38 -> x2, other arithmetic: 41.2 us -> 3.6 us  [the longest x1 1.8 us: on_device(): middle = shifted(first_out[0].astype(BF), 'pipe', 1)]
  transfers between devices with their start and end apart: 8 -> 2, of which waited for: 3 -> 2; matrix products, arithmetic and copies ran while one was open for 4% -> 0% of each run, Pallas kernels for 0% -> 0%
where the time goes in v2:
time: 507 us; the launch traced here: 505 us
  Pallas kernels  373 us (74%)
  waiting for transfers between devices  109 us (21%)
  local copies, waits for them, and re-layouts  10.8 us (2%)
  other arithmetic  9.28 us (2%)
    pallas_call x1, Pallas kernels, sum_grads(): pl.pallas_call(functools.partial(sum_kernel, dims, rows, lead), out_shape...  232 us
    ppermute x2, waiting for transfers between devices, shifted(): return lax.ppermute(x, axis, pairs)  109 us
    pallas_call x2, Pallas kernels, backward_block(): pl.pallas_call(functools.partial(backward_kernel, images), out_shape=[jax...  63.2 us
    pallas_call x2, Pallas kernels, forward_block(): pl.pallas_call(functools.partial(forward_kernel, images), out_shape=[jax....  53.6 us
    pallas_call x4, Pallas kernels, from_chunks(): pl.pallas_call(widen, grid=(rows // SIDE, across), in_specs=[pl.BlockSpec...  23.9 us
  transfers between devices with their start and end apart: 2, of which 2 were waited for; matrix products, arithmetic and copies ran while one was open for 0% of the time, Pallas kernels for 0%

profile of v2, /device:TPU:0, one launch (start us, length us, event | category | flops | bytes accessed | tf_op | source)
XLA Modules:
  0.0 505.4 jit_solution(6262277233677955445)
XLA Ops:
  0.6 0.6 pad_add_fusion.role
  1.2 1.5 copy.49
  2.7 52.1 %shard_map.211 = (f32[784,768]{1,0:T(8,128)}, f32[784,768]{1,0:T(8,128)}, f32[784,768]{1,0:T(8,128)}, f32[784,768]{1,0:T(8,128)}, bf16[784,768]{1,0:T(8,128)(2,1...) custom-call(s32[2]{0:T(128)} %pad_add_fusion.role, ...), custom_call_target="tpu_custom_call" | custom-call | tf_op jit(solution)/shard_map/pallas_call | solution.py:256
  54.8 1.8 convert_element_type.5
  56.6 1.4 collective-permute-start
  58.0 0.6 pad_add_fusion.1.role
  58.6 1.8 collective-permute-done.x
  60.4 1.1 copy-done.1
  61.5 1.5 shard_map.212
  63.1 2.0 shard_map.213
  65.1 1.8 convert_element_type.6
  66.9 1.3 collective-permute-start.1
  68.2 107.0 %collective-permute-done.1.cot = bf16[784,768]{1,0:T(8,128)(2,1)} collective-permute-done((bf16[784,768]{1,0:T(8,128)(2,1)S(1)}, bf16[784,768]{1,0:T(8,128)(2,1)}, u32[]{:S(2)}, u32[]{:S(2)}) %collective-permute-start.1) | collective-permute-done | bytes 1204256 | tf_op jit(solution)/shard_map/ppermute | solution.py:880
  175.2 61.2 %shard_map.214 = (f32[784,768]{1,0:T(8,128)}, bf16[784,2304]{1,0:T(8,128)(2,1)}, bf16[784,768]{1,0:T(8,128)(2,1)}, bf16[784,3072]{1,0:T(8,128)(2,1)}, f32[32,768]{1,0:T(8,128)}) custom-call(s32[2]{0:T(128)} %pad_add_fusion.role, ...), custom_call_target="tpu_custom_call", output_to_operand_aliasing={{0}: (15, {}), {1}: (16, {}), {2}: (17, {}), {3}: (18, {}),... | custom-call | tf_op jit(solution)/shard_map/pallas_call | solution.py:470
  236.4 0.9 reshape.57
  237.3 0.6 pad_bitcast_fusion.small_src
  238.0 2.8 broadcast_select_fusion.h_right
  240.8 232.2 %shard_map.215 = (bf16[24,768,384]{2,1,0:T(8,128)(2,1)}, f32[1,256,128]{2,1,0:T(8,128)}) custom-call(bf16[784,3072]{1,0:T(8,128)(2,1)} %get-tuple-element.70.h_left, bf16[784,768]{1,0:T(8,128)(2,1)} %broadcast_select_fusion.h_right, bf16[784,768]{1,0:T(8,128)(2,1)} %get-tuple-element.71.n_left, bf16[784,3072]{1,0:T(8,128)(2,1)} %get-tuple-element.72.n_right, ...), custom_call_target="tpu_custom_call" | custom-call | tf_op jit(solution)/shard_map/pallas_call | solution.py:853
  473.0 0.7 slice_bitcast_fusion
  473.7 1.3 slice.51
  475.0 0.8 fusion
  475.8 0.8 slice.45
  476.6 2.5 shard_map.217
  479.2 6.0 %shard_map.216 = f32[768,2304]{1,0:T(8,128)} custom-call(bf16[24,768,384]{2,1,0:T(8,128)(2,1)} %get-tuple-element.79.src), custom_call_target="tpu_custom_call" | custom-call | tf_op jit(solution)/shard_map/pallas_call | solution.py:890
  485.2 7.6 %shard_map.219 = f32[3072,768]{1,0:T(8,128)} custom-call(bf16[24,768,384]{2,1,0:T(8,128)(2,1)} %get-tuple-element.79.src), custom_call_target="tpu_custom_call" | custom-call | tf_op jit(solution)/shard_map/pallas_call | solution.py:890
  492.8 7.8 %shard_map.218 = f32[768,3072]{1,0:T(8,128)} custom-call(bf16[24,768,384]{2,1,0:T(8,128)(2,1)} %get-tuple-element.79.src), custom_call_target="tpu_custom_call" | custom-call | tf_op jit(solution)/shard_map/pallas_call | solution.py:890
  500.6 0.6 broadcast_in_dim.31
  501.2 0.6 broadcast_in_dim.30
  501.8 0.6 broadcast_in_dim.29
  502.4 0.7 copy.43
  503.1 1.7 broadcast_select_fusion.1
  504.8 0.6 copy_bitcast_fusion.1
  (4 shorter events, 0.0 us)
Async XLA Ops:
  56.6 3.8 collective-permute-start
  60.4 1.1 copy-start.1
  66.9 108.3 %collective-permute-start.1 = (bf16[784,768]{1,0:T(8,128)(2,1)S(1)}, bf16[784,768]{1,0:T(8,128)(2,1)}, u32[]{:S(2)}, u32[]{:S(2)}) collective-permute-start(bf16[784,768]{1,0:T(8,128)(2,1)S(1)} %convert_element_type.6), channel_id=1, source_target_pairs={{16,0},{17,1},{18,2},{19,3},{20,4},{21,5},{22,6},{23,7},{24,8},{25... | collective-permute-start | bytes 3612680 | tf_op jit(solution)/shard_map/ppermute | solution.py:880
  492.8 10.3 %copy-start = (f32[784,768]{1,0:T(8,128)S(1)}, f32[784,768]{1,0:T(8,128)}, u32[]{:S(2)}) copy-start(f32[784,768]{1,0:T(8,128)} %get-tuple-element.68) | copy-start | bytes 7225348

commit v3 on v2

v3 whole, which is shorter than its diff:
```python
import functools

import jax
import jax.numpy as jnp
from jax import lax
from jax.experimental import pallas as pl
from jax.experimental.pallas import tpu as pltpu
from jax.sharding import PartitionSpec as P

MESH = pl.DeviceIdType.MESH
SIDE = 768
HEAD = 32
GROUP = 256
SLOT = 64
BF = jnp.bfloat16
F32 = jnp.float32


def cols(j, width=GROUP):
    return pl.ds(pl.multiple_of(j * width, width), width)


def dot(a, b):
    return lax.dot_general(a, b, (((1,), (0,)), ((), ())), preferred_element_type=F32)


def dot_t(a, b):
    return lax.dot_general(a, b, (((1,), (1,)), ((), ())), preferred_element_type=F32)


def t_dot(a, b):
    return lax.dot_general(a, b, (((0,), (0,)), ((), ())), preferred_element_type=F32)


def fill_swap(ref, images):
    rows, columns = ref.shape
    block = 128

    @pl.loop(0, rows // block)
    def _(b):
        r = lax.broadcasted_iota(jnp.int32, (block, columns), 0) + b * block
        c = lax.broadcasted_iota(jnp.int32, (block, columns), 1)
        image, position = lax.div(r, SLOT), lax.rem(r, SLOT)
        hit = (c == position * images + image) & (position < 49)
        ref[pl.ds(pl.multiple_of(b * block, block), block), :] = jnp.where(hit, 1.0, 0.0).astype(BF)


def clear_border(pad, images):
    zero = jnp.zeros((9 * images, pad.shape[1]), pad.dtype)
    pad[0 : 9 * images, :] = zero
    pad[72 * images : 81 * images, :] = zero
    one = jnp.zeros((images, pad.shape[1]), pad.dtype)

    @pl.loop(1, 8)
    def _(r):
        pad[pl.ds(pl.multiple_of(r * 9 * images, 16), images), :] = one
        pad[pl.ds(pl.multiple_of((r * 9 + 8) * images, 16), images), :] = one


def inside(r, images):
    return pl.ds(pl.multiple_of(((r + 1) * 9 + 1) * images, 16), 7 * images)


def grid_row(r, images):
    return pl.ds(pl.multiple_of(r * 7 * images, 16), 7 * images)


def encode(pad, kernel, bias, out, images):
    @pl.loop(0, pad.shape[1] // 128)
    def _(lane):
        ls = cols(lane, 128)
        taps = [jnp.broadcast_to(kernel[pl.ds(t, 1), ls], (images, 128)) for t in range(9)]
        shift = jnp.broadcast_to(bias[:, ls], (images, 128))

        @pl.loop(0, 7)
        def _(r):
            for c in range(7):
                total = shift
                for t in range(9):
                    at = pl.multiple_of(((r + t // 3) * 9 + c + t % 3) * images, 16)
                    piece = pad[pl.ds(at, images), ls]
                    total = total + piece * taps[t]
                    if t == 4:
                        total = total + piece
                out[pl.ds(pl.multiple_of((r * 7 + c) * images, 16), images), ls] = total


def normalise(stream, gain, bias, out, images):
    @pl.loop(0, 49, unroll=7)
    def _(p):
        rows = pl.ds(pl.multiple_of(p * images, 16), images)
        s = stream[rows, :]
        centered = s - jnp.mean(s, axis=-1, keepdims=True)
        spread = jnp.mean(centered * centered, axis=-1, keepdims=True)
        out[rows, :] = (centered * lax.rsqrt(spread + 1e-5) * gain[...] + bias[...]).astype(BF)


def head_mask(rows_per, count, lanes):
    shape = (count * rows_per, lanes)
    r = lax.broadcasted_iota(jnp.int32, shape, 0)
    c = lax.broadcasted_iota(jnp.int32, shape, 1)
    return lax.div(r, rows_per) == lax.div(c, HEAD)


def spread_heads(x, mask):
    count = mask.shape[0] // x.shape[0]
    return jnp.where(mask, jnp.concatenate([x] * count, axis=0), jnp.zeros((), x.dtype))


def fold_heads(x, mask, rows_per):
    kept = jnp.where(mask, x, 0.0)
    total = kept[0:rows_per]
    for h in range(1, x.shape[0] // rows_per):
        total = total + kept[h * rows_per : (h + 1) * rows_per]
    return total


def soft_down(scores, valid):
    if valid < scores.shape[0]:
        r = lax.broadcasted_iota(jnp.int32, scores.shape, 0)
        scores = jnp.where(r < valid, scores, -jnp.inf)
    e = jnp.exp(scores - jnp.max(scores, axis=0, keepdims=True))
    return e / jnp.sum(e, axis=0, keepdims=True)


def spatial_forward(packed, mixed, soft, images):
    width = mixed.shape[1]
    groups = width // GROUP

    @pl.loop(0, images, unroll=4)
    def _(i):
        rows = pl.ds(pl.multiple_of(i * SLOT, SLOT), SLOT)
        mask = head_mask(SLOT, GROUP // HEAD, GROUP)
        for g in range(groups):
            q, k, v = (packed[rows, part * width + g * GROUP : part * width + (g + 1) * GROUP] for part in range(3))
            weights = soft_down(dot_t(k, spread_heads(q, mask)), 49).astype(BF)
            soft[i, g] = weights
            mixed[rows, g * GROUP : (g + 1) * GROUP] = fold_heads(t_dot(weights, v), mask, SLOT).astype(BF)


def channel_forward(packed, mixed, soft, images):
    width = mixed.shape[1]

    @pl.loop(0, images, unroll=4)
    def _(i):
        rows = pl.ds(pl.multiple_of(i * SLOT, SLOT), SLOT)
        mask = head_mask(HEAD, 128 // HEAD, 128)
        for g in range(width // 128):
            q, k, v = (packed[rows, part * width + g * 128 : part * width + (g + 1) * 128] for part in range(3))
            weights = soft_down(fold_heads(t_dot(k, q), mask, HEAD), HEAD).astype(BF)
            soft[i, g // 2, g % 2 * HEAD : (g % 2 + 1) * HEAD, 0:128] = weights
            mixed[rows, g * 128 : (g + 1) * 128] = dot(v, spread_heads(weights, mask)).astype(BF)


def gelu_both(x):
    half = 0.5 + 0.5 * lax.erf(x * 0.7071067811865476)
    return x * half, half + x * (0.3989422804014327 * jnp.exp(-0.5 * x * x))


def forward_kernel(images, role, x, conv_w, conv_b, gain, shift, b_proj, b_fc1, b_fc2,
                   w_qkv, w_proj, w_fc1, w_fc2, *refs):
    earlier = len(refs) - 32
    (result, o_one, o_mid, o_two, o_n1, o_packed, o_soft, o_mixed, o_n2, o_hidden, o_slope,
     v_qkv, v_proj, v_fc1, v_fc2, pad, one, mid, two, n1, swap, n1s, packed, soft, mixed_s, mixed,
     n2, hidden, slope, end, load, store) = refs[earlier:]
    rows = 49 * images
    width = x.shape[1]
    loads = [pltpu.make_async_copy(src, dst, load.at[at]) for at, (src, dst) in enumerate(
        ((w_qkv, v_qkv), (w_proj, v_proj), (w_fc1, v_fc1), (w_fc2, v_fc2)))]
    stores = [pltpu.make_async_copy(src, dst, store.at[at]) for at, (src, dst) in enumerate(
        ((one, o_one), (mid, o_mid), (two, o_two), (n1, o_n1), (packed, o_packed), (soft, o_soft),
         (mixed, o_mixed), (n2, o_n2), (hidden, o_hidden), (slope, o_slope), (end, result)))]

    @pl.when(role[1] == 1)
    def _():
        for copy in loads:
            copy.start()
        fill_swap(swap, images)
        clear_border(pad, images)

        @pl.loop(0, 7)
        def _(r):
            pad[inside(r, images), :] = x[grid_row(r, images), :].astype(F32)
        encode(pad, conv_w.at[0], conv_b.at[pl.ds(0, 1)], one, images)
        stores[0].start()
        normalise(one, gain.at[pl.ds(0, 1)], shift.at[pl.ds(0, 1)], n1, images)
        stores[3].start()

        @pl.loop(0, width // GROUP)
        def _(j):
            n1s[:, cols(j)] = dot(swap[...], n1[:, cols(j)]).astype(BF)
        loads[0].wait()

        @pl.loop(0, 3 * width // GROUP)
        def _(j):
            scale = jnp.where(j < width // GROUP, HEAD ** -0.5, 1.0)
            packed[:, cols(j)] = (dot(n1s[...], v_qkv[:, cols(j)]) * scale).astype(BF)
        stores[4].start()

        @pl.when(role[0] == 1)
        def _():
            spatial_forward(packed, mixed_s, soft, images)

        @pl.when(role[0] == 0)
        def _():
            channel_forward(packed, mixed_s, soft, images)
        stores[5].start()

        @pl.loop(0, width // GROUP)
        def _(j):
            mixed[:, cols(j)] = t_dot(swap[...], mixed_s[:, cols(j)]).astype(BF)
        stores[6].start()
        loads[1].wait()

        @pl.loop(0, width // GROUP)
        def _(j):
            mid[:, cols(j)] = one[:, cols(j)] + dot(mixed[...], v_proj[:, cols(j)]) + b_proj[:, cols(j)]
        stores[1].start()

        @pl.loop(0, 7)
        def _(r):
            pad[inside(r, images), :] = mid[grid_row(r, images), :]
        encode(pad, conv_w.at[1], conv_b.at[pl.ds(1, 1)], two, images)
        stores[2].start()
        normalise(two, gain.at[pl.ds(1, 1)], shift.at[pl.ds(1, 1)], n2, images)
        stores[7].start()
        loads[2].wait()

        @pl.loop(0, v_fc1.shape[1] // GROUP)
        def _(j):
            pre = dot(n2[...], v_fc1[:, cols(j)]) + b_fc1[:, cols(j)]
            value, rate = gelu_both(pre)
            hidden[:, cols(j)] = value.astype(BF)
            slope[:, cols(j)] = rate.astype(BF)
        stores[8].start()
        stores[9].start()
        loads[3].wait()

        @pl.loop(0, width // GROUP)
        def _(j):
            end[:, cols(j)] = two[:, cols(j)] + dot(hidden[...], v_fc2[:, cols(j)]) + b_fc2[:, cols(j)]
        stores[10].start()
        for copy in stores:
            copy.wait()


def forward_block(role, x, params, images, earlier=()):
    conv_w, conv_b, gain, shift, w_qkv, w_proj, b_proj, w_fc1, b_fc1, w_fc2, b_fc2 = params
    rows, width = x.shape
    wide = w_fc1.shape[1]
    slots = images * SLOT
    any_space = pl.BlockSpec(memory_space=pl.ANY)
    vmem = pl.BlockSpec(memory_space=pltpu.VMEM)
    outs = [((rows, width), F32), ((rows, width), F32), ((rows, width), F32), ((rows, width), F32),
            ((rows, width), BF), ((slots, 3 * width), BF), ((images, width // GROUP, SLOT, 2 * GROUP), BF),
            ((rows, width), BF), ((rows, width), BF), ((rows, wide), BF), ((rows, wide), BF)]
    scratch = [w_qkv, w_proj, w_fc1, w_fc2]
    return pl.pallas_call(
        functools.partial(forward_kernel, images),
        out_shape=[jax.ShapeDtypeStruct(*o) for o in outs],
        in_specs=[pl.BlockSpec(memory_space=pltpu.SMEM)] + [vmem] * 8 + [any_space] * (4 + len(earlier)),
        out_specs=[any_space] * len(outs),
        input_output_aliases={13 + at: at for at in range(len(earlier))},
        scratch_shapes=[pltpu.VMEM(w.shape, w.dtype) for w in scratch] + [
            pltpu.VMEM((81 * images, width), F32),
            pltpu.VMEM((rows, width), F32), pltpu.VMEM((rows, width), F32), pltpu.VMEM((rows, width), F32),
            pltpu.VMEM((rows, width), BF), pltpu.VMEM((slots, rows), BF), pltpu.VMEM((slots, width), BF),
            pltpu.VMEM((slots, 3 * width), BF), pltpu.VMEM((images, width // GROUP, SLOT, 2 * GROUP), BF),
            pltpu.VMEM((slots, width), BF), pltpu.VMEM((rows, width), BF), pltpu.VMEM((rows, width), BF),
            pltpu.VMEM((rows, wide), BF), pltpu.VMEM((rows, wide), BF), pltpu.VMEM((rows, width), F32),
            pltpu.SemaphoreType.DMA((4,)), pltpu.SemaphoreType.DMA((11,)),
        ],
        compiler_params=pltpu.CompilerParams(vmem_limit_bytes=62 * 2**20),
    )(role, x, conv_w, conv_b, gain, shift, b_proj, b_fc1, b_fc2, w_qkv, w_proj, w_fc1, w_fc2, *earlier)


def dp_dims(n):
    sizes = [1, 1, 1]
    at = 0
    left = n
    while left > 1:
        factor = 2 if left % 2 == 0 else left
        sizes[at % 3] *= factor
        left //= factor
        at += 1
    return tuple(sizes), (sizes[1] * sizes[2], sizes[2], 1)


class Place:
    def __init__(self, dp, size, stride):
        self.size = size
        pos = lax.rem(lax.div(dp, stride), size)
        low = pos < (size + 1) // 2
        self.outer = jnp.where(low, pos, size - 1 - pos)
        self.pos = pos
        self.low = low
        step = jnp.where(low, stride, -stride)
        self.inner_peer = dp + step
        self.outer_peer = dp - step


def pick(flag, a, b):
    out = object.__new__(Place)
    out.size = a.size
    for name in ("pos", "low", "outer", "inner_peer", "outer_peer"):
        setattr(out, name, jnp.where(flag, getattr(a, name), getattr(b, name)))
    return out


class Ring:
    def __init__(self, dp, dims, rows, grad, land, out, out_at, send, recv, local):
        (s0, s1, s2), (t0, t1, t2) = dims
        self.mids = Place(dp, s0, t0)
        self.fast, self.slow = Place(dp, s2, t2), Place(dp, s1, t1)
        self.grad, self.land, self.out, self.out_at = grad, land, out, out_at
        self.grads, self.lands = grad.shape[0], land.shape[0]
        self.send, self.recv, self.local = send, recv, local
        self.sizes, self.lens, self.starts, _ = Ring.shape(rows, dims)

    @staticmethod
    def shape(rows, dims):
        s0, s1, s2 = dims[0]
        sizes = (s2, s0, s1)
        lens = (rows // s2, rows // s2 // s0, rows // (s0 * s1 * s2))
        total, starts = 0, []
        for n, length in zip(sizes, lens):
            starts.append(total)
            total += length * (1 if n == 2 else 5)
        return sizes, lens, starts, total

    def level(self, c, i):
        flag = lax.rem(c, 2) == 0
        if i == 1:
            return self.mids
        return pick(flag, self.fast, self.slow) if i == 0 else pick(flag, self.slow, self.fast)

    def base(self, c, i):
        start = 0
        for j in range(i):
            start = start + self.level(c, j).pos * self.lens[j]
        return start

    def span(self, c, i, a, b):
        place, length, n = self.level(c, i), self.lens[i], self.sizes[i]
        start = self.base(c, i) + jnp.where(place.low, a * length, (n - b) * length)
        return pl.ds(pl.multiple_of(start, 8), (b - a) * length)

    def mine(self, c, rows):
        return self.grad.at[lax.rem(c, self.grads), rows]

    def landing(self, c, i, at, length):
        return self.land.at[lax.rem(c, self.lands), pl.ds(self.starts[i] + at, length)]

    def copy(self, c, ev, src, dst, peer):
        return pltpu.make_async_remote_copy(
            src_ref=src, dst_ref=dst, send_sem=self.send.at[c, ev], recv_sem=self.recv.at[c, ev],
            device_id={"dp": peer}, device_id_type=MESH)

    def add(self, c, i, a, b, at):
        rows = self.span(c, i, a, b)
        slot = lax.rem(c, self.grads)
        got = self.landing(c, i, at, (b - a) * self.lens[i])
        self.grad[slot, rows] = self.grad[slot, rows] + got[...]

    def give(self, c, i, ev, a, b, at, peer):
        return self.copy(c, ev, self.mine(c, self.span(c, i, a, b)), self.landing(c, i, at, (b - a) * self.lens[i]), peer)

    def reduce_stages(self, i):
        n, length = self.sizes[i], self.lens[i]
        ein, eout = 2 * i, 2 * i + 1
        if n == 1:
            return []
        if n == 2:
            def first(c):
                self.give(c, i, eout, 1, 2, 0, self.level(c, i).inner_peer).start()

            def last(c):
                self.give(c, i, eout, 0, 1, 0, self.level(c, i).inner_peer).wait_recv()
                self.add(c, i, 0, 1, 0)
            return [first, last]

        def zero(c):
            place = self.level(c, i)

            @pl.when(place.outer == 0)
            def _():
                self.give(c, i, ein, 1, 4, 0, place.inner_peer).start()

        def one(c):
            place = self.level(c, i)

            @pl.when(place.outer == 1)
            def _():
                self.give(c, i, ein, 1, 4, 0, place.inner_peer).wait_recv()
                self.add(c, i, 2, 4, jnp.where(place.low, length, 0))
                self.give(c, i, eout, 2, 4, 3 * length, place.inner_peer).start()
                self.add(c, i, 1, 2, jnp.where(place.low, 0, 2 * length))

        def two(c):
            place = self.level(c, i)

            @pl.when(place.outer == 1)
            def _():
                self.give(c, i, eout, 0, 2, 3 * length, place.inner_peer).wait_recv()
                self.add(c, i, 0, 2, 3 * length)
                self.give(c, i, ein, 0, 1, 3 * length, place.outer_peer).start()

        def three(c):
            place = self.level(c, i)

            @pl.when(place.outer == 0)
            def _():
                self.give(c, i, ein, 0, 1, 3 * length, place.inner_peer).wait_recv()
                self.add(c, i, 0, 1, 3 * length)
        return [zero, one, two, three]

    def reduce_ends(self, c):
        for i in range(3):
            n, place = self.sizes[i], self.level(c, i)
            ein, eout = 2 * i, 2 * i + 1
            if n == 2:
                self.give(c, i, eout, 1, 2, 0, place.inner_peer).wait_send()
            elif n == 4:
                @pl.when(place.outer == 0)
                def _():
                    self.give(c, i, ein, 1, 4, 0, place.inner_peer).wait_send()

                @pl.when(place.outer == 1)
                def _():
                    self.give(c, i, eout, 2, 4, 0, place.inner_peer).wait_send()
                    self.give(c, i, ein, 0, 1, 0, place.outer_peer).wait_send()

    def spread(self, c, i, ev, a, b, peer):
        dst = self.out.at[self.out_at(c), self.span(c, i, a, b)]
        return self.copy(c, ev, dst, dst, peer)

    def gather_stages(self, i):
        n = self.sizes[i]
        ein, eout = 6 + 2 * i, 7 + 2 * i
        if n == 1:
            return []
        if n == 2:
            def first(c):
                self.spread(c, i, eout, 0, 1, self.level(c, i).inner_peer).start()

            def last(c):
                self.spread(c, i, eout, 1, 2, self.level(c, i).inner_peer).wait_recv()
            return [first, last]

        def zero(c):
            place = self.level(c, i)

            @pl.when(place.outer == 0)
            def _():
                self.spread(c, i, ein, 0, 1, place.inner_peer).start()

        def one(c):
            place = self.level(c, i)

            @pl.when(place.outer == 1)
            def _():
                self.spread(c, i, ein, 0, 1, place.outer_peer).wait_recv()
                self.spread(c, i, eout, 0, 2, place.inner_peer).start()

        def two(c):
            place = self.level(c, i)

            @pl.when(place.outer == 1)
            def _():
                self.spread(c, i, eout, 2, 4, place.inner_peer).wait_recv()
                self.spread(c, i, ein, 1, 4, place.outer_peer).start()

        def three(c):
            place = self.level(c, i)

            @pl.when(place.outer == 0)
            def _():
                self.spread(c, i, ein, 1, 4, place.inner_peer).wait_recv()
        return [zero, one, two, three]

    def gather_ends(self, c):
        for i in range(3):
            n, place = self.sizes[i], self.level(c, i)
            ein, eout = 6 + 2 * i, 7 + 2 * i
            if n == 2:
                self.spread(c, i, eout, 0, 1, place.inner_peer).wait_send()
            elif n == 4:
                @pl.when(place.outer == 0)
                def _():
                    self.spread(c, i, ein, 0, 1, place.inner_peer).wait_send()

                @pl.when(place.outer == 1)
                def _():
                    self.spread(c, i, eout, 0, 2, place.inner_peer).wait_send()
                    self.spread(c, i, ein, 1, 4, place.outer_peer).wait_send()

    def settle(self, c):
        rows = pl.ds(pl.multiple_of(self.base(c, 3), 8), self.lens[2])
        copy = pltpu.make_async_copy(self.mine(c, rows), self.out.at[self.out_at(c), rows], self.local)
        copy.start()
        copy.wait()

    def stages(self, first, last):
        groups = [self.reduce_stages(0), self.reduce_stages(1), self.reduce_stages(2), [self.settle],
                  self.gather_stages(2), self.gather_stages(1), self.gather_stages(0), [last]]
        joined = [[first]]
        for group in groups:
            if group:
                joined[-1].append(group[0])
                joined += [[stage] for stage in group[1:]]
        return [functools.partial(run_all, stages) for stages in joined]

    def greet(self):
        barrier = pltpu.get_barrier_semaphore()
        pl.semaphore_signal(barrier, inc=1, device_id={"pipe": 1 - lax.axis_index("pipe")}, device_id_type=MESH)
        count = jnp.int32(1)
        for place in (self.fast, self.mids, self.slow):
            if place.size == 1:
                continue
            pl.semaphore_signal(barrier, inc=1, device_id={"dp": place.inner_peer}, device_id_type=MESH)
            count = count + 1
            if place.size == 4:
                @pl.when(place.outer == 1)
                def _():
                    pl.semaphore_signal(barrier, inc=1, device_id={"dp": place.outer_peer}, device_id_type=MESH)
                count = count + jnp.where(place.outer == 1, 1, 0)
        pl.semaphore_wait(barrier, count)


def run_all(stages, c):
    for stage in stages:
        stage(c)


def encode_back(gpad, given, kernel, out, put, first_row, bias_row, images):
    @pl.loop(0, gpad.shape[1] // 128)
    def _(lane):
        ls = cols(lane, 128)
        taps = [jnp.broadcast_to(kernel[pl.ds(8 - t, 1), ls], (images, 128)) for t in range(9)]

        def row(r, totals):
            totals = list(totals)
            for c in range(7):
                at = pl.ds(pl.multiple_of((r * 7 + c) * images, 16), images)
                source = given[at, ls].astype(F32)
                total = None
                for t in range(9):
                    near = pl.ds(pl.multiple_of(((r + t // 3) * 9 + c + t % 3) * images, 16), images)
                    piece = gpad[near, ls]
                    if t == 4:
                        totals[9] = totals[9] + piece
                        total = total + piece
                    total = piece * taps[t] if total is None else total + piece * taps[t]
                    totals[8 - t] = totals[8 - t] + source * piece
                out[at, ls] = total
            return tuple(totals)
        totals = lax.fori_loop(0, 7, row, (jnp.zeros((images, 128), F32),) * 10)
        for t in range(9):
            put(first_row + t, lane, jnp.sum(totals[t], axis=0, keepdims=True))
        put(bias_row, lane, jnp.sum(totals[9], axis=0, keepdims=True))


def normalise_back(stream, grad, base, gain, gpad, put, gain_row, shift_row, acc, images):
    acc[...] = jnp.zeros_like(acc)

    @pl.loop(0, 49, unroll=7)
    def _(p):
        rows = pl.ds(pl.multiple_of(p * images, 16), images)
        s, dy = stream[rows, :], grad[rows, :]
        centered = s - jnp.mean(s, axis=-1, keepdims=True)
        rate = lax.rsqrt(jnp.mean(centered * centered, axis=-1, keepdims=True) + 1e-5)
        unit = centered * rate
        acc[0] += dy * unit
        acc[1] += dy
        dg = dy * gain[...]
        m1 = jnp.mean(dg, axis=-1, keepdims=True)
        m2 = jnp.mean(dg * unit, axis=-1, keepdims=True)
        at = ((lax.div(p, 7) + 1) * 9 + lax.rem(p, 7) + 1) * images
        gpad[pl.ds(pl.multiple_of(at, 16), images), :] = base[rows, :].astype(F32) + rate * (dg - m1 - unit * m2)
    for row, total in ((gain_row, acc[0]), (shift_row, acc[1])):
        total = jnp.sum(total, axis=0, keepdims=True)
        for lane in range(total.shape[1] // 128):
            put(row, lane, total[:, lane * 128 : (lane + 1) * 128])


def spatial_backward(packed, grad_mixed, soft, images):
    width = grad_mixed.shape[1]

    @pl.loop(0, images)
    def _(i):
        rows = pl.ds(pl.multiple_of(i * SLOT, SLOT), SLOT)
        mask = head_mask(SLOT, GROUP // HEAD, GROUP)
        made = []
        for g in range(width // GROUP):
            at = [slice(part * width + g * GROUP, part * width + (g + 1) * GROUP) for part in range(3)]
            made.append((at, [packed[rows, a] for a in at], soft[i, g], grad_mixed[rows, g * GROUP : (g + 1) * GROUP]))
        ready = []
        for at, (q, k, v), weights, do in made:
            out_spread = spread_heads(do, mask)
            w = weights.astype(F32)
            dw = dot_t(v, out_spread)
            ds = (w * (dw - jnp.sum(dw * w, axis=0, keepdims=True))).astype(BF)
            dq = (fold_heads(t_dot(ds, k), mask, SLOT) * HEAD ** -0.5).astype(BF)
            ready += zip(at, (dq, dot(ds, spread_heads(q, mask)).astype(BF), dot(weights, out_spread).astype(BF)))
        for at, value in ready:
            packed[rows, at] = value


def channel_backward(packed, grad_mixed, soft, images):
    width = grad_mixed.shape[1]

    @pl.loop(0, images)
    def _(i):
        rows = pl.ds(pl.multiple_of(i * SLOT, SLOT), SLOT)
        mask = head_mask(HEAD, 128 // HEAD, 128)
        made = []
        for g in range(width // 128):
            at = [slice(part * width + g * 128, part * width + (g + 1) * 128) for part in range(3)]
            weights = soft[i, g // 2, g % 2 * HEAD : (g % 2 + 1) * HEAD, 0:128]
            made.append((at, [packed[rows, a] for a in at], weights, grad_mixed[rows, g * 128 : (g + 1) * 128]))
        ready = []
        for at, (q, k, v), weights, do in made:
            w = weights.astype(F32)
            dw = fold_heads(t_dot(v, do), mask, HEAD)
            ds = spread_heads((w * (dw - jnp.sum(dw * w, axis=0, keepdims=True))).astype(BF), mask)
            dq = (dot(k, ds) * HEAD ** -0.5).astype(BF)
            ready += zip(at, (dq, dot_t(q, ds).astype(BF), dot_t(do, spread_heads(weights, mask)).astype(BF)))
        for at, value in ready:
            packed[rows, at] = value


class Plan:
    def __init__(self, width, wide, n):
        self.chunk = 384 if n <= 16 else 128
        per = width // self.chunk
        self.fc2, self.fc1 = wide // SIDE * per, wide // self.chunk
        self.proj, self.qkv = per, 3 * per
        self.total = self.fc2 + self.fc1 + self.proj + self.qkv
        self.lent = self.fc2 + self.fc1 // 2
        self.taken = self.fc2 + self.fc1
        self.count = (self.lent + self.proj + self.qkv, self.total - self.lent + self.taken)
        self.slots = self.total + self.taken
        self.most = max(self.count)

    def where(self, first, c):
        theirs = jnp.where(first, c < self.lent, c >= self.total - self.lent)
        number = jnp.where(first, jnp.where(theirs, c, c - self.lent + self.taken),
                           jnp.where(theirs, c - (self.total - self.lent), c + self.lent))
        return theirs, number

    def out_at(self, first, c):
        theirs, number = self.where(first, c)
        return jnp.where(theirs, self.total + number, number)


def back_kernel(images, dims, rows, lags, early, plan,
                own, x, conv_w, gain, w_qkv, w_proj, w_fc1, w_fc2, one, mid, two, h_packed, h_soft, h_slope, hidden, n2, mixed, n1,
                o_grad, out, small_out, g_packed, g_att, g_pre, x_hidden, x_n2, x_cot, x_pre,
                v_a, v_fc1, gpad, stream, packed, soft, slope, swap, gm_s, gn, gmid, gatt, cot, acc, small_grad,
                grad, land, small_land, left_buf, right_buf,
                load, store, push_send, push_recv, fetch_sem, send, recv, local, ssend, srecv, slocal, bring_send, bring_recv):
    pipe, dp = lax.axis_index("pipe"), lax.axis_index("dp")
    first = pipe == 0
    width, wide = x.shape[1], w_fc1.shape[1]
    chunk = plan.chunk
    rank = width // GROUP
    main = Ring(dp, dims, rows, grad, land, out, functools.partial(plan.out_at, first), send, recv, local)
    small = Ring(dp, dims, small_grad.shape[1], small_grad, small_land, small_out, lambda c: 0, ssend, srecv, slocal)
    count = jnp.where(first, plan.count[0], plan.count[1])
    opening = jnp.where(first, plan.lent, 0)

    def to_core(at, src, dst):
        return pltpu.make_async_remote_copy(src_ref=src, dst_ref=dst, send_sem=push_send.at[at], recv_sem=push_recv.at[at],
                                            device_id={"pipe": 1 - pipe}, device_id_type=MESH)
    blocks = wide // SIDE
    push_hidden = [to_core(k, hidden.at[:, pl.ds(k * SIDE, SIDE)], x_hidden.at[:, pl.ds(k * SIDE, SIDE)]) for k in range(blocks)]
    push_n2 = to_core(blocks, n2, x_n2)
    push_pre = to_core(blocks + 1, slope, x_pre)
    push_cot = to_core(blocks + 2, own, x_cot)
    push_grad = to_core(blocks + 3, gatt, cot)

    def get(c, left, right):
        slot = lax.rem(c, 2)
        pltpu.make_async_copy(left, left_buf.at[slot], fetch_sem.at[slot, 0]).start()
        pltpu.make_async_copy(right, right_buf.at[slot], fetch_sem.at[slot, 1]).start()

    def fetch(c):
        theirs, number = plan.where(first, c)
        per = width // chunk
        at2, at1 = number, number - plan.fc2
        at_p, at_q = number - plan.taken, number - plan.taken - plan.proj

        @pl.when(theirs & (at1 < 0))
        def _():
            for k in range(blocks):
                @pl.when(at2 == k * per)
                def _():
                    push_hidden[k].wait_recv()

            @pl.when((at2 == 0) & first)
            def _():
                push_cot.wait_recv()
            get(c, x_hidden.at[:, cols(lax.div(at2, per), SIDE)], x_cot.at[:, cols(lax.rem(at2, per), chunk)])

        @pl.when(theirs & (at1 >= 0))
        def _():
            @pl.when(at1 == 0)
            def _():
                push_n2.wait_recv()
                push_pre.wait_recv()
            get(c, x_n2, x_pre.at[:, cols(at1, chunk)])

        @pl.when(jnp.logical_not(theirs) & (at_p < 0))
        def _():
            get(c, n2, g_pre.at[:, cols(at1, chunk)])

        @pl.when(jnp.logical_not(theirs) & (at_p >= 0) & (at_q < 0))
        def _():
            get(c, mixed, g_att.at[:, cols(at_p, chunk)])

        @pl.when(jnp.logical_not(theirs) & (at_q >= 0))
        def _():
            get(c, n1, g_packed.at[:, cols(at_q, chunk)])

    def make(end, c):
        slot = lax.rem(c, 2)
        pltpu.make_async_copy(n2, left_buf.at[slot], fetch_sem.at[slot, 0]).wait()
        pltpu.make_async_copy(n2.at[:, pl.ds(0, chunk)], right_buf.at[slot], fetch_sem.at[slot, 1]).wait()

        @pl.when(c + 1 < end)
        def _():
            fetch(c + 1)

        @pl.when(c >= main.grads)
        def _():
            main.reduce_ends(c - main.grads)
        place = lax.rem(c, main.grads)
        for j in range(SIDE // GROUP):
            part = slice(j * GROUP, (j + 1) * GROUP)
            grad[place, part] = t_dot(left_buf[slot, :, part], right_buf[slot]).astype(BF)
        if rows > SIDE:
            grad[place, SIDE:rows] = jnp.zeros((rows - SIDE, chunk), BF)

    def bring(c):
        _, number = plan.where(first, c)
        return pltpu.make_async_remote_copy(
            src_ref=out.at[plan.out_at(first, c)], dst_ref=out.at[number], send_sem=bring_send.at[number], recv_sem=bring_recv.at[number],
            device_id={"pipe": 1 - pipe}, device_id_type=MESH)

    def hand_over(c):
        @pl.when(plan.where(first, c)[0])
        def _():
            bring(c).start()

    def tick(t, start, end, with_small):
        stages = main.stages(functools.partial(make, end), hand_over)
        small_stages = small.stages(lambda c: None, lambda c: None)
        for s in reversed(range(len(stages))):
            c = t - lags[s]

            @pl.when((c >= start) & (c < end))
            def _():
                stages[s](c)
            if with_small:
                @pl.when(c == end)
                def _():
                    small_stages[s](0)

    def put(row, lane, value):
        small_grad[0, pl.ds(lane * 32 + row, 1), :] = value

    main.greet()
    for copy in push_hidden:
        copy.start()
    push_n2.start()
    load_cot = pltpu.make_async_copy(own, cot, load.at[10])

    @pl.when(jnp.logical_not(first))
    def _():
        push_cot.start()
        load_cot.start()
    v_qkv = [(w_qkv.at[:, pl.ds(part * width, width)], v_a.at[pl.ds(part * width, width)]) for part in range(3)]
    loads = {at: pltpu.make_async_copy(src, dst, load.at[at]) for at, (src, dst) in enumerate(
        [(w_fc2, v_a), (h_slope, slope), (w_fc1, v_fc1), (two, stream), (mid, gmid), (h_soft, soft), (h_packed, packed)]
        + v_qkv)}
    load_proj = pltpu.make_async_copy(w_proj, v_a.at[pl.ds(3 * width, width)], load.at[11])
    load_one = pltpu.make_async_copy(one, stream, load.at[12])
    for at in range(7):
        loads[at].start()
    fill_swap(swap, images)
    clear_border(gpad, images)
    small_grad[...] = jnp.zeros_like(small_grad)

    @pl.when(first)
    def _():
        fetch(0)

        @pl.loop(0, plan.lent + early)
        def _(t):
            tick(t, 0, plan.lent, False)
        push_grad.wait_recv()

    @pl.when(jnp.logical_not(first))
    def _():
        load_cot.wait()
    loads[0].wait()
    loads[1].wait()
    steps = wide // GROUP
    left_over = lags[-1] + 1 - early
    each = -(-left_over // steps)

    @pl.loop(0, steps)
    def _(j):
        if each > 0:
            @pl.when(first)
            def _():
                @pl.loop(0, each)
                def _(k):
                    tick(plan.lent + early + j * each + k, 0, plan.lent, False)
        pre = dot_t(cot[...], v_a[cols(j), :]) * slope[:, cols(j)].astype(F32)
        slope[:, cols(j)] = pre.astype(BF)
        total = jnp.sum(pre, axis=0, keepdims=True)
        for half in range(GROUP // 128):
            at = j * (GROUP // 128) + half
            put(25 + lax.div(at, width // 128), lax.rem(at, width // 128), total[:, half * 128 : (half + 1) * 128])
    push_pre.start()
    store_pre = pltpu.make_async_copy(slope, g_pre, store.at[0])
    store_pre.start()
    for at in range(7, 10):
        loads[at].start()
    load_proj.start()
    for lane in range(width // 128):
        put(29, lane, jnp.sum(cot[:, lane * 128 : (lane + 1) * 128].astype(F32), axis=0, keepdims=True))
    loads[2].wait()

    @pl.loop(0, rank)
    def _(j):
        gn[:, cols(j)] = dot_t(slope[...], v_fc1[cols(j), :])
    loads[3].wait()
    normalise_back(stream, gn, cot, gain.at[pl.ds(1, 1)], gpad, put, 21, 23, acc, images)
    load_one.start()
    loads[4].wait()
    encode_back(gpad, gmid, conv_w.at[1], gmid, put, 9, 19, images)
    for lane in range(width // 128):
        part = gmid[:, lane * 128 : (lane + 1) * 128]
        put(24, lane, jnp.sum(part, axis=0, keepdims=True))
        gatt[:, lane * 128 : (lane + 1) * 128] = part.astype(BF)
    store_att = pltpu.make_async_copy(gatt, g_att, store.at[1])
    store_att.start()
    push_pre.wait_send()
    store_pre.wait()
    load_proj.wait()

    @pl.loop(0, rank)
    def _(j):
        at = pl.ds(pl.multiple_of(3 * width + j * GROUP, GROUP), GROUP)
        slope[:, cols(j)] = dot_t(gatt[...], v_a[at, :]).astype(BF)

    @pl.loop(0, rank)
    def _(j):
        gm_s[:, cols(j)] = dot(swap[...], slope[:, cols(j)]).astype(BF)
    loads[5].wait()
    loads[6].wait()

    @pl.when(first)
    def _():
        spatial_backward(packed, gm_s, soft, images)

    @pl.when(jnp.logical_not(first))
    def _():
        channel_backward(packed, gm_s, soft, images)

    @pl.loop(0, 3 * rank)
    def _(j):
        slope[:, cols(j)] = t_dot(swap[...], packed[:, cols(j)]).astype(BF)
    grad_packed = slope.at[:, pl.ds(0, 3 * width)]
    store_packed = pltpu.make_async_copy(grad_packed, g_packed, store.at[2])
    store_packed.start()
    for at in range(7, 10):
        loads[at].wait()

    @pl.loop(0, rank)
    def _(j):
        w = jnp.concatenate([v_a[pl.ds(pl.multiple_of(part * width + j * GROUP, GROUP), GROUP), :] for part in range(3)], axis=1)
        gn[:, cols(j)] = dot_t(slope[:, 0 : 3 * width], w)
    load_one.wait()
    normalise_back(stream, gn, gmid, gain.at[pl.ds(0, 1)], gpad, put, 20, 22, acc, images)
    encode_back(gpad, x, conv_w.at[0], gmid, put, 0, 18, images)
    store_att.wait()
    store_packed.wait()
    store_grad = pltpu.make_async_copy(gmid, o_grad, store.at[3])
    store_grad.start()

    @pl.when(jnp.logical_not(first))
    def _():
        gatt[...] = gmid[...].astype(BF)
        push_grad.start()
        keep = pltpu.make_async_copy(gatt, x_cot, store.at[4])
        keep.start()
        keep.wait()

    fetch(opening)

    @pl.loop(opening, count + 1 + lags[-1])
    def _(t):
        tick(t, opening, count, True)

    @pl.loop(jnp.maximum(count - main.grads, 0), count)
    def _(c):
        main.reduce_ends(c)

    @pl.loop(0, count)
    def _(c):
        main.gather_ends(c)

        @pl.when(plan.where(first, c)[0])
        def _():
            bring(c).wait_send()
    small.reduce_ends(0)
    small.gather_ends(0)
    for copy in push_hidden:
        copy.wait_send()
    push_n2.wait_send()
    store_grad.wait()

    @pl.when(jnp.logical_not(first))
    def _():
        push_cot.wait_send()
        push_grad.wait_send()

    @pl.loop(0, jnp.where(first, plan.taken, plan.lent))
    def _(k):
        pltpu.make_async_remote_copy(
            src_ref=out.at[k], dst_ref=out.at[k], send_sem=bring_send.at[k], recv_sem=bring_recv.at[k],
            device_id={"pipe": 1 - pipe}, device_id_type=MESH).wait_recv()


def backward(own, x, saved, params, images, n, early=12, collective_id=0):
    conv_w, conv_b, gain, shift, w_qkv, w_proj, b_proj, w_fc1, b_fc1, w_fc2, b_fc2 = params
    one, mid, two, n1, packed, soft, mixed, n2, hidden, slope = saved
    tokens, width = x.shape
    wide = w_fc1.shape[1]
    slots = images * SLOT
    dims = dp_dims(n)
    plan = Plan(width, wide, n)
    rows = -(-SIDE // (16 * n)) * 16 * n
    small_rows = 16 * n
    _, _, _, land = Ring.shape(rows, dims)
    _, _, _, small_land = Ring.shape(small_rows, dims)
    hops = sum(0 if s == 1 else 1 if s == 2 else 3 for s in dims[0])
    gaps = [3] + [2] * (2 * hops - 2) + [3]
    lags = [sum(gaps[:s]) for s in range(2 * hops + 1)]
    grads, lands = lags[hops] + 3, 2 * gaps[0] + 4
    lands += lands % 2
    any_space = pl.BlockSpec(memory_space=pl.ANY)
    vmem = pl.BlockSpec(memory_space=pltpu.VMEM)
    outs = [((tokens, width), F32), ((plan.slots, rows, plan.chunk), BF), ((1, small_rows, 128), F32),
            ((tokens, 3 * width), BF), ((tokens, width), BF), ((tokens, wide), BF),
            ((tokens, wide), BF), ((tokens, width), BF), ((tokens, width), BF), ((tokens, wide), BF)]
    dma = pltpu.SemaphoreType.DMA
    results = pl.pallas_call(
        functools.partial(back_kernel, images, dims, rows, lags, early, plan),
        out_shape=[jax.ShapeDtypeStruct(*o) for o in outs],
        in_specs=[any_space] + [vmem] * 3 + [any_space] * 14,
        out_specs=[any_space] * len(outs),
        scratch_shapes=[
            pltpu.VMEM(w_fc2.shape, BF), pltpu.VMEM(w_fc1.shape, BF), pltpu.VMEM((81 * images, width), F32),
            pltpu.VMEM((tokens, width), F32), pltpu.VMEM(packed.shape, BF), pltpu.VMEM(soft.shape, BF), pltpu.VMEM((tokens, wide), BF),
            pltpu.VMEM((slots, tokens), BF), pltpu.VMEM((slots, width), BF),
            pltpu.VMEM((tokens, width), F32), pltpu.VMEM((tokens, width), F32), pltpu.VMEM((tokens, width), BF), pltpu.VMEM((tokens, width), BF),
            pltpu.VMEM((2, images, width), F32), pltpu.VMEM((1, small_rows, 128), F32),
            pltpu.VMEM((grads, rows, plan.chunk), BF), pltpu.VMEM((lands, land, plan.chunk), BF), pltpu.VMEM((1, small_land, 128), F32),
            pltpu.VMEM((2, tokens, SIDE), BF), pltpu.VMEM((2, tokens, plan.chunk), BF),
            dma((13,)), dma((5,)), dma((wide // SIDE + 4,)), dma((wide // SIDE + 4,)), dma((2, 2)),
            dma((plan.most, 12)), dma((plan.most, 12)), dma, dma((1, 12)), dma((1, 12)), dma, dma((plan.taken,)), dma((plan.taken,)),
        ],
        compiler_params=pltpu.CompilerParams(collective_id=collective_id, has_side_effects=True, vmem_limit_bytes=63 * 2**20),
    )(own, x, conv_w, gain, w_qkv, w_proj, w_fc1, w_fc2, one, mid, two, packed, soft, slope, hidden, n2, mixed, n1)
    return results[0], results[1], results[2], plan


def shifted(x, axis, by):
    count = lax.axis_size(axis)
    pairs = [(i, i + by) for i in range(count) if 0 <= i + by < count]
    return lax.ppermute(x, axis, pairs)


def widen(src, dst):
    dst[...] = src[0].astype(F32)


def from_chunks(done, start, shape):
    rows, columns = shape
    chunk = done.shape[2]
    across = columns // chunk
    return pl.pallas_call(
        widen,
        grid=(rows // SIDE, across),
        in_specs=[pl.BlockSpec((1, SIDE, chunk), lambda r, j: (start + r * across + j, 0, 0))],
        out_specs=pl.BlockSpec((SIDE, chunk), lambda r, j: (r, j)),
        out_shape=jax.ShapeDtypeStruct(shape, F32),
    )(done)


def on_device(section_inputs, conv_weight, conv_bias, norm_gain, norm_bias, w_qkv, w_proj, b_proj, w_fc1, b_fc1, w_fc2, b_fc2):
    pipe, n = lax.axis_index("pipe"), lax.axis_size("dp")
    is_first = pipe == 0
    weights = (conv_weight, conv_bias, norm_gain, norm_bias, w_qkv, w_proj, b_proj, w_fc1, b_fc1, w_fc2, b_fc2)
    conv_w, conv_b, gain, shift, wq, wp, bp, w1, b1, w2, b2 = (weight[0] for weight in weights)
    params = (conv_w, conv_b, gain, shift, wq, wp, bp[None], w1, b1[None], w2, b2[None])
    images, _, width = section_inputs.shape[1:]

    def role(first):
        return jnp.stack([is_first.astype(jnp.int32), (is_first == first).astype(jnp.int32)])

    own = jnp.swapaxes(section_inputs[0], 0, 1).reshape(-1, width)
    first_out = forward_block(role(True), own, params, images)
    middle = shifted(first_out[0].astype(BF), "pipe", 1)
    second_out = forward_block(role(False), middle, params, images, first_out)
    x = jnp.where(is_first, own, middle)
    result, *saved = second_out
    grad_in, done, small_done, plan = backward(own, x, saved, params, images, n)
    ends = jnp.where(is_first, grad_in, result).reshape(49, images, width)
    section_ends = jnp.swapaxes(ends, 0, 1)[None]
    grads, at = [], 0
    for shape in (w2.shape, w1.shape, wp.shape, wq.shape):
        grads.append(from_chunks(done, at, shape)[None])
        at += shape[0] // SIDE * shape[1] // plan.chunk
    grad_fc2, grad_fc1, grad_proj, grad_qkv = grads
    lanes = width // 128
    sums = jnp.swapaxes(small_done[0, : 32 * lanes].reshape(lanes, 32, 128), 0, 1).reshape(32, width)
    return (section_ends, sums[:18].reshape(conv_weight.shape), sums[18:20][None], sums[20:22][None], sums[22:24][None],
            grad_qkv, grad_proj, sums[24:25], grad_fc1, sums[25:29].reshape(b_fc1.shape), grad_fc2, sums[29:30])


def solution(mesh):
    return jax.shard_map(
        on_device,
        mesh=mesh,
        in_specs=(
            P("pipe", "dp", None, None),
            P("pipe", None, None, None),
            P("pipe", None, None),
            P("pipe", None, None),
            P("pipe", None, None),
            P("pipe", None, None),
            P("pipe", None, None),
            P("pipe", None),
            P("pipe", None, None),
            P("pipe", None),
            P("pipe", None, None),
            P("pipe", None),
        ),
        out_specs=(
            P("pipe", "dp", None, None),
            P("pipe", None, None, None),
            P("pipe", None, None),
            P("pipe", None, None),
            P("pipe", None, None),
            P("pipe", None, None),
            P("pipe", None, None),
            P("pipe", None),
            P("pipe", None, None),
            P("pipe", None),
            P("pipe", None, None),
            P("pipe", None),
        ),
        check_vma=False,
    )
```

time: 507 us -> 377 us (0.74)
  waiting for transfers between devices: 109 us -> 2.03 us
  Pallas kernels: 373 us -> 357 us
    ppermute x2 -> x1, waiting for transfers between devices: 109 us -> 2.03 us  [shifted(): return lax.ppermute(x, axis, pairs)]
    pallas_call x3 -> x1, Pallas kernels: 295 us -> 286 us  [backward(): pl.pallas_call(functools.partial(back_kernel, images, dims, rows, lags, e...]
    pallas_call x2, Pallas kernels: 53.6 us -> 46.5 us  [forward_block(): pl.pallas_call(functools.partial(forward_kernel, images), out_shape=[jax....]
  transfers between devices with their start and end apart: 2 -> 1, of which waited for: 2 -> 1; matrix products, arithmetic and copies ran while one was open for 0% -> 0% of each run, Pallas kernels for 0% -> 0%
where the time goes in v3:
time: 377 us; the launch traced here: 376 us
  Pallas kernels  357 us (95%)
  other arithmetic  8.86 us (2%)
  local copies, waits for them, and re-layouts  6.19 us (2%)
    pallas_call x1, Pallas kernels, backward(): pl.pallas_call(functools.partial(back_kernel, images, dims, rows, lags, e...  286 us
    pallas_call x2, Pallas kernels, forward_block(): pl.pallas_call(functools.partial(forward_kernel, images), out_shape=[jax....  46.5 us
    pallas_call x4, Pallas kernels, from_chunks(): pl.pallas_call(widen, grid=(rows // SIDE, across), in_specs=[pl.BlockSpec...  24 us
  transfers between devices with their start and end apart: 1, of which 1 were waited for; matrix products, arithmetic and copies ran while one was open for 0% of the time, Pallas kernels for 0%

profile of v3, /device:TPU:0, one launch (start us, length us, event | category | flops | bytes accessed | tf_op | source)
XLA Modules:
  0.0 376.0 jit_solution(3642208063824612810)
XLA Ops:
  0.6 0.6 pad_add_fusion.role
  1.2 1.5 copy.53
  2.7 44.7 %shard_map.211 = (f32[784,768]{1,0:T(8,128)}, f32[784,768]{1,0:T(8,128)}, f32[784,768]{1,0:T(8,128)}, f32[784,768]{1,0:T(8,128)}, bf16[784,768]{1,0:T(8,128)(2,1...) custom-call(s32[2]{0:T(128)} %pad_add_fusion.role, ...), custom_call_target="tpu_custom_call" | custom-call | tf_op jit(solution)/shard_map/pallas_call | solution.py:258
  47.4 0.0 copy-start.1
  47.4 2.9 convert_element_type.2
  50.4 1.4 collective-permute-start
  51.7 0.6 pad_add_fusion.1.role
  52.3 2.0 collective-permute-done.x
  54.3 0.0 copy-done.1
  54.3 0.0 copy-start.2
  54.3 1.4 broadcast_select_fusion.1.x
  55.7 0.1 copy-done.2
  55.8 1.8 shard_map.212
  57.5 286.4 %shard_map.213 = (f32[784,768]{1,0:T(8,128)}, bf16[40,768,384]{2,1,0:T(8,128)(2,1)}, f32[1,256,128]{2,1,0:T(8,128)}, bf16[784,2304]{1,0:T(8,128)(2,1)}, bf16[784...) custom-call(bf16[784,768]{1,0:T(8,128)(2,1)} %bitcast.49, ...), custom_call_target="tpu_custom_call" | custom-call | tf_op jit(solution)/shard_map/pallas_call | solution.py:961
  343.9 0.9 slice.35
  344.8 0.1 copy.52
  344.9 2.6 shard_map.215
  347.5 6.0 %shard_map.214 = f32[768,2304]{1,0:T(8,128)} custom-call(bf16[40,768,384]{2,1,0:T(8,128)(2,1)} %get-tuple-element.61.src), custom_call_target="tpu_custom_call" | custom-call | tf_op jit(solution)/shard_map/pallas_call | solution.py:996
  353.5 7.6 %shard_map.217 = f32[3072,768]{1,0:T(8,128)} custom-call(bf16[40,768,384]{2,1,0:T(8,128)(2,1)} %get-tuple-element.61.src), custom_call_target="tpu_custom_call" | custom-call | tf_op jit(solution)/shard_map/pallas_call | solution.py:996
  361.1 0.0 copy-start
  361.1 7.8 %shard_map.216 = f32[768,3072]{1,0:T(8,128)} custom-call(bf16[40,768,384]{2,1,0:T(8,128)(2,1)} %get-tuple-element.61.src), custom_call_target="tpu_custom_call" | custom-call | tf_op jit(solution)/shard_map/pallas_call | solution.py:996
  368.9 0.6 reshape.52
  369.5 0.6 broadcast_in_dim.27
  370.1 0.6 broadcast_in_dim.26
  370.7 0.6 broadcast_in_dim.25
  371.3 0.7 copy.45
  372.0 0.0 copy-done
  372.0 3.4 broadcast_select_fusion
  375.4 0.6 copy_bitcast_fusion.2
  (5 shorter events, 0.0 us)
Async XLA Ops:
  47.4 6.9 %copy-start.1 = (bf16[1,16,49,768]{3,1,2,0:T(8,128)(2,1)S(1)}, bf16[1,16,49,768]{3,1,2,0:T(8,128)(2,1)}, u32[]{:S(2)}) copy-start(bf16[1,16,49,768]{3,1,2,0:T(8,128)(2,1)} %param.12) | copy-start | bytes 3612676
  50.4 4.0 %collective-permute-start = (bf16[784,768]{1,0:T(8,128)(2,1)}, bf16[784,768]{1,0:T(8,128)(2,1)S(1)}, u32[]{:S(2)}, u32[]{:S(2)}) collective-permute-start(bf16[784,768]{1,0:T(8,128)(2,1)} %convert_element_type.2), channel_id=1, source_target_pairs={{0,16},{1,17},{2,18},{3,19},{4,20},{5,21},{6,22},{7,23},{8,24},{9,... | collective-permute-start | bytes 3612680 | tf_op jit(solution)/shard_map/ppermute | solution.py:985
  54.3 1.4 copy-start.2
  361.1 10.9 %copy-start = (f32[784,768]{1,0:T(8,128)S(1)}, f32[784,768]{1,0:T(8,128)}, u32[]{:S(2)}) copy-start(f32[784,768]{1,0:T(8,128)} %get-tuple-element.59) | copy-start | bytes 7225348

commit v4 on v3

v4 whole, which is shorter than its diff:
```python
import functools

import jax
import jax.numpy as jnp
from jax import lax
from jax.experimental import pallas as pl
from jax.experimental.pallas import tpu as pltpu
from jax.sharding import PartitionSpec as P

MESH = pl.DeviceIdType.MESH
SIDE = 768


HEAD = 32
GROUP = 256
SLOT = 64
BF = jnp.bfloat16
F32 = jnp.float32


def cols(j, width=GROUP):
    return pl.ds(pl.multiple_of(j * width, width), width)


def dot(a, b):
    return lax.dot_general(a, b, (((1,), (0,)), ((), ())), preferred_element_type=F32)


def dot_t(a, b):
    return lax.dot_general(a, b, (((1,), (1,)), ((), ())), preferred_element_type=F32)


def t_dot(a, b):
    return lax.dot_general(a, b, (((0,), (0,)), ((), ())), preferred_element_type=F32)


def fill_swap(ref, images):
    rows, columns = ref.shape
    block = 128

    @pl.loop(0, rows // block)
    def _(b):
        r = lax.broadcasted_iota(jnp.int32, (block, columns), 0) + b * block
        c = lax.broadcasted_iota(jnp.int32, (block, columns), 1)
        image, position = lax.div(r, SLOT), lax.rem(r, SLOT)
        hit = (c == position * images + image) & (position < 49)
        ref[pl.ds(pl.multiple_of(b * block, block), block), :] = jnp.where(hit, 1.0, 0.0).astype(BF)


def clear_border(pad, images):
    zero = jnp.zeros((9 * images, pad.shape[1]), pad.dtype)
    pad[0 : 9 * images, :] = zero
    pad[72 * images : 81 * images, :] = zero
    one = jnp.zeros((images, pad.shape[1]), pad.dtype)

    @pl.loop(1, 8)
    def _(r):
        pad[pl.ds(pl.multiple_of(r * 9 * images, 8), images), :] = one
        pad[pl.ds(pl.multiple_of((r * 9 + 8) * images, 8), images), :] = one


def head_mask(rows_per, count, lanes):
    shape = (count * rows_per, lanes)
    r = lax.broadcasted_iota(jnp.int32, shape, 0)
    c = lax.broadcasted_iota(jnp.int32, shape, 1)
    return lax.div(r, rows_per) == lax.div(c, HEAD)


def spread_heads(x, mask):
    count = mask.shape[0] // x.shape[0]
    return jnp.where(mask, jnp.concatenate([x] * count, axis=0), jnp.zeros((), x.dtype))


def fold_heads(x, mask, rows_per):
    kept = jnp.where(mask, x, 0.0)
    total = kept[0:rows_per]
    for h in range(1, x.shape[0] // rows_per):
        total = total + kept[h * rows_per : (h + 1) * rows_per]
    return total


def soft_down(scores, valid):
    if valid < scores.shape[0]:
        r = lax.broadcasted_iota(jnp.int32, scores.shape, 0)
        scores = jnp.where(r < valid, scores, -jnp.inf)
    e = jnp.exp(scores - jnp.max(scores, axis=0, keepdims=True))
    return e / jnp.sum(e, axis=0, keepdims=True)


def gelu_both(x):
    half = 0.5 + 0.5 * lax.erf(x * 0.7071067811865476)
    return x * half, half + x * (0.3989422804014327 * jnp.exp(-0.5 * x * x))


def dp_dims(n):
    sizes = [1, 1, 1]
    at = 0
    left = n
    while left > 1:
        factor = 2 if left % 2 == 0 else left
        sizes[at % 3] *= factor
        left //= factor
        at += 1
    return tuple(sizes), (sizes[1] * sizes[2], sizes[2], 1)


class Place:
    def __init__(self, dp, size, stride):
        self.size = size
        pos = lax.rem(lax.div(dp, stride), size)
        low = pos < (size + 1) // 2
        self.outer = jnp.where(low, pos, size - 1 - pos)
        self.pos = pos
        self.low = low
        step = jnp.where(low, stride, -stride)
        self.inner_peer = dp + step
        self.outer_peer = dp - step


def pick(flag, a, b):
    out = object.__new__(Place)
    out.size = a.size
    for name in ("pos", "low", "outer", "inner_peer", "outer_peer"):
        setattr(out, name, jnp.where(flag, getattr(a, name), getattr(b, name)))
    return out


class Ring:
    def __init__(self, dp, dims, rows, grad, land, out, out_at, send, recv, local):
        (s0, s1, s2), (t0, t1, t2) = dims
        self.mids = Place(dp, s0, t0)
        self.fast, self.slow = Place(dp, s2, t2), Place(dp, s1, t1)
        self.grad, self.land, self.out, self.out_at = grad, land, out, out_at
        self.grads, self.lands = grad.shape[0], land.shape[0]
        self.send, self.recv, self.local = send, recv, local
        self.sizes, self.lens, self.starts, _ = Ring.shape(rows, dims)

    @staticmethod
    def shape(rows, dims):
        s0, s1, s2 = dims[0]
        sizes = (s2, s0, s1)
        lens = (rows // s2, rows // s2 // s0, rows // (s0 * s1 * s2))
        total, starts = 0, []
        for n, length in zip(sizes, lens):
            starts.append(total)
            total += length * (1 if n == 2 else 5)
        return sizes, lens, starts, total

    def level(self, c, i):
        flag = lax.rem(c + lax.axis_index("pipe"), 2) == 0
        if i == 1:
            return self.mids
        return pick(flag, self.fast, self.slow) if i == 0 else pick(flag, self.slow, self.fast)

    def base(self, c, i):
        start = 0
        for j in range(i):
            start = start + self.level(c, j).pos * self.lens[j]
        return start

    def span(self, c, i, a, b):
        place, length, n = self.level(c, i), self.lens[i], self.sizes[i]
        start = self.base(c, i) + jnp.where(place.low, a * length, (n - b) * length)
        return pl.ds(pl.multiple_of(start, 8), (b - a) * length)

    def mine(self, c, rows):
        return self.grad.at[lax.rem(c, self.grads), rows]

    def landing(self, c, i, at, length):
        return self.land.at[lax.rem(c, self.lands), pl.ds(self.starts[i] + at, length)]

    def copy(self, c, ev, src, dst, peer):
        return pltpu.make_async_remote_copy(
            src_ref=src, dst_ref=dst, send_sem=self.send.at[c, ev], recv_sem=self.recv.at[c, ev],
            device_id={"dp": peer}, device_id_type=MESH)

    def add(self, c, i, a, b, at):
        rows = self.span(c, i, a, b)
        slot = lax.rem(c, self.grads)
        got = self.landing(c, i, at, (b - a) * self.lens[i])
        self.grad[slot, rows] = self.grad[slot, rows] + got[...]

    def give(self, c, i, ev, a, b, at, peer):
        return self.copy(c, ev, self.mine(c, self.span(c, i, a, b)), self.landing(c, i, at, (b - a) * self.lens[i]), peer)

    def reduce_stages(self, i):
        n, length = self.sizes[i], self.lens[i]
        ein, eout = 2 * i, 2 * i + 1
        if n == 1:
            return []
        if n == 2:
            def first(c):
                self.give(c, i, eout, 1, 2, 0, self.level(c, i).inner_peer).start()

            def last(c):
                self.give(c, i, eout, 0, 1, 0, self.level(c, i).inner_peer).wait_recv()
                self.add(c, i, 0, 1, 0)
            return [first, last]

        def zero(c):
            place = self.level(c, i)

            @pl.when(place.outer == 0)
            def _():
                self.give(c, i, ein, 1, 4, 0, place.inner_peer).start()

        def one(c):
            place = self.level(c, i)

            @pl.when(place.outer == 1)
            def _():
                self.give(c, i, ein, 1, 4, 0, place.inner_peer).wait_recv()
                self.add(c, i, 2, 4, jnp.where(place.low, length, 0))
                self.give(c, i, eout, 2, 4, 3 * length, place.inner_peer).start()
                self.add(c, i, 1, 2, jnp.where(place.low, 0, 2 * length))

        def two(c):
            place = self.level(c, i)

            @pl.when(place.outer == 1)
            def _():
                self.give(c, i, eout, 0, 2, 3 * length, place.inner_peer).wait_recv()
                self.add(c, i, 0, 2, 3 * length)
                self.give(c, i, ein, 0, 1, 3 * length, place.outer_peer).start()

        def three(c):
            place = self.level(c, i)

            @pl.when(place.outer == 0)
            def _():
                self.give(c, i, ein, 0, 1, 3 * length, place.inner_peer).wait_recv()
                self.add(c, i, 0, 1, 3 * length)
        return [zero, one, two, three]

    def reduce_ends(self, c):
        for i in range(3):
            n, place = self.sizes[i], self.level(c, i)
            ein, eout = 2 * i, 2 * i + 1
            if n == 2:
                self.give(c, i, eout, 1, 2, 0, place.inner_peer).wait_send()
            elif n == 4:
                @pl.when(place.outer == 0)
                def _():
                    self.give(c, i, ein, 1, 4, 0, place.inner_peer).wait_send()

                @pl.when(place.outer == 1)
                def _():
                    self.give(c, i, eout, 2, 4, 0, place.inner_peer).wait_send()
                    self.give(c, i, ein, 0, 1, 0, place.outer_peer).wait_send()

    def spread(self, c, i, ev, a, b, peer):
        dst = self.out.at[self.out_at(c), self.span(c, i, a, b)]
        return self.copy(c, ev, dst, dst, peer)

    def gather_stages(self, i):
        n = self.sizes[i]
        ein, eout = 6 + 2 * i, 7 + 2 * i
        if n == 1:
            return []
        if n == 2:
            def first(c):
                self.spread(c, i, eout, 0, 1, self.level(c, i).inner_peer).start()

            def last(c):
                self.spread(c, i, eout, 1, 2, self.level(c, i).inner_peer).wait_recv()
            return [first, last]

        def zero(c):
            place = self.level(c, i)

            @pl.when(place.outer == 0)
            def _():
                self.spread(c, i, ein, 0, 1, place.inner_peer).start()

        def one(c):
            place = self.level(c, i)

            @pl.when(place.outer == 1)
            def _():
                self.spread(c, i, ein, 0, 1, place.outer_peer).wait_recv()
                self.spread(c, i, eout, 0, 2, place.inner_peer).start()

        def two(c):
            place = self.level(c, i)

            @pl.when(place.outer == 1)
            def _():
                self.spread(c, i, eout, 2, 4, place.inner_peer).wait_recv()
                self.spread(c, i, ein, 1, 4, place.outer_peer).start()

        def three(c):
            place = self.level(c, i)

            @pl.when(place.outer == 0)
            def _():
                self.spread(c, i, ein, 1, 4, place.inner_peer).wait_recv()
        return [zero, one, two, three]

    def gather_ends(self, c):
        for i in range(3):
            n, place = self.sizes[i], self.level(c, i)
            ein, eout = 6 + 2 * i, 7 + 2 * i
            if n == 2:
                self.spread(c, i, eout, 0, 1, place.inner_peer).wait_send()
            elif n == 4:
                @pl.when(place.outer == 0)
                def _():
                    self.spread(c, i, ein, 0, 1, place.inner_peer).wait_send()

                @pl.when(place.outer == 1)
                def _():
                    self.spread(c, i, eout, 0, 2, place.inner_peer).wait_send()
                    self.spread(c, i, ein, 1, 4, place.outer_peer).wait_send()

    def settle(self, c):
        rows = pl.ds(pl.multiple_of(self.base(c, 3), 8), self.lens[2])
        copy = pltpu.make_async_copy(self.mine(c, rows), self.out.at[self.out_at(c), rows], self.local)
        copy.start()
        copy.wait()

    def stages(self, first, second, last):
        groups = [self.reduce_stages(0), self.reduce_stages(1), self.reduce_stages(2), [self.settle],
                  self.gather_stages(2), self.gather_stages(1), self.gather_stages(0), [last]]
        joined = [[first], [second]]
        for group in groups:
            if group:
                joined[-1].append(group[0])
                joined += [[stage] for stage in group[1:]]
        return [functools.partial(run_all, stages) for stages in joined]

    def greet(self):
        barrier = pltpu.get_barrier_semaphore()
        pl.semaphore_signal(barrier, inc=1, device_id={"pipe": 1 - lax.axis_index("pipe")}, device_id_type=MESH)
        count = jnp.int32(1)
        for place in (self.fast, self.mids, self.slow):
            if place.size == 1:
                continue
            pl.semaphore_signal(barrier, inc=1, device_id={"dp": place.inner_peer}, device_id_type=MESH)
            count = count + 1
            if place.size == 4:
                @pl.when(place.outer == 1)
                def _():
                    pl.semaphore_signal(barrier, inc=1, device_id={"dp": place.outer_peer}, device_id_type=MESH)
                count = count + jnp.where(place.outer == 1, 1, 0)
        pl.semaphore_wait(barrier, count)


def run_all(stages, c):
    for stage in stages:
        stage(c)


def spatial_forward(packed, mixed, soft, images):
    width = mixed.shape[1]

    @pl.loop(0, images, unroll=4)
    def _(i):
        rows = pl.ds(pl.multiple_of(i * SLOT, SLOT), SLOT)
        mask = head_mask(SLOT, GROUP // HEAD, GROUP)
        for g in range(width // GROUP):
            q, k, v = (packed[rows, part * width + g * GROUP : part * width + (g + 1) * GROUP] for part in range(3))
            weights = soft_down(dot_t(k, spread_heads(q, mask)), 49).astype(BF)
            soft[i, g] = weights
            mixed[rows, g * GROUP : (g + 1) * GROUP] = fold_heads(t_dot(weights, v), mask, SLOT).astype(BF)


def channel_forward(packed, mixed, soft, images):
    width = mixed.shape[1]

    @pl.loop(0, images, unroll=4)
    def _(i):
        rows = pl.ds(pl.multiple_of(i * SLOT, SLOT), SLOT)
        mask = head_mask(HEAD, 128 // HEAD, 128)
        for g in range(width // 128):
            q, k, v = (packed[rows, part * width + g * 128 : part * width + (g + 1) * 128] for part in range(3))
            weights = soft_down(fold_heads(t_dot(k, q), mask, HEAD), HEAD).astype(BF)
            soft[i, g // 2, g % 2 * HEAD : (g % 2 + 1) * HEAD, 0:128] = weights
            mixed[rows, g * 128 : (g + 1) * 128] = dot(v, spread_heads(weights, mask)).astype(BF)


def spatial_backward(packed, grad_mixed, soft, start, stop):
    width = grad_mixed.shape[1]

    @pl.loop(start, stop)
    def _(i):
        rows = pl.ds(pl.multiple_of(i * SLOT, SLOT), SLOT)
        mask = head_mask(SLOT, GROUP // HEAD, GROUP)
        made = []
        for g in range(width // GROUP):
            at = [slice(part * width + g * GROUP, part * width + (g + 1) * GROUP) for part in range(3)]
            made.append((at, [packed[rows, a] for a in at], soft[i, g], grad_mixed[rows, g * GROUP : (g + 1) * GROUP]))
        ready = []
        for at, (q, k, v), weights, do in made:
            out_spread = spread_heads(do, mask)
            w = weights.astype(F32)
            dw = dot_t(v, out_spread)
            ds = (w * (dw - jnp.sum(dw * w, axis=0, keepdims=True))).astype(BF)
            dq = (fold_heads(t_dot(ds, k), mask, SLOT) * HEAD ** -0.5).astype(BF)
            ready += zip(at, (dq, dot(ds, spread_heads(q, mask)).astype(BF), dot(weights, out_spread).astype(BF)))
        for at, value in ready:
            packed[rows, at] = value


def channel_backward(packed, grad_mixed, soft, start, stop):
    width = grad_mixed.shape[1]

    @pl.loop(start, stop)
    def _(i):
        rows = pl.ds(pl.multiple_of(i * SLOT, SLOT), SLOT)
        mask = head_mask(HEAD, 128 // HEAD, 128)
        made = []
        for g in range(width // 128):
            at = [slice(part * width + g * 128, part * width + (g + 1) * 128) for part in range(3)]
            weights = soft[i, g // 2, g % 2 * HEAD : (g % 2 + 1) * HEAD, 0:128]
            made.append((at, [packed[rows, a] for a in at], weights, grad_mixed[rows, g * 128 : (g + 1) * 128]))
        ready = []
        for at, (q, k, v), weights, do in made:
            w = weights.astype(F32)
            dw = fold_heads(t_dot(v, do), mask, HEAD)
            ds = spread_heads((w * (dw - jnp.sum(dw * w, axis=0, keepdims=True))).astype(BF), mask)
            dq = (dot(k, ds) * HEAD ** -0.5).astype(BF)
            ready += zip(at, (dq, dot_t(q, ds).astype(BF), dot_t(do, spread_heads(weights, mask)).astype(BF)))
        for at, value in ready:
            packed[rows, at] = value


def encode(pad, kernel, bias, out, images):
    @pl.loop(0, pad.shape[1] // 128)
    def _(lane):
        ls = cols(lane, 128)
        taps = [jnp.broadcast_to(kernel(t, ls), (images, 128)) for t in range(9)]
        shift = jnp.broadcast_to(bias(ls), (images, 128))

        @pl.loop(0, 7, unroll=7)
        def _(r):
            for c in range(7):
                total = shift
                for t in range(9):
                    at = pl.multiple_of(((r + t // 3) * 9 + c + t % 3) * images, 8)
                    piece = pad[pl.ds(at, images), ls]
                    total = total + piece * taps[t]
                    if t == 4:
                        total = total + piece
                out[pl.ds(pl.multiple_of((r * 7 + c) * images, 8), images), ls] = total


def normalise(stream, gain, bias, out):
    @pl.loop(0, stream.shape[0] // 16, unroll=5)
    def _(p):
        rows = pl.ds(pl.multiple_of(p * 16, 16), 16)
        s = stream[rows, :]
        centered = s - jnp.mean(s, axis=-1, keepdims=True)
        spread = jnp.mean(centered * centered, axis=-1, keepdims=True)
        out[rows, :] = (centered * lax.rsqrt(spread + 1e-5) * gain + bias).astype(BF)


def encode_back(gpad, given, kernel, out, put, first_row, bias_row, images):
    @pl.loop(0, gpad.shape[1] // 128)
    def _(lane):
        ls = cols(lane, 128)
        taps = [jnp.broadcast_to(kernel(8 - t, ls), (images, 128)) for t in range(9)]

        def row(r, totals):
            totals = list(totals)
            for c in range(7):
                at = pl.ds(pl.multiple_of((r * 7 + c) * images, 8), images)
                source = given[at, ls]
                total = None
                for t in range(9):
                    near = pl.ds(pl.multiple_of(((r + t // 3) * 9 + c + t % 3) * images, 8), images)
                    piece = gpad[near, ls]
                    if t == 4:
                        totals[9] = totals[9] + piece
                        total = total + piece
                    total = piece * taps[t] if total is None else total + piece * taps[t]
                    totals[8 - t] = totals[8 - t] + source * piece
                out[at, ls] = total
            return tuple(totals)
        totals = lax.fori_loop(0, 7, row, (jnp.zeros((images, 128), F32),) * 10, unroll=True)
        for t in range(9):
            put(first_row + t, lane, jnp.sum(totals[t], axis=0, keepdims=True))
        put(bias_row, lane, jnp.sum(totals[9], axis=0, keepdims=True))


def normalise_back(stream, grad, base, gain, gpad, put, gain_row, shift_row, acc, images):
    acc[...] = jnp.zeros_like(acc)

    @pl.loop(0, 49, unroll=7)
    def _(p):
        rows = pl.ds(pl.multiple_of(p * images, 8), images)
        s, dy = stream[rows, :], grad[rows, :]
        centered = s - jnp.mean(s, axis=-1, keepdims=True)
        rate = lax.rsqrt(jnp.mean(centered * centered, axis=-1, keepdims=True) + 1e-5)
        unit = centered * rate
        acc[0] += dy * unit
        acc[1] += dy
        dg = dy * gain
        m1 = jnp.mean(dg, axis=-1, keepdims=True)
        m2 = jnp.mean(dg * unit, axis=-1, keepdims=True)
        at = ((lax.div(p, 7) + 1) * 9 + lax.rem(p, 7) + 1) * images
        gpad[pl.ds(pl.multiple_of(at, 8), images), :] = base[rows, :] + rate * (dg - m1 - unit * m2)
    for row, total in ((gain_row, acc[0]), (shift_row, acc[1])):
        total = jnp.sum(total, axis=0, keepdims=True)
        for lane in range(total.shape[1] // 128):
            put(row, lane, total[:, lane * 128 : (lane + 1) * 128])


def fill_pad(pad, source, images):
    @pl.loop(0, 7)
    def _(r):
        inner = pl.ds(pl.multiple_of(((r + 1) * 9 + 1) * images, 8), 7 * images)
        pad[inner, :] = source[pl.ds(pl.multiple_of(r * 7 * images, 8), 7 * images), :]


CONV, CONV_BIAS, GAIN, SHIFT, B_PROJ, B_FC1, B_FC2 = 0, 18, 20, 22, 24, 25, 29
HIDDEN, COT, N2, PRE, MIXED, ATT, N1, PACKED = 0, 4, 5, 6, 10, 11, 12, 13
SEGMENTS = 12


def section_kernel(images, dims, rows, lags, chunk,
                   halves, conv_w, conv_b, gain, shift, b_proj, b_fc1, b_fc2, w_qkv, w_proj, w_fc1, w_fc2,
                   ends, out, small_out, acts, k_one, k_mid, k_two, k_packed, k_soft, k_slope, x_qkv, x_proj, x_fc1, x_fc2,
                   v_qkv, v_proj, v_fc1, v_fc2, params, xb, cot, pad, one, stream, gmid, gn, packed, soft, slope, hidden,
                   swap, gm_s, n1, n2, mixed, gatt, acc, small_grad, small_pair,
                   grad, land, pair_out, pair_in, small_land, left_buf, right_buf,
                   load, store, push_send, push_recv, fetch_sem, pair_send, pair_recv, send, recv, local, ssend, srecv, slocal,
                   bring_send, bring_recv):
    pipe, dp = lax.axis_index("pipe"), lax.axis_index("dp")
    other = 1 - pipe
    first = pipe == 0
    tokens, width = gn.shape
    wide = v_fc1.shape[1]
    real = 49 * images
    per = SIDE // (2 * chunk)
    block_pairs = SEGMENTS * per
    pairs = 2 * block_pairs
    weights = ((w_qkv, x_qkv, v_qkv), (w_proj, x_proj, v_proj), (w_fc1, x_fc1, v_fc1), (w_fc2, x_fc2, v_fc2))
    QKV, PROJ, FC1, FC2 = range(4)

    def to_core(at, src, dst):
        return pltpu.make_async_remote_copy(src_ref=src, dst_ref=dst, send_sem=push_send.at[at], recv_sem=push_recv.at[at],
                                            device_id={"pipe": other}, device_id_type=MESH)
    push_params = to_core(0, params.at[pipe], params.at[pipe])
    push_x = to_core(1, halves.at[1], xb.at[0])
    push_cot = to_core(1, halves.at[0], cot)
    push_weights = [to_core(2 + at, own, far) for at, (own, far, _) in enumerate(weights)]
    lanes = [pl.ds(lane * 128, 128) for lane in range(width // 128)]
    push_result = [to_core(8 + at, gn.at[:, ls], ends.at[0, at]) for at, ls in enumerate(lanes)]
    push_grad = [to_core(8 + at, gmid.at[:, ls], ends.at[1, at]) for at, ls in enumerate(lanes)]

    def load_weight(b, at, fresh):
        own, far, near = weights[at]

        @pl.when(b == pipe)
        def _():
            pltpu.make_async_copy(own, near, load.at[at]).start()

        @pl.when(b != pipe)
        def _():
            if fresh:
                push_weights[at].wait_recv()
            pltpu.make_async_copy(far, near, load.at[at]).start()

    def wait_weight(at):
        own, _, near = weights[at]
        pltpu.make_async_copy(own, near, load.at[at]).wait()

    def keep(at, src, dst):
        return pltpu.make_async_copy(src, dst, store.at[at])

    def block_stores(b):
        return [keep(0, one, k_one.at[b]), keep(1, gmid, k_mid.at[b]), keep(2, stream, k_two.at[b]), keep(3, packed, k_packed.at[b]),
                keep(4, soft, k_soft.at[b]), keep(5, slope, k_slope.at[b]), keep(6, n1, acts.at[b, N1]), keep(7, mixed, acts.at[b, MIXED]),
                keep(8, n2, acts.at[b, N2])] + [
                    keep(9 + s, hidden.at[:, pl.ds(s * SIDE, SIDE)], acts.at[b, HIDDEN + s]) for s in range(wide // SIDE)]

    def row_of(b, row):
        return params[b, row : row + 1, :]

    def taps_of(b, j):
        return (lambda t, ls: params[b, pl.ds(CONV + 9 * j + t, 1), ls]), (lambda ls: params[b, pl.ds(CONV_BIAS + j, 1), ls])

    def block_of(k):
        return jnp.where(k < block_pairs, 1, 0)

    def number_of(k, core):
        return 2 * lax.rem(k, block_pairs) + core

    def out_at(k):
        return jnp.where(block_of(k) == pipe, number_of(k, pipe), 2 * block_pairs + lax.rem(k, block_pairs))

    main = Ring(dp, dims, rows, grad, land, out, out_at, send, recv, local)
    small = Ring(dp, dims, small_grad.shape[1], small_pair, small_land, small_out, lambda c: 0, ssend, srecv, slocal)

    def slots_of(k):
        at = lax.div(lax.rem(k, block_pairs), per)
        left = jnp.where(at < 4, HIDDEN + at, jnp.where(at < 8, N2, jnp.where(at < 9, MIXED, N1)))
        right = jnp.where(at < 4, COT, jnp.where(at < 8, PRE + at - 4, jnp.where(at < 9, ATT, PACKED + at - 9)))
        return left, right, lax.rem(lax.rem(k, block_pairs), per)

    def fetches(k):
        left, right, part = slots_of(k)
        slot, b = lax.rem(k, 2), block_of(k)
        return (pltpu.make_async_copy(acts.at[b, left], left_buf.at[slot], fetch_sem.at[slot, 0]),
                pltpu.make_async_copy(acts.at[b, right, :, cols(part, 2 * chunk)], right_buf.at[slot], fetch_sem.at[slot, 1]))

    def pair_copy(k):
        return pltpu.make_async_remote_copy(
            src_ref=pair_out.at[lax.rem(k, pair_out.shape[0])], dst_ref=pair_in.at[lax.rem(k, pair_in.shape[0])],
            send_sem=pair_send.at[k], recv_sem=pair_recv.at[k], device_id={"pipe": other}, device_id_type=MESH)

    def make(k):
        for copy in fetches(k):
            copy.wait()

        @pl.when(k >= pair_out.shape[0])
        def _():
            pair_copy(k - pair_out.shape[0]).wait_send()

        @pl.when(k >= main.grads)
        def _():
            main.reduce_ends(k - main.grads)
        slot, place, far = lax.rem(k, 2), lax.rem(k, main.grads), lax.rem(k, pair_out.shape[0])
        both = t_dot(left_buf[slot], right_buf[slot]).astype(BF)

        @pl.when(first)
        def _():
            grad[place, 0:SIDE] = both[:, :chunk]
            pair_out[far] = both[:, chunk:]

        @pl.when(jnp.logical_not(first))
        def _():
            pair_out[far] = both[:, :chunk]
            grad[place, 0:SIDE] = both[:, chunk:]
        pair_copy(k).start()
        if rows > SIDE:
            grad[place, SIDE:rows] = jnp.zeros((rows - SIDE, chunk), BF)

    def join(k):
        pair_copy(k).wait_recv()
        place = lax.rem(k, main.grads)
        grad[place, 0:SIDE] = grad[place, 0:SIDE] + pair_in[lax.rem(k, pair_in.shape[0])]

    def bring(k):
        number = number_of(k, pipe)
        at = lax.rem(k, block_pairs)
        return pltpu.make_async_remote_copy(
            src_ref=out.at[out_at(k)], dst_ref=out.at[number], send_sem=bring_send.at[at], recv_sem=bring_recv.at[at],
            device_id={"pipe": other}, device_id_type=MESH)

    def hand_over(k):
        @pl.when(block_of(k) != pipe)
        def _():
            bring(k).start()
    small_copy = to_core(7, small_grad.at[other], small_pair.at[1])

    def small_make(k):
        small_copy.start()
        small_pair[0] = small_grad[pipe]

    def small_join(k):
        small_copy.wait_recv()
        small_pair[0] = small_pair[0] + small_pair[1]

    def tick(t):
        stages = main.stages(make, join, hand_over)
        small_stages = small.stages(small_make, small_join, lambda k: None)
        for s in reversed(range(len(stages))):
            k = t - lags[s]

            @pl.when((k >= 0) & (k < pairs))
            def _():
                stages[s](k)

            @pl.when(k == pairs)
            def _():
                small_stages[s](0)

    main.greet()
    for j in range(2):
        params[pipe, CONV + 9 * j : CONV + 9 * (j + 1), :] = conv_w[j]
    for row, ref in ((CONV_BIAS, conv_b), (GAIN, gain), (SHIFT, shift), (B_PROJ, b_proj), (B_FC2, b_fc2)):
        params[pipe, row : row + ref.shape[0], :] = ref[...]
    for j in range(wide // width):
        params[pipe, B_FC1 + j : B_FC1 + j + 1, :] = b_fc1[:, j * width : (j + 1) * width]
    x_copy = pltpu.make_async_copy(halves.at[0], xb.at[0], load.at[5])
    cot_copy = pltpu.make_async_copy(halves.at[1], cot, load.at[5])
    push_params.start()

    @pl.when(first)
    def _():
        push_x.start()
        x_copy.start()

    @pl.when(jnp.logical_not(first))
    def _():
        push_cot.start()
        cot_copy.start()
    push_weights[QKV].start()
    fill_swap(swap, images)
    clear_border(pad, images)
    small_grad[...] = jnp.zeros_like(small_grad)
    one[real:tokens, :] = jnp.zeros((tokens - real, width), F32)
    stream[real:tokens, :] = jnp.zeros((tokens - real, width), F32)
    push_params.wait_recv()

    @pl.when(first)
    def _():
        x_copy.wait()

    @pl.when(jnp.logical_not(first))
    def _():
        push_x.wait_recv()

    @pl.loop(0, 2)
    def _(b):
        stores = block_stores(b)

        @pl.when(b > 0)
        def _():
            for copy in stores:
                copy.wait()
        load_weight(b, QKV, True)
        gn[...] = xb[b].astype(F32)
        fill_pad(pad, gn, images)
        kernel, bias = taps_of(b, 0)
        encode(pad, kernel, bias, one, images)
        stores[0].start()
        normalise(one, row_of(b, GAIN), row_of(b, SHIFT), n1)
        stores[6].start()

        @pl.when(b == 0)
        def _():
            push_weights[PROJ].start()
            push_weights[FC1].start()

        gm_s[...] = dot(swap[...], n1[...]).astype(BF)
        wait_weight(QKV)

        @pl.loop(0, 3)
        def _(j):
            scale = jnp.where(j == 0, HEAD ** -0.5, 1.0)
            packed[:, cols(j, width)] = (dot(gm_s[...], v_qkv[:, cols(j, width)]) * scale).astype(BF)
        stores[3].start()

        @pl.when(b == 0)
        def _():
            push_weights[FC2].start()
        load_weight(b, PROJ, True)

        @pl.when(b == 0)
        def _():
            spatial_forward(packed, gm_s, soft, images)

        @pl.when(b == 1)
        def _():
            channel_forward(packed, gm_s, soft, images)
        stores[4].start()
        load_weight(b, FC1, True)

        mixed[...] = t_dot(swap[...], gm_s[...]).astype(BF)
        stores[7].start()
        wait_weight(PROJ)

        gmid[...] = one[...] + dot(mixed[...], v_proj[...]) + row_of(b, B_PROJ)
        stores[1].start()
        fill_pad(pad, gmid, images)
        kernel, bias = taps_of(b, 1)
        encode(pad, kernel, bias, stream, images)
        stores[2].start()
        normalise(stream, row_of(b, GAIN + 1), row_of(b, SHIFT + 1), n2)
        stores[8].start()
        wait_weight(FC1)
        load_weight(b, FC2, True)

        @pl.loop(0, wide // width)
        def _(j):
            at = cols(j, width)
            value, rate = gelu_both(dot(n2[...], v_fc1[:, at]) + params[b, pl.ds(B_FC1 + j, 1), :])
            hidden[:, at] = value.astype(BF)
            slope[:, at] = rate.astype(BF)
        stores[5].start()
        for copy in stores[9:]:
            copy.start()
        wait_weight(FC2)

        gn[...] = stream[...] + dot(hidden[...], v_fc2[...]) + row_of(b, B_FC2)

        @pl.when(b == 0)
        def _():
            xb[1] = gn[...].astype(BF)

    end_copy = [pltpu.make_async_copy(gn.at[:, ls], ends.at[1, at], load.at[13 + at]) for at, ls in enumerate(lanes)]
    last_copy = [pltpu.make_async_copy(gmid.at[:, ls], ends.at[0, at], load.at[13 + at]) for at, ls in enumerate(lanes)]

    @pl.when(first)
    def _():
        for copy in push_result:
            copy.start()
        push_cot.wait_recv()

    @pl.when(jnp.logical_not(first))
    def _():
        for copy in end_copy:
            copy.start()
        cot_copy.wait()
    keep_cot = keep(13, cot, acts.at[1, COT])
    keep_cot.start()
    for copy in block_stores(1):
        copy.wait()
    keep_cot.wait()
    for copy in fetches(0):
        copy.start()

    def put(b):
        def at(row, lane, value):
            small_grad[b, pl.ds(lane * 32 + row, 1), :] = value
        return at

    loads = [pltpu.make_async_copy(k_slope.at[0], slope, load.at[7]), pltpu.make_async_copy(k_packed.at[0], packed, load.at[8]),
             pltpu.make_async_copy(k_soft.at[0], soft, load.at[9]), pltpu.make_async_copy(k_two.at[0], stream, load.at[10]),
             pltpu.make_async_copy(k_mid.at[0], gmid, load.at[11])]

    def later(b, at):
        @pl.when(b == 0)
        def _():
            loads[at].wait()

    def later_weight(b, at):
        @pl.when(b == 0)
        def _():
            wait_weight(at)

    def ahead(b, do):
        pl.when(b == 1)(do)

    def pre_part(part):
        def run(b):
            if part == 0:
                later(b, 0)
                later_weight(b, FC2)
                one[...] = cot[...].astype(F32)
            each = wide // 3
            at = slice(part * each, (part + 1) * each)
            pre = dot_t(cot[...], v_fc2[at, :]) * slope[:, at].astype(F32)
            slope[:, at] = pre.astype(BF)
            total = jnp.sum(pre, axis=0, keepdims=True)
            for piece in range(each // 128):
                lane = part * each // 128 + piece
                put(b)(B_FC1 + lane // (width // 128), lane % (width // 128), total[:, piece * 128 : (piece + 1) * 128])
            if part == 2:
                ahead(b, lambda: load_weight(0, FC2, False))
                copies = [keep(s, slope.at[:, pl.ds(s * SIDE, SIDE)], acts.at[b, PRE + s]) for s in range(wide // SIDE)]
                for copy in copies:
                    copy.start()
                for lane in range(width // 128):
                    put(b)(B_FC2, lane, jnp.sum(one[:, lane * 128 : (lane + 1) * 128], axis=0, keepdims=True))
                for copy in copies:
                    copy.wait()
        return run

    def through_fc1(b):
        @pl.when(b == 1)
        def _():
            @pl.when(first)
            def _():
                for copy in push_result:
                    copy.wait_send()

            @pl.when(jnp.logical_not(first))
            def _():
                for copy in end_copy:
                    copy.wait()
        later_weight(b, FC1)

        gn[...] = dot_t(slope[...], v_fc1[...])
        ahead(b, lambda: load_weight(0, FC1, False))

    def through_second(b):
        later(b, 3)
        normalise_back(stream, gn, one, row_of(b, GAIN + 1), pad, put(b), GAIN + 1, SHIFT + 1, acc, images)
        pltpu.make_async_copy(k_one.at[b], stream, load.at[12]).start()
        later(b, 4)
        encode_back(pad, gmid, taps_of(b, 1)[0], gmid, put(b), CONV + 9, CONV_BIAS + 1, images)
        gmid[real:tokens, :] = jnp.zeros((tokens - real, width), F32)
        for lane in range(width // 128):
            part = gmid[:, lane * 128 : (lane + 1) * 128]
            put(b)(B_PROJ, lane, jnp.sum(part, axis=0, keepdims=True))
            gatt[:, lane * 128 : (lane + 1) * 128] = part.astype(BF)
        keep(4, gatt, acts.at[b, ATT]).start()

    def through_proj(b):
        later_weight(b, PROJ)

        n2[...] = dot_t(gatt[...], v_proj[...]).astype(BF)
        ahead(b, lambda: load_weight(0, PROJ, False))
        gm_s[...] = dot(swap[...], n2[...]).astype(BF)
        later(b, 1)
        later(b, 2)

    def through_mix(part):
        def run(b):
            each = images // 2

            @pl.when(b == 0)
            def _():
                spatial_backward(packed, gm_s, soft, part * each, (part + 1) * each)

            @pl.when(b == 1)
            def _():
                channel_backward(packed, gm_s, soft, part * each, (part + 1) * each)
            if part == 1:
                keep(4, gatt, acts.at[b, ATT]).wait()
        return run

    def unswap(b):
        @pl.loop(0, 3)
        def _(j):
            slope[:, cols(j, width)] = t_dot(swap[...], packed[:, cols(j, width)]).astype(BF)
        copies = [keep(s, slope.at[:, pl.ds(s * SIDE, SIDE)], acts.at[b, PACKED + s]) for s in range(3)]
        for copy in copies:
            copy.start()
        for copy in copies:
            copy.wait()

    def through_qkv(b):
        later_weight(b, QKV)

        gn[...] = dot_t(slope[:, 0 : 3 * width], v_qkv[...])

        def prepare():
            load_weight(0, QKV, False)
            for at in range(3):
                loads[at].start()
        ahead(b, prepare)

    def through_first(b):
        pltpu.make_async_copy(k_one.at[b], stream, load.at[12]).wait()
        normalise_back(stream, gn, gmid, row_of(b, GAIN), pad, put(b), GAIN, SHIFT, acc, images)
        ahead(b, lambda: loads[3].start())

    def finish(b):
        gn[...] = xb[b].astype(F32)
        encode_back(pad, gn, taps_of(b, 0)[0], gmid, put(b), CONV, CONV_BIAS, images)

        @pl.when(b == 1)
        def _():
            cot[...] = gmid[...].astype(BF)
            copy = keep(5, cot, acts.at[0, COT])
            copy.start()
            loads[4].start()
            copy.wait()

        @pl.when((b == 0) & first)
        def _():
            for copy in last_copy:
                copy.start()

        @pl.when((b == 0) & jnp.logical_not(first))
        def _():
            for copy in push_grad:
                copy.start()
    segments = [pre_part(0), pre_part(1), pre_part(2), through_fc1, through_second, through_proj, through_mix(0), through_mix(1),
                unswap, through_qkv, through_first, finish]

    @pl.loop(0, pairs + 1 + lags[-1])
    def _(t):
        tick(t)

        @pl.when((t < pairs) & (lax.rem(t, per) == 0))
        def _():
            b, at = block_of(t), lax.div(lax.rem(t, block_pairs), per)
            for number, segment in enumerate(segments):
                @pl.when(at == number)
                def _():
                    segment(b)

        @pl.when(t + 1 < pairs)
        def _():
            for copy in fetches(t + 1):
                copy.start()

    @pl.loop(pairs - main.grads, pairs)
    def _(k):
        main.reduce_ends(k)

    @pl.loop(pairs - pair_out.shape[0], pairs)
    def _(k):
        pair_copy(k).wait_send()

    @pl.loop(0, pairs)
    def _(k):
        main.gather_ends(k)

        @pl.when(block_of(k) != pipe)
        def _():
            bring(k).wait_send()
    small.reduce_ends(0)
    small.gather_ends(0)
    small_copy.wait_send()
    push_params.wait_send()
    for copy in push_weights:
        copy.wait_send()

    @pl.when(first)
    def _():
        push_x.wait_send()
        for copy in last_copy:
            copy.wait()
        for copy in push_grad:
            copy.wait_recv()

    @pl.when(jnp.logical_not(first))
    def _():
        push_cot.wait_send()
        for copy in push_grad:
            copy.wait_send()
        for copy in push_result:
            copy.wait_recv()

    @pl.loop(0, block_pairs)
    def _(at):
        number = 2 * at + other
        pltpu.make_async_remote_copy(
            src_ref=out.at[number], dst_ref=out.at[number], send_sem=bring_send.at[at], recv_sem=bring_recv.at[at],
            device_id={"pipe": other}, device_id_type=MESH).wait_recv()


def section(halves, small, weights, images, n, collective_id=0):
    w_qkv, w_proj, w_fc1, w_fc2 = weights
    _, tokens, width = halves.shape
    wide = w_fc1.shape[1]
    slots = images * SLOT
    dims = dp_dims(n)
    chunk = 384 if n <= 16 else 128
    total = (wide // SIDE * 2 + 4) * SIDE // chunk
    pairs = total
    rows = -(-SIDE // (16 * n)) * 16 * n
    small_rows = 16 * n
    _, _, _, land = Ring.shape(rows, dims)
    _, _, _, small_land = Ring.shape(small_rows, dims)
    hops = sum(0 if s == 1 else 1 if s == 2 else 3 for s in dims[0])
    gaps = [1, 2] + [1] * (2 * hops - 2) + [2]
    lags = [sum(gaps[:s]) for s in range(2 * hops + 2)]
    grads, lands = lags[hops + 1] + 3, 10
    any_space = pl.BlockSpec(memory_space=pl.ANY)
    vmem = pl.BlockSpec(memory_space=pltpu.VMEM)
    soft = (images, width // GROUP, SLOT, 2 * GROUP)
    outs = [((2, width // 128, tokens, 128), F32), ((total + total // 2, rows, chunk), BF), ((1, small_rows, 128), F32),
            ((2, 16, tokens, SIDE), BF), ((2, tokens, width), F32), ((2, tokens, width), F32), ((2, tokens, width), F32),
            ((2, slots, 3 * width), BF), ((2, *soft), BF), ((2, tokens, wide), BF),
            (w_qkv.shape, BF), (w_proj.shape, BF), (w_fc1.shape, BF), (w_fc2.shape, BF)]
    dma = pltpu.SemaphoreType.DMA

    def plain(shape):
        return pltpu.VMEM(shape, F32)

    def low(shape):
        return pltpu.VMEM(shape, BF)
    results = pl.pallas_call(
        functools.partial(section_kernel, images, dims, rows, lags, chunk),
        out_shape=[jax.ShapeDtypeStruct(*o) for o in outs],
        in_specs=[any_space] + [vmem] * 7 + [any_space] * 4,
        out_specs=[any_space] * len(outs),
        scratch_shapes=[low(w.shape) for w in weights] + [
            plain((2, 32, width)), low((2, tokens, width)), low((tokens, width)), plain((81 * images, width)),
            plain((tokens, width)), plain((tokens, width)), plain((tokens, width)), plain((tokens, width)),
            low((slots, 3 * width)), low(soft), low((tokens, wide)), low((tokens, wide)),
            low((slots, tokens)), low((slots, width)), low((tokens, width)), low((tokens, width)), low((tokens, width)), low((tokens, width)),
            plain((2, images, width)), plain((2, small_rows, 128)), plain((2, small_rows, 128)),
            low((grads, rows, chunk)), low((lands, land, chunk)), low((4, SIDE, chunk)), low((6, SIDE, chunk)), plain((1, small_land, 128)),
            low((2, tokens, SIDE)), low((2, tokens, 2 * chunk)),
            dma((13 + width // 128,)), dma((14,)), dma((8 + width // 128,)), dma((8 + width // 128,)), dma((2, 2)), dma((pairs,)), dma((pairs,)),
            dma((pairs, 12)), dma((pairs, 12)), dma, dma((1, 12)), dma((1, 12)), dma, dma((pairs // 2,)), dma((pairs // 2,)),
        ],
        compiler_params=pltpu.CompilerParams(collective_id=collective_id, has_side_effects=True, vmem_limit_bytes=63 * 2**20),
    )(halves, *small, w_qkv, w_proj, w_fc1, w_fc2)
    return results[:3]


def finish_kernel(images, chunk, done, sums, ends, fc2, fc1, proj, qkv, conv_w, conv_b, gain, shift, b_proj, b_fc1, b_fc2, section,
                  low_buf, wide_buf, end_buf, read, write, end_sem):
    depth = low_buf.shape[0]
    jobs, start = [], 0
    for dst in (fc2, fc1, proj, qkv):
        across = dst.shape[2] // chunk
        number = dst.shape[1] // SIDE * across
        jobs.append((start, number, across, dst))
        start += number
    end_copy = pltpu.make_async_copy(ends, end_buf, end_sem)
    end_copy.start()

    def get(c):
        return pltpu.make_async_copy(done.at[c, pl.ds(0, SIDE)], low_buf.at[lax.rem(c, depth)], read.at[lax.rem(c, depth)])

    def give(c, dst, across, at):
        rows = pl.ds(pl.multiple_of(lax.div(at, across) * SIDE, SIDE), SIDE)
        return pltpu.make_async_copy(wide_buf.at[lax.rem(c, depth)], dst.at[0, rows, cols(lax.rem(at, across), chunk)],
                                     write.at[lax.rem(c, depth)])

    @pl.loop(0, depth)
    def _(c):
        get(c).start()
    for begin, number, across, dst in jobs:
        @pl.loop(0, number)
        def _(at):
            c = begin + at
            slot = lax.rem(c, depth)
            get(c).wait()

            @pl.when(c >= depth)
            def _():
                give(c, dst, across, at).wait()
            for r in range(0, SIDE, 128):
                wide_buf[slot, r : r + 128] = low_buf[slot, r : r + 128].astype(F32)
            give(c, dst, across, at).start()

            @pl.when(c + depth < start)
            def _():
                get(c + depth).start()
    lanes = fc2.shape[2] // 128
    width = fc2.shape[2]

    def take(first_row, ref, index, rows):
        for lane in range(lanes):
            ref[index + (slice(lane * 128, (lane + 1) * 128),)] = sums[0, lane * 32 + first_row : lane * 32 + first_row + rows, :]
    for j in range(2):
        take(CONV + 9 * j, conv_w, (0, j, slice(0, 9)), 9)
    take(CONV_BIAS, conv_b, (0, slice(0, 2)), 2)
    take(GAIN, gain, (0, slice(0, 2)), 2)
    take(SHIFT, shift, (0, slice(0, 2)), 2)
    take(B_PROJ, b_proj, (slice(0, 1),), 1)
    take(B_FC2, b_fc2, (slice(0, 1),), 1)
    for lane in range(b_fc1.shape[1] // 128):
        at = lane % lanes * 32 + B_FC1 + lane // lanes
        b_fc1[0:1, lane * 128 : (lane + 1) * 128] = sums[0, at : at + 1, :]
    end_copy.wait()
    for half in range(2):
        for lane in range(lanes):
            for i in range(images):
                section[0, half * images + i, :, lane * 128 : (lane + 1) * 128] = end_buf[half, lane, pl.ds(i, 49, stride=images), :]

    @pl.loop(start - depth, start)
    def _(c):
        give(c, fc2, 1, 0).wait()


def finish(done, sums, ends, shapes, images):
    any_space = pl.BlockSpec(memory_space=pl.ANY)
    vmem = pl.BlockSpec(memory_space=pltpu.VMEM)
    chunk, depth = done.shape[2], 6
    return pl.pallas_call(
        functools.partial(finish_kernel, images, chunk),
        out_shape=[jax.ShapeDtypeStruct(s, F32) for s in shapes],
        in_specs=[any_space, vmem, any_space],
        out_specs=[any_space] * 4 + [vmem] * 8,
        scratch_shapes=[pltpu.VMEM((depth, SIDE, chunk), BF), pltpu.VMEM((depth, SIDE, chunk), F32), pltpu.VMEM(ends.shape, F32),
                        pltpu.SemaphoreType.DMA((depth,)), pltpu.SemaphoreType.DMA((depth,)), pltpu.SemaphoreType.DMA],
        compiler_params=pltpu.CompilerParams(vmem_limit_bytes=48 * 2**20),
    )(done, sums, ends)


def on_device(section_inputs, conv_weight, conv_bias, norm_gain, norm_bias, w_qkv, w_proj, b_proj, w_fc1, b_fc1, w_fc2, b_fc2):
    n = lax.axis_size("dp")
    images, positions, width = section_inputs.shape[1:]
    half = images // 2
    spare = -(-positions * half // 16) * 16 // half - positions
    halves = jnp.pad(section_inputs.reshape(2, half, positions, width), ((0, 0), (0, 0), (0, spare), (0, 0)))
    halves = jnp.swapaxes(halves, 1, 2).reshape(2, -1, width)
    small = (conv_weight[0], conv_bias[0], norm_gain[0], norm_bias[0], b_proj, b_fc1, b_fc2)
    ends, done, sums = section(halves, small, (w_qkv[0], w_proj[0], w_fc1[0], w_fc2[0]), half, n)
    shapes = [a.shape for a in (w_fc2, w_fc1, w_proj, w_qkv, conv_weight, conv_bias, norm_gain, norm_bias, b_proj, b_fc1, b_fc2, section_inputs)]
    fc2, fc1, proj, qkv, conv_w, conv_b, gain, shift, g_proj, g_fc1, g_fc2, section_ends = finish(done, sums, ends, shapes, half)
    return section_ends, conv_w, conv_b, gain, shift, qkv, proj, g_proj, fc1, g_fc1, fc2, g_fc2


def solution(mesh):
    return jax.shard_map(
        on_device,
        mesh=mesh,
        in_specs=(
            P("pipe", "dp", None, None),
            P("pipe", None, None, None),
            P("pipe", None, None),
            P("pipe", None, None),
            P("pipe", None, None),
            P("pipe", None, None),
            P("pipe", None, None),
            P("pipe", None),
            P("pipe", None, None),
            P("pipe", None),
            P("pipe", None, None),
            P("pipe", None),
        ),
        out_specs=(
            P("pipe", "dp", None, None),
            P("pipe", None, None, None),
            P("pipe", None, None),
            P("pipe", None, None),
            P("pipe", None, None),
            P("pipe", None, None),
            P("pipe", None, None),
            P("pipe", None),
            P("pipe", None, None),
            P("pipe", None),
            P("pipe", None, None),
            P("pipe", None),
        ),
        check_vma=False,
    )
```

time: 377 us -> 308 us (0.82)
  Pallas kernels: 357 us -> 297 us
  other arithmetic: 8.86 us -> 0 us
    pallas_call x7 -> x2, Pallas kernels: 357 us -> 297 us  [the longest x1 283 us: section(): pl.pallas_call(functools.partial(section_kernel, images, dims, rows, lags...]
    select_n x2 -> x0, other arithmetic: 4.78 us -> none  [the longest x1 3.4 us: on_device(): ends = jnp.where(is_first, grad_in, result).reshape(49, images, width)]
    unnamed x9 -> x7, local copies, waits for them, and re-layouts: 2.2 us -> 6.88 us
  transfers between devices with their start and end apart: 1 -> 0, of which waited for: 1 -> 0; matrix products, arithmetic and copies ran while one was open for 0% -> 0% of each run, Pallas kernels for 0% -> 0%
where the time goes in v4:
time: 308 us; the launch traced here: 307 us
  Pallas kernels  297 us (96%)
  local copies, waits for them, and re-layouts  9.26 us (3%)
    pallas_call x1, Pallas kernels, section(): pl.pallas_call(functools.partial(section_kernel, images, dims, rows, lags...  283 us
    pallas_call x1, Pallas kernels, finish(): pl.pallas_call(functools.partial(finish_kernel, images, chunk), out_shape...  14.8 us
    unnamed x7, local copies, waits for them, and re-layouts  6.88 us

profile of v4, /device:TPU:0, one launch (start us, length us, event | category | flops | bytes accessed | tf_op | source)
XLA Modules:
  0.0 307.3 jit_solution(1808078091634772218)
XLA Ops:
  0.6 1.5 copy.31
  2.1 2.4 pad_bitcast_fusion.halves
  4.5 282.6 %shard_map.211 = (f32[2,6,400,128]{3,2,1,0:T(8,128)}, bf16[36,768,384]{2,1,0:T(8,128)(2,1)}, f32[1,256,128]{2,1,0:T(8,128)}, bf16[2,16,400,768]{3,2,1,0:T(8,128)...) custom-call(bf16[2,400,768]{2,1,0:T(8,128)(2,1)} %pad_bitcast_fusion, ...), custom_call_target="tpu_custom_call" | custom-call | tf_op jit(solution)/shard_map/pallas_call | solution.py:1060
  287.1 0.0 copy-start
  287.1 1.7 copy-done
  288.8 0.0 copy-start.1
  288.8 0.9 copy-done.1
  289.7 14.8 %shard_map.212 = (f32[1,3072,768]{2,1,0:T(8,128)}, f32[1,768,3072]{2,1,0:T(8,128)}, f32[1,768,768]{2,1,0:T(8,128)}, f32[1,768,2304]{2,1,0:T(8,128)}, f32[1,2,9,7...) custom-call(bf16[36,768,384]{2,1,0:T(8,128)(2,1)} %get-tuple-element, ...), custom_call_target="tpu_custom_call" | custom-call | tf_op jit(solution)/shard_map/pallas_call | solution.py:1152
  304.5 2.2 copy.26
  306.7 0.7 copy.27
Async XLA Ops:
  287.1 1.7 copy-start
  288.8 0.9 copy-start.1

commit v5 on v4

--- a/solution.py
+++ b/solution.py
@@ -110,7 +110,6 @@
         pos = lax.rem(lax.div(dp, stride), size)
         low = pos < (size + 1) // 2
         self.outer = jnp.where(low, pos, size - 1 - pos)
-        self.pos = pos
         self.low = low
         step = jnp.where(low, stride, -stride)
         self.inner_peer = dp + step
@@ -120,149 +119,191 @@
 def pick(flag, a, b):
     out = object.__new__(Place)
     out.size = a.size
-    for name in ("pos", "low", "outer", "inner_peer", "outer_peer"):
+    for name in ("low", "outer", "inner_peer", "outer_peer"):
         setattr(out, name, jnp.where(flag, getattr(a, name), getattr(b, name)))
     return out
 
 
+class Shape:
+    def __init__(self, rows, dims):
+        s0, s1, s2 = dims[0]
+        self.sizes = (s2, s0, s1)
+        first = rows // s2
+        mid = [first // s0] * s0
+        tails = sorted(set(mid), reverse=True) if s0 == 4 else [mid[0]]
+
+        def cut(parts):
+            return [sum(parts[:j]) for j in range(len(parts) + 1)]
+        self.cuts = ([cut([first] * s2)], [cut(mid)], [cut([tail // s1] * s1) for tail in tails])
+        self.starts, total = [], 0
+        for n, lists in zip(self.sizes, self.cuts):
+            self.starts.append(total)
+            at = lists[0]
+            total += 0 if n == 1 else at[1] if n == 2 else at[4] + at[1]
+        self.land = total
+        self.events, self.first_event = 0, []
+        for n in self.sizes * 2:
+            self.first_event.append(self.events)
+            self.events += {1: 0, 2: 1, 4: 4}[n]
+
+
 class Ring:
-    def __init__(self, dp, dims, rows, grad, land, out, out_at, send, recv, local):
+    def __init__(self, dp, dims, shape, grad, land, out, out_at, send, recv, local):
         (s0, s1, s2), (t0, t1, t2) = dims
         self.mids = Place(dp, s0, t0)
         self.fast, self.slow = Place(dp, s2, t2), Place(dp, s1, t1)
         self.grad, self.land, self.out, self.out_at = grad, land, out, out_at
         self.grads, self.lands = grad.shape[0], land.shape[0]
         self.send, self.recv, self.local = send, recv, local
-        self.sizes, self.lens, self.starts, _ = Ring.shape(rows, dims)
-
-    @staticmethod
-    def shape(rows, dims):
-        s0, s1, s2 = dims[0]
-        sizes = (s2, s0, s1)
-        lens = (rows // s2, rows // s2 // s0, rows // (s0 * s1 * s2))
-        total, starts = 0, []
-        for n, length in zip(sizes, lens):
-            starts.append(total)
-            total += length * (1 if n == 2 else 5)
-        return sizes, lens, starts, total
+        self.shape, self.sizes, self.cuts = shape, shape.sizes, shape.cuts
 
     def level(self, c, i):
-        flag = lax.rem(c + lax.axis_index("pipe"), 2) == 0
         if i == 1:
             return self.mids
+        flag = lax.rem(c + lax.axis_index("pipe"), 2) == 0
         return pick(flag, self.fast, self.slow) if i == 0 else pick(flag, self.slow, self.fast)
+
+    def each(self, i, do):
+        if len(self.cuts[i]) == 1:
+            do(0)
+        else:
+            for v in range(2):
+                pl.when(self.mids.outer == v)(functools.partial(do, v))
+
+    def own(self, c, i, v):
+        place, at = self.level(c, i), self.cuts[i][v]
+        near = jnp.where(place.low, at[0], at[-1] - at[1])
+        if place.size != 4:
+            return near
+        return jnp.where(place.outer == 0, near, jnp.where(place.low, at[1], at[-1] - at[2]))
 
     def base(self, c, i):
         start = 0
         for j in range(i):
-            start = start + self.level(c, j).pos * self.lens[j]
+            start = start + self.own(c, j, 0)
         return start
 
-    def span(self, c, i, a, b):
-        place, length, n = self.level(c, i), self.lens[i], self.sizes[i]
-        start = self.base(c, i) + jnp.where(place.low, a * length, (n - b) * length)
-        return pl.ds(pl.multiple_of(start, 8), (b - a) * length)
+    def span(self, c, i, v, a, b):
+        at = self.cuts[i][v]
+        start = self.base(c, i) + jnp.where(self.level(c, i).low, at[a], at[-1] - at[b])
+        return pl.ds(pl.multiple_of(start, 8), at[b] - at[a])
 
     def mine(self, c, rows):
         return self.grad.at[lax.rem(c, self.grads), rows]
 
     def landing(self, c, i, at, length):
-        return self.land.at[lax.rem(c, self.lands), pl.ds(self.starts[i] + at, length)]
+        return self.land.at[lax.rem(c, self.lands), pl.ds(self.shape.starts[i] + at, length)]
 
     def copy(self, c, ev, src, dst, peer):
         return pltpu.make_async_remote_copy(
             src_ref=src, dst_ref=dst, send_sem=self.send.at[c, ev], recv_sem=self.recv.at[c, ev],
             device_id={"dp": peer}, device_id_type=MESH)
 
-    def add(self, c, i, a, b, at):
-        rows = self.span(c, i, a, b)
+    def add(self, c, i, v, a, b, at):
+        rows = self.span(c, i, v, a, b)
         slot = lax.rem(c, self.grads)
-        got = self.landing(c, i, at, (b - a) * self.lens[i])
-        self.grad[slot, rows] = self.grad[slot, rows] + got[...]
-
-    def give(self, c, i, ev, a, b, at, peer):
-        return self.copy(c, ev, self.mine(c, self.span(c, i, a, b)), self.landing(c, i, at, (b - a) * self.lens[i]), peer)
+        self.grad[slot, rows] = self.grad[slot, rows] + self.landing(c, i, at, rows.size)[...]
+
+    def give(self, c, i, v, ev, a, b, at, peer):
+        rows = self.span(c, i, v, a, b)
+        return self.copy(c, ev, self.mine(c, rows), self.landing(c, i, at, rows.size), peer)
 
     def reduce_stages(self, i):
-        n, length = self.sizes[i], self.lens[i]
-        ein, eout = 2 * i, 2 * i + 1
+        n = self.sizes[i]
+        ev = self.shape.first_event[i]
         if n == 1:
             return []
         if n == 2:
             def first(c):
-                self.give(c, i, eout, 1, 2, 0, self.level(c, i).inner_peer).start()
+                self.each(i, lambda v: self.give(c, i, v, ev, 1, 2, 0, self.level(c, i).inner_peer).start())
 
             def last(c):
-                self.give(c, i, eout, 0, 1, 0, self.level(c, i).inner_peer).wait_recv()
-                self.add(c, i, 0, 1, 0)
+                def do(v):
+                    self.give(c, i, v, ev, 0, 1, 0, self.level(c, i).inner_peer).wait_recv()
+                    self.add(c, i, v, 0, 1, 0)
+                self.each(i, do)
             return [first, last]
+        length = self.cuts[i][0][1]
 
         def zero(c):
             place = self.level(c, i)
 
             @pl.when(place.outer == 0)
             def _():
-                self.give(c, i, ein, 1, 4, 0, place.inner_peer).start()
+                self.give(c, i, 0, ev, 2, 4, 0, place.inner_peer).start()
 
         def one(c):
             place = self.level(c, i)
 
+            @pl.when(place.outer == 0)
+            def _():
+                self.give(c, i, 0, ev + 1, 1, 2, 2 * length, place.inner_peer).start()
+
             @pl.when(place.outer == 1)
             def _():
-                self.give(c, i, ein, 1, 4, 0, place.inner_peer).wait_recv()
-                self.add(c, i, 2, 4, jnp.where(place.low, length, 0))
-                self.give(c, i, eout, 2, 4, 3 * length, place.inner_peer).start()
-                self.add(c, i, 1, 2, jnp.where(place.low, 0, 2 * length))
+                self.give(c, i, 0, ev, 2, 4, 0, place.inner_peer).wait_recv()
+                self.add(c, i, 0, 2, 4, 0)
+                self.give(c, i, 0, ev + 2, 3, 4, 3 * length, place.inner_peer).start()
 
         def two(c):
             place = self.level(c, i)
 
             @pl.when(place.outer == 1)
             def _():
-                self.give(c, i, eout, 0, 2, 3 * length, place.inner_peer).wait_recv()
-                self.add(c, i, 0, 2, 3 * length)
-                self.give(c, i, ein, 0, 1, 3 * length, place.outer_peer).start()
+                self.give(c, i, 0, ev + 2, 0, 1, 3 * length, place.inner_peer).wait_recv()
+                self.add(c, i, 0, 0, 1, 3 * length)
+                self.give(c, i, 0, ev, 0, 1, 3 * length, place.outer_peer).start()
+                self.give(c, i, 0, ev + 3, 2, 3, 4 * length, place.inner_peer).start()
 
         def three(c):
             place = self.level(c, i)
 
             @pl.when(place.outer == 0)
             def _():
-                self.give(c, i, ein, 0, 1, 3 * length, place.inner_peer).wait_recv()
-                self.add(c, i, 0, 1, 3 * length)
+                self.give(c, i, 0, ev, 0, 1, 3 * length, place.inner_peer).wait_recv()
+                self.add(c, i, 0, 0, 1, 3 * length)
+
+            @pl.when(place.outer == 1)
+            def _():
+                self.give(c, i, 0, ev + 1, 1, 2, 2 * length, place.inner_peer).wait_recv()
+                self.add(c, i, 0, 1, 2, 2 * length)
+                self.give(c, i, 0, ev + 3, 1, 2, 4 * length, place.inner_peer).wait_recv()
+                self.add(c, i, 0, 1, 2, 4 * length)
         return [zero, one, two, three]
 
     def reduce_ends(self, c):
         for i in range(3):
             n, place = self.sizes[i], self.level(c, i)
-            ein, eout = 2 * i, 2 * i + 1
+            ev = self.shape.first_event[i]
             if n == 2:
-                self.give(c, i, eout, 1, 2, 0, place.inner_peer).wait_send()
+                self.each(i, lambda v: self.give(c, i, v, ev, 1, 2, 0, place.inner_peer).wait_send())
             elif n == 4:
                 @pl.when(place.outer == 0)
                 def _():
-                    self.give(c, i, ein, 1, 4, 0, place.inner_peer).wait_send()
+                    self.give(c, i, 0, ev, 2, 4, 0, place.inner_peer).wait_send()
+                    self.give(c, i, 0, ev + 1, 1, 2, 0, place.inner_peer).wait_send()
 
                 @pl.when(place.outer == 1)
                 def _():
-                    self.give(c, i, eout, 2, 4, 0, place.inner_peer).wait_send()
-                    self.give(c, i, ein, 0, 1, 0, place.outer_peer).wait_send()
-
-    def spread(self, c, i, ev, a, b, peer):
-        dst = self.out.at[self.out_at(c), self.span(c, i, a, b)]
+                    self.give(c, i, 0, ev + 2, 3, 4, 0, place.inner_peer).wait_send()
+                    self.give(c, i, 0, ev, 0, 1, 0, place.outer_peer).wait_send()
+                    self.give(c, i, 0, ev + 3, 2, 3, 0, place.inner_peer).wait_send()
+
+    def spread(self, c, i, v, ev, a, b, peer):
+        dst = self.out.at[self.out_at(c), self.span(c, i, v, a, b)]
         return self.copy(c, ev, dst, dst, peer)
 
     def gather_stages(self, i):
         n = self.sizes[i]
-        ein, eout = 6 + 2 * i, 7 + 2 * i
+        ev = self.shape.first_event[3 + i]
         if n == 1:
             return []
         if n == 2:
             def first(c):
-                self.spread(c, i, eout, 0, 1, self.level(c, i).inner_peer).start()
+                self.each(i, lambda v: self.spread(c, i, v, ev, 0, 1, self.level(c, i).inner_peer).start())
 
             def last(c):
-                self.spread(c, i, eout, 1, 2, self.level(c, i).inner_peer).wait_recv()
+                self.each(i, lambda v: self.spread(c, i, v, ev, 1, 2, self.level(c, i).inner_peer).wait_recv())
             return [first, last]
 
         def zero(c):
@@ -270,53 +311,65 @@
 
             @pl.when(place.outer == 0)
             def _():
-                self.spread(c, i, ein, 0, 1, place.inner_peer).start()
+                self.spread(c, i, 0, ev, 0, 1, place.inner_peer).start()
+
+            @pl.when(place.outer == 1)
+            def _():
+                self.spread(c, i, 0, ev + 2, 1, 2, place.inner_peer).start()
+                self.spread(c, i, 0, ev, 1, 2, place.outer_peer).start()
 
         def one(c):
             place = self.level(c, i)
 
             @pl.when(place.outer == 1)
             def _():
-                self.spread(c, i, ein, 0, 1, place.outer_peer).wait_recv()
-                self.spread(c, i, eout, 0, 2, place.inner_peer).start()
+                self.spread(c, i, 0, ev, 0, 1, place.outer_peer).wait_recv()
+                self.spread(c, i, 0, ev + 3, 0, 1, place.inner_peer).start()
 
         def two(c):
             place = self.level(c, i)
 
             @pl.when(place.outer == 1)
             def _():
-                self.spread(c, i, eout, 2, 4, place.inner_peer).wait_recv()
-                self.spread(c, i, ein, 1, 4, place.outer_peer).start()
+                self.spread(c, i, 0, ev + 2, 2, 3, place.inner_peer).wait_recv()
+                self.spread(c, i, 0, ev + 3, 3, 4, place.inner_peer).wait_recv()
+                self.spread(c, i, 0, ev + 1, 2, 4, place.outer_peer).start()
 
         def three(c):
             place = self.level(c, i)
 
             @pl.when(place.outer == 0)
             def _():
-                self.spread(c, i, ein, 1, 4, place.inner_peer).wait_recv()
+                self.spread(c, i, 0, ev, 1, 2, place.inner_peer).wait_recv()
+                self.spread(c, i, 0, ev + 1, 2, 4, place.inner_peer).wait_recv()
         return [zero, one, two, three]
 
     def gather_ends(self, c):
         for i in range(3):
             n, place = self.sizes[i], self.level(c, i)
-            ein, eout = 6 + 2 * i, 7 + 2 * i
+            ev = self.shape.first_event[3 + i]
             if n == 2:
-                self.spread(c, i, eout, 0, 1, place.inner_peer).wait_send()
+                self.each(i, lambda v: self.spread(c, i, v, ev, 0, 1, place.inner_peer).wait_send())
             elif n == 4:
                 @pl.when(place.outer == 0)
                 def _():
-                    self.spread(c, i, ein, 0, 1, place.inner_peer).wait_send()
+                    self.spread(c, i, 0, ev, 0, 1, place.inner_peer).wait_send()
 
                 @pl.when(place.outer == 1)
                 def _():
-                    self.spread(c, i, eout, 0, 2, place.inner_peer).wait_send()
-                    self.spread(c, i, ein, 1, 4, place.outer_peer).wait_send()
+                    self.spread(c, i, 0, ev + 2, 1, 2, place.inner_peer).wait_send()
+                    self.spread(c, i, 0, ev, 1, 2, place.outer_peer).wait_send()
+                    self.spread(c, i, 0, ev + 3, 0, 1, place.inner_peer).wait_send()
+                    self.spread(c, i, 0, ev + 1, 2, 4, place.outer_peer).wait_send()
 
     def settle(self, c):
-        rows = pl.ds(pl.multiple_of(self.base(c, 3), 8), self.lens[2])
-        copy = pltpu.make_async_copy(self.mine(c, rows), self.out.at[self.out_at(c), rows], self.local)
-        copy.start()
-        copy.wait()
+        def do(v):
+            at = self.cuts[2][v]
+            rows = pl.ds(pl.multiple_of(self.base(c, 2) + self.own(c, 2, v), 8), at[1])
+            copy = pltpu.make_async_copy(self.mine(c, rows), self.out.at[self.out_at(c), rows], self.local)
+            copy.start()
+            copy.wait()
+        self.each(2, do)
 
     def stages(self, first, second, last):
         groups = [self.reduce_stages(0), self.reduce_stages(1), self.reduce_stages(2), [self.settle],
@@ -378,50 +431,44 @@
             mixed[rows, g * 128 : (g + 1) * 128] = dot(v, spread_heads(weights, mask)).astype(BF)
 
 
-def spatial_backward(packed, grad_mixed, soft, start, stop):
+def spatial_backward(packed, made, grad_mixed, soft, start, stop):
     width = grad_mixed.shape[1]
 
-    @pl.loop(start, stop)
+    @pl.loop(start, stop, unroll=stop - start)
     def _(i):
         rows = pl.ds(pl.multiple_of(i * SLOT, SLOT), SLOT)
         mask = head_mask(SLOT, GROUP // HEAD, GROUP)
-        made = []
         for g in range(width // GROUP):
             at = [slice(part * width + g * GROUP, part * width + (g + 1) * GROUP) for part in range(3)]
-            made.append((at, [packed[rows, a] for a in at], soft[i, g], grad_mixed[rows, g * GROUP : (g + 1) * GROUP]))
-        ready = []
-        for at, (q, k, v), weights, do in made:
-            out_spread = spread_heads(do, mask)
+            q, k, v = (packed[rows, a] for a in at)
+            weights = soft[i, g]
+            out_spread = spread_heads(grad_mixed[rows, g * GROUP : (g + 1) * GROUP], mask)
             w = weights.astype(F32)
             dw = dot_t(v, out_spread)
             ds = (w * (dw - jnp.sum(dw * w, axis=0, keepdims=True))).astype(BF)
-            dq = (fold_heads(t_dot(ds, k), mask, SLOT) * HEAD ** -0.5).astype(BF)
-            ready += zip(at, (dq, dot(ds, spread_heads(q, mask)).astype(BF), dot(weights, out_spread).astype(BF)))
-        for at, value in ready:
-            packed[rows, at] = value
-
-
-def channel_backward(packed, grad_mixed, soft, start, stop):
+            made[rows, at[2]] = dot(weights, out_spread).astype(BF)
+            made[rows, at[1]] = dot(ds, spread_heads(q, mask)).astype(BF)
+            made[rows, at[0]] = (fold_heads(t_dot(ds, k), mask, SLOT) * HEAD ** -0.5).astype(BF)
+
+
+def channel_backward(packed, made, grad_mixed, soft, start, stop):
     width = grad_mixed.shape[1]
 
-    @pl.loop(start, stop)
+    @pl.loop(start, stop, unroll=stop - start)
     def _(i):
         rows = pl.ds(pl.multiple_of(i * SLOT, SLOT), SLOT)
         mask = head_mask(HEAD, 128 // HEAD, 128)
-        made = []
         for g in range(width // 128):
             at = [slice(part * width + g * 128, part * width + (g + 1) * 128) for part in range(3)]
+            q, k, v = (packed[rows, a] for a in at)
             weights = soft[i, g // 2, g % 2 * HEAD : (g % 2 + 1) * HEAD, 0:128]
-            made.append((at, [packed[rows, a] for a in at], weights, grad_mixed[rows, g * 128 : (g + 1) * 128]))
-        ready = []
-        for at, (q, k, v), weights, do in made:
+            do = grad_mixed[rows, g * 128 : (g + 1) * 128]
             w = weights.astype(F32)
             dw = fold_heads(t_dot(v, do), mask, HEAD)
             ds = spread_heads((w * (dw - jnp.sum(dw * w, axis=0, keepdims=True))).astype(BF), mask)
-            dq = (dot(k, ds) * HEAD ** -0.5).astype(BF)
-            ready += zip(at, (dq, dot_t(q, ds).astype(BF), dot_t(do, spread_heads(weights, mask)).astype(BF)))
-        for at, value in ready:
-            packed[rows, at] = value
+            made[rows, at[2]] = dot_t(do, spread_heads(weights, mask)).astype(BF)
+            made[rows, at[1]] = dot_t(q, ds).astype(BF)
+            made[rows, at[0]] = (dot(k, ds) * HEAD ** -0.5).astype(BF)
 
 
 def encode(pad, kernel, bias, out, images):
@@ -517,7 +564,7 @@
 SEGMENTS = 12
 
 
-def section_kernel(images, dims, rows, lags, chunk,
+def section_kernel(images, dims, shapes, rows, lags, beat, chunk,
                    halves, conv_w, conv_b, gain, shift, b_proj, b_fc1, b_fc2, w_qkv, w_proj, w_fc1, w_fc2,
                    ends, out, small_out, acts, k_one, k_mid, k_two, k_packed, k_soft, k_slope, x_qkv, x_proj, x_fc1, x_fc2,
                    v_qkv, v_proj, v_fc1, v_fc2, params, xb, cot, pad, one, stream, gmid, gn, packed, soft, slope, hidden,
@@ -544,9 +591,8 @@
     push_x = to_core(1, halves.at[1], xb.at[0])
     push_cot = to_core(1, halves.at[0], cot)
     push_weights = [to_core(2 + at, own, far) for at, (own, far, _) in enumerate(weights)]
-    lanes = [pl.ds(lane * 128, 128) for lane in range(width // 128)]
-    push_result = [to_core(8 + at, gn.at[:, ls], ends.at[0, at]) for at, ls in enumerate(lanes)]
-    push_grad = [to_core(8 + at, gmid.at[:, ls], ends.at[1, at]) for at, ls in enumerate(lanes)]
+    push_result = to_core(6, gn, ends.at[0])
+    push_grad = to_core(6, gmid, ends.at[1])
 
     def load_weight(b, at, fresh):
         own, far, near = weights[at]
@@ -572,7 +618,7 @@
         return [keep(0, one, k_one.at[b]), keep(1, gmid, k_mid.at[b]), keep(2, stream, k_two.at[b]), keep(3, packed, k_packed.at[b]),
                 keep(4, soft, k_soft.at[b]), keep(5, slope, k_slope.at[b]), keep(6, n1, acts.at[b, N1]), keep(7, mixed, acts.at[b, MIXED]),
                 keep(8, n2, acts.at[b, N2])] + [
-                    keep(9 + s, hidden.at[:, pl.ds(s * SIDE, SIDE)], acts.at[b, HIDDEN + s]) for s in range(wide // SIDE)]
+                    keep(9 + s, hidden.at[pl.ds(0, tokens), pl.ds(s * SIDE, SIDE)], acts.at[b, HIDDEN + s]) for s in range(wide // SIDE)]
 
     def row_of(b, row):
         return params[b, row : row + 1, :]
@@ -589,8 +635,8 @@
     def out_at(k):
         return jnp.where(block_of(k) == pipe, number_of(k, pipe), 2 * block_pairs + lax.rem(k, block_pairs))
 
-    main = Ring(dp, dims, rows, grad, land, out, out_at, send, recv, local)
-    small = Ring(dp, dims, small_grad.shape[1], small_pair, small_land, small_out, lambda c: 0, ssend, srecv, slocal)
+    main = Ring(dp, dims, shapes[0], grad, land, out, out_at, send, recv, local)
+    small = Ring(dp, dims, shapes[1], small_pair, small_land, small_out, lambda c: 0, ssend, srecv, slocal)
 
     def slots_of(k):
         at = lax.div(lax.rem(k, block_pairs), per)
@@ -652,6 +698,20 @@
         @pl.when(block_of(k) != pipe)
         def _():
             bring(k).start()
+
+    def leave(k):
+        main.gather_ends(k)
+
+        @pl.when(block_of(k) != pipe)
+        def _():
+            bring(k).wait_send()
+
+        @pl.when(block_of(k) == pipe)
+        def _():
+            arrival = pltpu.make_async_remote_copy(
+                src_ref=out.at[number_of(k, other)], dst_ref=out.at[number_of(k, other)], send_sem=bring_send.at[lax.rem(k, block_pairs)],
+                recv_sem=bring_recv.at[lax.rem(k, block_pairs)], device_id={"pipe": other}, device_id_type=MESH)
+            arrival.wait_recv()
     small_copy = to_core(7, small_grad.at[other], small_pair.at[1])
 
     def small_make(k):
@@ -666,19 +726,22 @@
         stages = main.stages(make, join, hand_over)
         small_stages = small.stages(small_make, small_join, lambda k: None)
         for s in reversed(range(len(stages))):
-            k = t - lags[s]
-
-            @pl.when((k >= 0) & (k < pairs))
+            since = t - lags[s]
+            k = lax.div(since, beat)
+            due = (since >= 0) & (lax.rem(since, beat) == 0)
+
+            @pl.when(due & (k < pairs))
             def _():
                 stages[s](k)
 
-            @pl.when(k == pairs)
+            @pl.when(since == pairs * beat)
             def _():
                 small_stages[s](0)
 
     main.greet()
     for j in range(2):
-        params[pipe, CONV + 9 * j : CONV + 9 * (j + 1), :] = conv_w[j]
+        for t in range(9):
+            params[pipe, CONV + 9 * j + t : CONV + 9 * j + t + 1, :] = conv_w[t, j : j + 1, :]
     for row, ref in ((CONV_BIAS, conv_b), (GAIN, gain), (SHIFT, shift), (B_PROJ, b_proj), (B_FC2, b_fc2)):
         params[pipe, row : row + ref.shape[0], :] = ref[...]
     for j in range(wide // width):
@@ -777,32 +840,30 @@
         def _(j):
             at = cols(j, width)
             value, rate = gelu_both(dot(n2[...], v_fc1[:, at]) + params[b, pl.ds(B_FC1 + j, 1), :])
-            hidden[:, at] = value.astype(BF)
+            hidden[0:tokens, at] = value.astype(BF)
             slope[:, at] = rate.astype(BF)
         stores[5].start()
         for copy in stores[9:]:
             copy.start()
         wait_weight(FC2)
 
-        gn[...] = stream[...] + dot(hidden[...], v_fc2[...]) + row_of(b, B_FC2)
+        gn[...] = stream[...] + dot(hidden[0:tokens, :], v_fc2[...]) + row_of(b, B_FC2)
 
         @pl.when(b == 0)
         def _():
             xb[1] = gn[...].astype(BF)
 
-    end_copy = [pltpu.make_async_copy(gn.at[:, ls], ends.at[1, at], load.at[13 + at]) for at, ls in enumerate(lanes)]
-    last_copy = [pltpu.make_async_copy(gmid.at[:, ls], ends.at[0, at], load.at[13 + at]) for at, ls in enumerate(lanes)]
+    end_copy = pltpu.make_async_copy(gn, ends.at[1], load.at[6])
+    last_copy = pltpu.make_async_copy(gmid, ends.at[0], load.at[6])
 
     @pl.when(first)
     def _():
-        for copy in push_result:
-            copy.start()
+        push_result.start()
         push_cot.wait_recv()
 
     @pl.when(jnp.logical_not(first))
     def _():
-        for copy in end_copy:
-            copy.start()
+        end_copy.start()
         cot_copy.wait()
     keep_cot = keep(13, cot, acts.at[1, COT])
     keep_cot.start()
@@ -864,13 +925,11 @@
         def _():
             @pl.when(first)
             def _():
-                for copy in push_result:
-                    copy.wait_send()
+                push_result.wait_send()
 
             @pl.when(jnp.logical_not(first))
             def _():
-                for copy in end_copy:
-                    copy.wait()
+                end_copy.wait()
         later_weight(b, FC1)
 
         gn[...] = dot_t(slope[...], v_fc1[...])
@@ -904,11 +963,11 @@
 
             @pl.when(b == 0)
             def _():
-                spatial_backward(packed, gm_s, soft, part * each, (part + 1) * each)
+                spatial_backward(packed, hidden, gm_s, soft, part * each, (part + 1) * each)
 
             @pl.when(b == 1)
             def _():
-                channel_backward(packed, gm_s, soft, part * each, (part + 1) * each)
+                channel_backward(packed, hidden, gm_s, soft, part * each, (part + 1) * each)
             if part == 1:
                 keep(4, gatt, acts.at[b, ATT]).wait()
         return run
@@ -916,7 +975,7 @@
     def unswap(b):
         @pl.loop(0, 3)
         def _(j):
-            slope[:, cols(j, width)] = t_dot(swap[...], packed[:, cols(j, width)]).astype(BF)
+            slope[:, cols(j, width)] = t_dot(swap[...], hidden[:, cols(j, width)]).astype(BF)
         copies = [keep(s, slope.at[:, pl.ds(s * SIDE, SIDE)], acts.at[b, PACKED + s]) for s in range(3)]
         for copy in copies:
             copy.start()
@@ -953,31 +1012,36 @@
 
         @pl.when((b == 0) & first)
         def _():
-            for copy in last_copy:
-                copy.start()
+            last_copy.start()
 
         @pl.when((b == 0) & jnp.logical_not(first))
         def _():
-            for copy in push_grad:
-                copy.start()
+            push_grad.start()
     segments = [pre_part(0), pre_part(1), pre_part(2), through_fc1, through_second, through_proj, through_mix(0), through_mix(1),
                 unswap, through_qkv, through_first, finish]
 
-    @pl.loop(0, pairs + 1 + lags[-1])
+    @pl.loop(0, pairs * beat + 1 + lags[-1])
     def _(t):
         tick(t)
-
-        @pl.when((t < pairs) & (lax.rem(t, per) == 0))
-        def _():
-            b, at = block_of(t), lax.div(lax.rem(t, block_pairs), per)
+        since = t - lags[-1] - 1
+        k = lax.div(t, beat)
+        on_beat = (lax.rem(t, beat) == 0) & (k < pairs)
+
+        @pl.when((since >= 0) & (lax.rem(since, beat) == 0) & (since < pairs * beat))
+        def _():
+            leave(lax.div(since, beat))
+
+        @pl.when(on_beat & (lax.rem(k, per) == 0))
+        def _():
+            b, at = block_of(k), lax.div(lax.rem(k, block_pairs), per)
             for number, segment in enumerate(segments):
                 @pl.when(at == number)
                 def _():
                     segment(b)
 
-        @pl.when(t + 1 < pairs)
-        def _():
-            for copy in fetches(t + 1):
+        @pl.when(on_beat & (k + 1 < pairs))
+        def _():
+            for copy in fetches(k + 1):
                 copy.start()
 
     @pl.loop(pairs - main.grads, pairs)
@@ -988,13 +1052,6 @@
     def _(k):
         pair_copy(k).wait_send()
 
-    @pl.loop(0, pairs)
-    def _(k):
-        main.gather_ends(k)
-
-        @pl.when(block_of(k) != pipe)
-        def _():
-            bring(k).wait_send()
     small.reduce_ends(0)
     small.gather_ends(0)
     small_copy.wait_send()
@@ -1005,25 +1062,14 @@
     @pl.when(first)
     def _():
         push_x.wait_send()
-        for copy in last_copy:
-            copy.wait()
-        for copy in push_grad:
-            copy.wait_recv()
+        last_copy.wait()
+        push_grad.wait_recv()
 
     @pl.when(jnp.logical_not(first))
     def _():
         push_cot.wait_send()
-        for copy in push_grad:
-            copy.wait_send()
-        for copy in push_result:
-            copy.wait_recv()
-
-    @pl.loop(0, block_pairs)
-    def _(at):
-        number = 2 * at + other
-        pltpu.make_async_remote_copy(
-            src_ref=out.at[number], dst_ref=out.at[number], send_sem=bring_send.at[at], recv_sem=bring_recv.at[at],
-            device_id={"pipe": other}, device_id_type=MESH).wait_recv()
+        push_grad.wait_send()
+        push_result.wait_recv()
 
 
 def section(halves, small, weights, images, n, collective_id=0):
@@ -1037,16 +1083,17 @@
     pairs = total
     rows = -(-SIDE // (16 * n)) * 16 * n
     small_rows = 16 * n
-    _, _, _, land = Ring.shape(rows, dims)
-    _, _, _, small_land = Ring.shape(small_rows, dims)
+    shapes = (Shape(rows, dims), Shape(small_rows, dims))
+    events = shapes[0].events
     hops = sum(0 if s == 1 else 1 if s == 2 else 3 for s in dims[0])
+    beat = 1
     gaps = [1, 2] + [1] * (2 * hops - 2) + [2]
     lags = [sum(gaps[:s]) for s in range(2 * hops + 2)]
-    grads, lands = lags[hops + 1] + 3, 10
+    grads, lands = -(-lags[hops + 1] // beat) + 3, 10
     any_space = pl.BlockSpec(memory_space=pl.ANY)
     vmem = pl.BlockSpec(memory_space=pltpu.VMEM)
     soft = (images, width // GROUP, SLOT, 2 * GROUP)
-    outs = [((2, width // 128, tokens, 128), F32), ((total + total // 2, rows, chunk), BF), ((1, small_rows, 128), F32),
+    outs = [((2, tokens, width), F32), ((total + total // 2, rows, chunk), BF), ((1, small_rows, 128), F32),
             ((2, 16, tokens, SIDE), BF), ((2, tokens, width), F32), ((2, tokens, width), F32), ((2, tokens, width), F32),
             ((2, slots, 3 * width), BF), ((2, *soft), BF), ((2, tokens, wide), BF),
             (w_qkv.shape, BF), (w_proj.shape, BF), (w_fc1.shape, BF), (w_fc2.shape, BF)]
@@ -1058,20 +1105,20 @@
     def low(shape):
         return pltpu.VMEM(shape, BF)
     results = pl.pallas_call(
-        functools.partial(section_kernel, images, dims, rows, lags, chunk),
+        functools.partial(section_kernel, images, dims, shapes, rows, lags, beat, chunk),
         out_shape=[jax.ShapeDtypeStruct(*o) for o in outs],
         in_specs=[any_space] + [vmem] * 7 + [any_space] * 4,
         out_specs=[any_space] * len(outs),
         scratch_shapes=[low(w.shape) for w in weights] + [
             plain((2, 32, width)), low((2, tokens, width)), low((tokens, width)), plain((81 * images, width)),
             plain((tokens, width)), plain((tokens, width)), plain((tokens, width)), plain((tokens, width)),
-            low((slots, 3 * width)), low(soft), low((tokens, wide)), low((tokens, wide)),
+            low((slots, 3 * width)), low(soft), low((tokens, wide)), low((slots, wide)),
             low((slots, tokens)), low((slots, width)), low((tokens, width)), low((tokens, width)), low((tokens, width)), low((tokens, width)),
             plain((2, images, width)), plain((2, small_rows, 128)), plain((2, small_rows, 128)),
-            low((grads, rows, chunk)), low((lands, land, chunk)), low((4, SIDE, chunk)), low((6, SIDE, chunk)), plain((1, small_land, 128)),
+            low((grads, rows, chunk)), low((lands, shapes[0].land, chunk)), low((4, SIDE, chunk)), low((6, SIDE, chunk)), plain((1, shapes[1].land, 128)),
             low((2, tokens, SIDE)), low((2, tokens, 2 * chunk)),
-            dma((13 + width // 128,)), dma((14,)), dma((8 + width // 128,)), dma((8 + width // 128,)), dma((2, 2)), dma((pairs,)), dma((pairs,)),
-            dma((pairs, 12)), dma((pairs, 12)), dma, dma((1, 12)), dma((1, 12)), dma, dma((pairs // 2,)), dma((pairs // 2,)),
+            dma((13,)), dma((14,)), dma((8,)), dma((8,)), dma((2, 2)), dma((pairs,)), dma((pairs,)),
+            dma((pairs, events)), dma((pairs, events)), dma, dma((1, events)), dma((1, events)), dma, dma((pairs // 2,)), dma((pairs // 2,)),
         ],
         compiler_params=pltpu.CompilerParams(collective_id=collective_id, has_side_effects=True, vmem_limit_bytes=63 * 2**20),
     )(halves, *small, w_qkv, w_proj, w_fc1, w_fc2)
@@ -1079,7 +1126,7 @@
 
 
 def finish_kernel(images, chunk, done, sums, ends, fc2, fc1, proj, qkv, conv_w, conv_b, gain, shift, b_proj, b_fc1, b_fc2, section,
-                  low_buf, wide_buf, end_buf, read, write, end_sem):
+                  low_buf, wide_buf, end_buf, section_buf, read, write, end_sem):
     depth = low_buf.shape[0]
     jobs, start = [], 0
     for dst in (fc2, fc1, proj, qkv):
@@ -1087,7 +1134,7 @@
         number = dst.shape[1] // SIDE * across
         jobs.append((start, number, across, dst))
         start += number
-    end_copy = pltpu.make_async_copy(ends, end_buf, end_sem)
+    end_copy = pltpu.make_async_copy(ends, end_buf, end_sem.at[0])
     end_copy.start()
 
     def get(c):
@@ -1118,6 +1165,12 @@
             @pl.when(c + depth < start)
             def _():
                 get(c + depth).start()
+        if begin == 0:
+            end_copy.wait()
+            for half in range(2):
+                section_buf[:, half * images : (half + 1) * images, :] = end_buf[half, 0:49]
+            section_copy = pltpu.make_async_copy(section_buf, section.at[0], end_sem.at[1])
+            section_copy.start()
     lanes = fc2.shape[2] // 128
     width = fc2.shape[2]
 
@@ -1125,7 +1178,8 @@
         for lane in range(lanes):
             ref[index + (slice(lane * 128, (lane + 1) * 128),)] = sums[0, lane * 32 + first_row : lane * 32 + first_row + rows, :]
     for j in range(2):
-        take(CONV + 9 * j, conv_w, (0, j, slice(0, 9)), 9)
+        for t in range(9):
+            take(CONV + 9 * j + t, conv_w, (0, t, slice(j, j + 1)), 1)
     take(CONV_BIAS, conv_b, (0, slice(0, 2)), 2)
     take(GAIN, gain, (0, slice(0, 2)), 2)
     take(SHIFT, shift, (0, slice(0, 2)), 2)
@@ -1134,15 +1188,10 @@
     for lane in range(b_fc1.shape[1] // 128):
         at = lane % lanes * 32 + B_FC1 + lane // lanes
         b_fc1[0:1, lane * 128 : (lane + 1) * 128] = sums[0, at : at + 1, :]
-    end_copy.wait()
-    for half in range(2):
-        for lane in range(lanes):
-            for i in range(images):
-                section[0, half * images + i, :, lane * 128 : (lane + 1) * 128] = end_buf[half, lane, pl.ds(i, 49, stride=images), :]
-
     @pl.loop(start - depth, start)
     def _(c):
         give(c, fc2, 1, 0).wait()
+    section_copy.wait()
 
 
 def finish(done, sums, ends, shapes, images):
@@ -1153,10 +1202,11 @@
         functools.partial(finish_kernel, images, chunk),
         out_shape=[jax.ShapeDtypeStruct(s, F32) for s in shapes],
         in_specs=[any_space, vmem, any_space],
-        out_specs=[any_space] * 4 + [vmem] * 8,
+        out_specs=[any_space] * 4 + [vmem] * 7 + [any_space],
         scratch_shapes=[pltpu.VMEM((depth, SIDE, chunk), BF), pltpu.VMEM((depth, SIDE, chunk), F32), pltpu.VMEM(ends.shape, F32),
-                        pltpu.SemaphoreType.DMA((depth,)), pltpu.SemaphoreType.DMA((depth,)), pltpu.SemaphoreType.DMA],
-        compiler_params=pltpu.CompilerParams(vmem_limit_bytes=48 * 2**20),
+                        pltpu.VMEM(shapes[-1][1:], F32),
+                        pltpu.SemaphoreType.DMA((depth,)), pltpu.SemaphoreType.DMA((depth,)), pltpu.SemaphoreType.DMA((2,))],
+        compiler_params=pltpu.CompilerParams(vmem_limit_bytes=62 * 2**20),
     )(done, sums, ends)
 
 
@@ -1167,11 +1217,13 @@
     spare = -(-positions * half // 16) * 16 // half - positions
     halves = jnp.pad(section_inputs.reshape(2, half, positions, width), ((0, 0), (0, 0), (0, spare), (0, 0)))
     halves = jnp.swapaxes(halves, 1, 2).reshape(2, -1, width)
-    small = (conv_weight[0], conv_bias[0], norm_gain[0], norm_bias[0], b_proj, b_fc1, b_fc2)
+    small = (jnp.swapaxes(conv_weight[0], 0, 1), conv_bias[0], norm_gain[0], norm_bias[0], b_proj, b_fc1, b_fc2)
     ends, done, sums = section(halves, small, (w_qkv[0], w_proj[0], w_fc1[0], w_fc2[0]), half, n)
-    shapes = [a.shape for a in (w_fc2, w_fc1, w_proj, w_qkv, conv_weight, conv_bias, norm_gain, norm_bias, b_proj, b_fc1, b_fc2, section_inputs)]
-    fc2, fc1, proj, qkv, conv_w, conv_b, gain, shift, g_proj, g_fc1, g_fc2, section_ends = finish(done, sums, ends, shapes, half)
-    return section_ends, conv_w, conv_b, gain, shift, qkv, proj, g_proj, fc1, g_fc1, fc2, g_fc2
+    ends = ends.reshape(2, -1, half, width)
+    arrays = (w_fc2, w_fc1, w_proj, w_qkv, jnp.swapaxes(conv_weight, 1, 2), conv_bias, norm_gain, norm_bias, b_proj, b_fc1, b_fc2,
+              jnp.swapaxes(section_inputs, 1, 2))
+    fc2, fc1, proj, qkv, conv_w, conv_b, gain, shift, g_proj, g_fc1, g_fc2, section_ends = finish(done, sums, ends, [a.shape for a in arrays], half)
+    return (jnp.swapaxes(section_ends, 1, 2), jnp.swapaxes(conv_w, 1, 2), conv_b, gain, shift, qkv, proj, g_proj, fc1, g_fc1, fc2, g_fc2)
 
 
 def solution(mesh):

time: 308 us -> 297 us (0.964)
  local copies, waits for them, and re-layouts: 9.26 us -> 2.39 us
  Pallas kernels: 297 us -> 293 us
    unnamed x7 -> x0, local copies, waits for them, and re-layouts: 6.88 us -> none
    pallas_call x1, Pallas kernels: 283 us -> 276 us  [section(): pl.pallas_call(functools.partial(section_kernel, images, dims, shapes, ro...]
where the time goes in v5:
time: 297 us; the launch traced here: 296 us
  Pallas kernels  293 us (99%)
    pallas_call x1, Pallas kernels, section(): pl.pallas_call(functools.partial(section_kernel, images, dims, shapes, ro...  276 us
    pallas_call x1, Pallas kernels, finish(): pl.pallas_call(functools.partial(finish_kernel, images, chunk), out_shape...  16.8 us

profile of v5, /device:TPU:0, one launch (start us, length us, event | category | flops | bytes accessed | tf_op | source)
XLA Modules:
  0.0 296.4 jit_solution(4888344339271471301)
XLA Ops:
  0.6 2.4 pad_bitcast_fusion.halves
  3.0 276.4 %shard_map.211 = (f32[2,400,768]{2,1,0:T(8,128)}, bf16[36,768,384]{2,1,0:T(8,128)(2,1)}, f32[1,256,128]{2,1,0:T(8,128)}, bf16[2,16,400,768]{3,2,1,0:T(8,128)(2,1...) custom-call(bf16[2,400,768]{2,1,0:T(8,128)(2,1)} %pad_bitcast_fusion, ...), custom_call_target="tpu_custom_call" | custom-call | tf_op jit(solution)/shard_map/pallas_call | solution.py:1107
  279.4 16.8 %shard_map.212 = (f32[1,3072,768]{2,1,0:T(8,128)}, f32[1,768,3072]{2,1,0:T(8,128)}, f32[1,768,768]{2,1,0:T(8,128)}, f32[1,768,2304]{2,1,0:T(8,128)}, f32[1,9,2,7...) custom-call(bf16[36,768,384]{2,1,0:T(8,128)(2,1)} %get-tuple-element, ...), custom_call_target="tpu_custom_call" | custom-call | tf_op jit(solution)/shard_map/pallas_call | solution.py:1201

commit v6 on v5

--- a/solution.py
+++ b/solution.py
@@ -406,7 +406,7 @@
 def spatial_forward(packed, mixed, soft, images):
     width = mixed.shape[1]
 
-    @pl.loop(0, images, unroll=4)
+    @pl.loop(0, images, unroll=8)
     def _(i):
         rows = pl.ds(pl.multiple_of(i * SLOT, SLOT), SLOT)
         mask = head_mask(SLOT, GROUP // HEAD, GROUP)
@@ -420,7 +420,7 @@
 def channel_forward(packed, mixed, soft, images):
     width = mixed.shape[1]
 
-    @pl.loop(0, images, unroll=4)
+    @pl.loop(0, images, unroll=8)
     def _(i):
         rows = pl.ds(pl.multiple_of(i * SLOT, SLOT), SLOT)
         mask = head_mask(HEAD, 128 // HEAD, 128)
@@ -564,7 +564,7 @@
 SEGMENTS = 12
 
 
-def section_kernel(images, dims, shapes, rows, lags, beat, chunk,
+def section_kernel(images, dims, shapes, rows, lags, chunk,
                    halves, conv_w, conv_b, gain, shift, b_proj, b_fc1, b_fc2, w_qkv, w_proj, w_fc1, w_fc2,
                    ends, out, small_out, acts, k_one, k_mid, k_two, k_packed, k_soft, k_slope, x_qkv, x_proj, x_fc1, x_fc2,
                    v_qkv, v_proj, v_fc1, v_fc2, params, xb, cot, pad, one, stream, gmid, gn, packed, soft, slope, hidden,
@@ -629,20 +629,26 @@
     def block_of(k):
         return jnp.where(k < block_pairs, 1, 0)
 
+    def within(k):
+        return k - jnp.where(k < block_pairs, 0, block_pairs)
+
+    def parts_of(k):
+        return (k, 0) if per == 1 else (lax.div(k, per), lax.rem(k, per))
+
     def number_of(k, core):
-        return 2 * lax.rem(k, block_pairs) + core
+        return 2 * within(k) + core
 
     def out_at(k):
-        return jnp.where(block_of(k) == pipe, number_of(k, pipe), 2 * block_pairs + lax.rem(k, block_pairs))
+        return jnp.where(block_of(k) == pipe, number_of(k, pipe), 2 * block_pairs + within(k))
 
     main = Ring(dp, dims, shapes[0], grad, land, out, out_at, send, recv, local)
     small = Ring(dp, dims, shapes[1], small_pair, small_land, small_out, lambda c: 0, ssend, srecv, slocal)
 
     def slots_of(k):
-        at = lax.div(lax.rem(k, block_pairs), per)
+        at, part = parts_of(within(k))
         left = jnp.where(at < 4, HIDDEN + at, jnp.where(at < 8, N2, jnp.where(at < 9, MIXED, N1)))
         right = jnp.where(at < 4, COT, jnp.where(at < 8, PRE + at - 4, jnp.where(at < 9, ATT, PACKED + at - 9)))
-        return left, right, lax.rem(lax.rem(k, block_pairs), per)
+        return left, right, part
 
     def fetches(k):
         left, right, part = slots_of(k)
@@ -689,7 +695,7 @@
 
     def bring(k):
         number = number_of(k, pipe)
-        at = lax.rem(k, block_pairs)
+        at = within(k)
         return pltpu.make_async_remote_copy(
             src_ref=out.at[out_at(k)], dst_ref=out.at[number], send_sem=bring_send.at[at], recv_sem=bring_recv.at[at],
             device_id={"pipe": other}, device_id_type=MESH)
@@ -709,8 +715,8 @@
         @pl.when(block_of(k) == pipe)
         def _():
             arrival = pltpu.make_async_remote_copy(
-                src_ref=out.at[number_of(k, other)], dst_ref=out.at[number_of(k, other)], send_sem=bring_send.at[lax.rem(k, block_pairs)],
-                recv_sem=bring_recv.at[lax.rem(k, block_pairs)], device_id={"pipe": other}, device_id_type=MESH)
+                src_ref=out.at[number_of(k, other)], dst_ref=out.at[number_of(k, other)], send_sem=bring_send.at[within(k)],
+                recv_sem=bring_recv.at[within(k)], device_id={"pipe": other}, device_id_type=MESH)
             arrival.wait_recv()
     small_copy = to_core(7, small_grad.at[other], small_pair.at[1])
 
@@ -722,19 +728,17 @@
         small_copy.wait_recv()
         small_pair[0] = small_pair[0] + small_pair[1]
 
-    def tick(t):
+    def tick(t, low, high):
         stages = main.stages(make, join, hand_over)
         small_stages = small.stages(small_make, small_join, lambda k: None)
-        for s in reversed(range(len(stages))):
-            since = t - lags[s]
-            k = lax.div(since, beat)
-            due = (since >= 0) & (lax.rem(since, beat) == 0)
-
-            @pl.when(due & (k < pairs))
+        for s in reversed(range(low, high)):
+            k = t - lags[s]
+
+            @pl.when((k >= 0) & (k < pairs))
             def _():
                 stages[s](k)
 
-            @pl.when(since == pairs * beat)
+            @pl.when(k == pairs)
             def _():
                 small_stages[s](0)
 
@@ -759,7 +763,8 @@
     def _():
         push_cot.start()
         cot_copy.start()
-    push_weights[QKV].start()
+    for copy in push_weights:
+        copy.start()
     fill_swap(swap, images)
     clear_border(pad, images)
     small_grad[...] = jnp.zeros_like(small_grad)
@@ -792,10 +797,6 @@
         normalise(one, row_of(b, GAIN), row_of(b, SHIFT), n1)
         stores[6].start()
 
-        @pl.when(b == 0)
-        def _():
-            push_weights[PROJ].start()
-            push_weights[FC1].start()
 
         gm_s[...] = dot(swap[...], n1[...]).astype(BF)
         wait_weight(QKV)
@@ -805,10 +806,6 @@
             scale = jnp.where(j == 0, HEAD ** -0.5, 1.0)
             packed[:, cols(j, width)] = (dot(gm_s[...], v_qkv[:, cols(j, width)]) * scale).astype(BF)
         stores[3].start()
-
-        @pl.when(b == 0)
-        def _():
-            push_weights[FC2].start()
         load_weight(b, PROJ, True)
 
         @pl.when(b == 0)
@@ -1020,28 +1017,30 @@
     segments = [pre_part(0), pre_part(1), pre_part(2), through_fc1, through_second, through_proj, through_mix(0), through_mix(1),
                 unswap, through_qkv, through_first, finish]
 
-    @pl.loop(0, pairs * beat + 1 + lags[-1])
+    late = len(lags) * 2 // 3
+
+    @pl.loop(0, pairs + 1 + lags[-1])
     def _(t):
-        tick(t)
-        since = t - lags[-1] - 1
-        k = lax.div(t, beat)
-        on_beat = (lax.rem(t, beat) == 0) & (k < pairs)
-
-        @pl.when((since >= 0) & (lax.rem(since, beat) == 0) & (since < pairs * beat))
-        def _():
-            leave(lax.div(since, beat))
-
-        @pl.when(on_beat & (lax.rem(k, per) == 0))
-        def _():
-            b, at = block_of(k), lax.div(lax.rem(k, block_pairs), per)
+        tick(t, late, len(lags))
+        gone = t - lags[-1] - 1
+
+        @pl.when((gone >= 0) & (gone < pairs))
+        def _():
+            leave(gone)
+        at, part = parts_of(within(t))
+
+        @pl.when((t < pairs) & (part == 0))
+        def _():
+            b = block_of(t)
             for number, segment in enumerate(segments):
                 @pl.when(at == number)
                 def _():
                     segment(b)
-
-        @pl.when(on_beat & (k + 1 < pairs))
-        def _():
-            for copy in fetches(k + 1):
+        tick(t, 0, late)
+
+        @pl.when(t + 1 < pairs)
+        def _():
+            for copy in fetches(t + 1):
                 copy.start()
 
     @pl.loop(pairs - main.grads, pairs)
@@ -1086,10 +1085,10 @@
     shapes = (Shape(rows, dims), Shape(small_rows, dims))
     events = shapes[0].events
     hops = sum(0 if s == 1 else 1 if s == 2 else 3 for s in dims[0])
-    beat = 1
-    gaps = [1, 2] + [1] * (2 * hops - 2) + [2]
+    gaps = [1, 2] + [1] * (2 * hops - 2) + [3]
     lags = [sum(gaps[:s]) for s in range(2 * hops + 2)]
-    grads, lands = -(-lags[hops + 1] // beat) + 3, 10
+    grads = 8 if lags[hops + 1] < 8 else 16
+    lands = 8 if 2 * gaps[1] + 3 <= 8 else 16
     any_space = pl.BlockSpec(memory_space=pl.ANY)
     vmem = pl.BlockSpec(memory_space=pltpu.VMEM)
     soft = (images, width // GROUP, SLOT, 2 * GROUP)
@@ -1105,7 +1104,7 @@
     def low(shape):
         return pltpu.VMEM(shape, BF)
     results = pl.pallas_call(
-        functools.partial(section_kernel, images, dims, shapes, rows, lags, beat, chunk),
+        functools.partial(section_kernel, images, dims, shapes, rows, lags, chunk),
         out_shape=[jax.ShapeDtypeStruct(*o) for o in outs],
         in_specs=[any_space] + [vmem] * 7 + [any_space] * 4,
         out_specs=[any_space] * len(outs),
@@ -1115,7 +1114,7 @@
             low((slots, 3 * width)), low(soft), low((tokens, wide)), low((slots, wide)),
             low((slots, tokens)), low((slots, width)), low((tokens, width)), low((tokens, width)), low((tokens, width)), low((tokens, width)),
             plain((2, images, width)), plain((2, small_rows, 128)), plain((2, small_rows, 128)),
-            low((grads, rows, chunk)), low((lands, shapes[0].land, chunk)), low((4, SIDE, chunk)), low((6, SIDE, chunk)), plain((1, shapes[1].land, 128)),
+            low((grads, rows, chunk)), low((lands, shapes[0].land, chunk)), low((4, SIDE, chunk)), low((8, SIDE, chunk)), plain((1, shapes[1].land, 128)),
             low((2, tokens, SIDE)), low((2, tokens, 2 * chunk)),
             dma((13,)), dma((14,)), dma((8,)), dma((8,)), dma((2, 2)), dma((pairs,)), dma((pairs,)),
             dma((pairs, events)), dma((pairs, events)), dma, dma((1, events)), dma((1, events)), dma, dma((pairs // 2,)), dma((pairs // 2,)),

time: 297 us -> 287 us (0.966)
  Pallas kernels: 293 us -> 283 us
    pallas_call x1, Pallas kernels: 276 us -> 267 us  [section(): pl.pallas_call(functools.partial(section_kernel, images, dims, shapes, ro...]
where the time goes in v6:
time: 287 us
  Pallas kernels  283 us (99%)
    pallas_call x1, Pallas kernels, section(): pl.pallas_call(functools.partial(section_kernel, images, dims, shapes, ro...  267 us
    pallas_call x1, Pallas kernels, finish(): pl.pallas_call(functools.partial(finish_kernel, images, chunk), out_shape...  16.8 us

profile of v6, /device:TPU:0, one launch (start us, length us, event | category | flops | bytes accessed | tf_op | source)
XLA Modules:
  0.0 286.7 jit_solution(6232366043753992250)
XLA Ops:
  0.6 2.4 pad_bitcast_fusion.halves
  3.0 266.7 %shard_map.211 = (f32[2,400,768]{2,1,0:T(8,128)}, bf16[36,768,384]{2,1,0:T(8,128)(2,1)}, f32[1,256,128]{2,1,0:T(8,128)}, bf16[2,16,400,768]{3,2,1,0:T(8,128)(2,1...) custom-call(bf16[2,400,768]{2,1,0:T(8,128)(2,1)} %pad_bitcast_fusion, ...), custom_call_target="tpu_custom_call" | custom-call | tf_op jit(solution)/shard_map/pallas_call | solution.py:1106
  269.7 16.8 %shard_map.212 = (f32[1,3072,768]{2,1,0:T(8,128)}, f32[1,768,3072]{2,1,0:T(8,128)}, f32[1,768,768]{2,1,0:T(8,128)}, f32[1,768,2304]{2,1,0:T(8,128)}, f32[1,9,2,7...) custom-call(bf16[36,768,384]{2,1,0:T(8,128)(2,1)} %get-tuple-element, ...), custom_call_target="tpu_custom_call" | custom-call | tf_op jit(solution)/shard_map/pallas_call | solution.py:1200

commit v7 on v6

--- a/solution.py
+++ b/solution.py
@@ -492,7 +492,7 @@
 
 
 def normalise(stream, gain, bias, out):
-    @pl.loop(0, stream.shape[0] // 16, unroll=5)
+    @pl.loop(0, stream.shape[0] // 16, unroll=stream.shape[0] // 16)
     def _(p):
         rows = pl.ds(pl.multiple_of(p * 16, 16), 16)
         s = stream[rows, :]
@@ -833,7 +833,7 @@
         wait_weight(FC1)
         load_weight(b, FC2, True)
 
-        @pl.loop(0, wide // width)
+        @pl.loop(0, wide // width, unroll=2)
         def _(j):
             at = cols(j, width)
             value, rate = gelu_both(dot(n2[...], v_fc1[:, at]) + params[b, pl.ds(B_FC1 + j, 1), :])

time: 287 us -> 286 us (level)
  no operation moved by 1% of the time
where the time goes in v7:
time: 286 us
  Pallas kernels  283 us (99%)
    pallas_call x1, Pallas kernels, section(): pl.pallas_call(functools.partial(section_kernel, images, dims, shapes, ro...  266 us
    pallas_call x1, Pallas kernels, finish(): pl.pallas_call(functools.partial(finish_kernel, images, chunk), out_shape...  16.8 us

profile of v7, /device:TPU:0, one launch (start us, length us, event | category | flops | bytes accessed | tf_op | source)
XLA Modules:
  0.0 286.0 jit_solution(8246291668234830807)
XLA Ops:
  0.6 2.4 pad_bitcast_fusion.halves
  3.0 266.0 %shard_map.211 = (f32[2,400,768]{2,1,0:T(8,128)}, bf16[36,768,384]{2,1,0:T(8,128)(2,1)}, f32[1,256,128]{2,1,0:T(8,128)}, bf16[2,16,400,768]{3,2,1,0:T(8,128)(2,1...) custom-call(bf16[2,400,768]{2,1,0:T(8,128)(2,1)} %pad_bitcast_fusion, ...), custom_call_target="tpu_custom_call" | custom-call | tf_op jit(solution)/shard_map/pallas_call | solution.py:1106
  269.0 16.8 %shard_map.212 = (f32[1,3072,768]{2,1,0:T(8,128)}, f32[1,768,3072]{2,1,0:T(8,128)}, f32[1,768,768]{2,1,0:T(8,128)}, f32[1,768,2304]{2,1,0:T(8,128)}, f32[1,9,2,7...) custom-call(bf16[36,768,384]{2,1,0:T(8,128)(2,1)} %get-tuple-element, ...), custom_call_target="tpu_custom_call" | custom-call | tf_op jit(solution)/shard_map/pallas_call | solution.py:1200
